TPU v7x, 128 devices: a whole 4x4x4 slice. The times are simulated.
128 devices in a mesh: ctx: 32 (over x, z, y_hi), tp: 4 (over y_lo, core).
Axes of the slice: x: 4, y: 4 (y_hi: 2, y_lo: 2; y = y_hi * 2 + y_lo), z: 4, core: 2. Of those that a mesh axis runs over, the one named last changes fastest.
Arguments:
- queries: bfloat16 [4, 4096, 4096], P('tp', 'ctx')
- attn_keys: bfloat16 [4, 4096, 512], P('tp', 'ctx')
- hidden: bfloat16 [4, 4096, 5120], P('tp', 'ctx'), may hold values from -6 to 6
- out_grad: bfloat16 [4, 4096, 4096], P('tp', 'ctx'), may hold values from -6 to 6
- logp_new: float32 [4, 4096], P('tp', 'ctx'), may hold values from -1.2 to -0.2
- logp_old: float32 [4, 4096], P('tp', 'ctx'), may hold values from -1.2 to -0.2
- logp_ref: float32 [4, 4096], P('tp', 'ctx'), may hold values from -3 to -0.05
- lengths: int32 [4, 2], P('tp'), may hold values from 1 to 3584, 4096 in all within a row
- rewards: float32 [4, 2], replicated, may hold values from -4 to 4
- groups: int32 [4, 2], replicated, may hold values from 0 to 1, as said below
- master: float32 [5120, 512], P(('ctx', 'tp')), may hold values from -0.078125 to 0.078125
- first_moment: float32 [5120, 512], P(('ctx', 'tp')), may hold values from -3 to 3
- second_moment: float32 [5120, 512], P(('ctx', 'tp')), may hold values from 0.1 to 1
- dec_hidden: bfloat16 [4, 1024, 5120], P(None, 'ctx'), may hold values from -6 to 6
- dec_query: bfloat16 [4, 1024, 4096], P(None, 'ctx', 'tp')
- dec_key: bfloat16 [4, 1024, 512], P(None, 'ctx', 'tp'), may hold values from -16 to 16
- cache_keys: bfloat16 [1024, 512, 512], P('ctx', None, 'tp')
- cache_values: bfloat16 [1024, 512, 512], P('ctx', None, 'tp'), may hold values from -6 to 6
- cache_len: int32 [1024], P('ctx'), may hold values from 1 to 508, as said below
- out_weight: bfloat16 [4096, 5120], P('tp'), may hold values from -0.5 to 0.5
Outputs:
- new_master: float32 [5120, 512], P(('ctx', 'tp'))
- new_first: float32 [5120, 512], P(('ctx', 'tp'))
- new_second: float32 [5120, 512], P(('ctx', 'tp'))
- rollout_weights: bfloat16 [5120, 512], P(None, 'tp')
- dec_out: bfloat16 [4, 1024, 5120], P(None, 'ctx')
Inputs may be any that keep to these rules, and one draw needn't show every extreme that they name: `groups`: each of the 2 prompts is named by exactly 4 rollouts. `cache_len`: in the 32 rows of each device group one row has 508 filled positions.
All inputs are finite; a program needn't handle non-finite values.
Results may differ from a plain program's by a relative error of at most 0.0067.
Values may be sent and summed in bfloat16 or wider, within the bound.
No kernel may reach another device: no remote copies, remote signals or barrier semaphores. Data moves between devices by JAX's collectives and lax.ppermute only.
A program may use at most 128 MiB of HBM per device.

v0:
```python
import math

import jax
import jax.numpy as jnp
from jax import lax
from jax.sharding import PartitionSpec as P

HD = 128
HEADS = 32
KV = 4


first_decay = 0.9
second_decay = 0.95
adam_eps = 1e-08
learn_rate = 0.001
decay_weight = 0.1
kl_weight = 0.1


def segment_ids(lengths_row, position):
    doc_ends = jnp.cumsum(lengths_row)
    return jnp.sum((position[:, None] >= doc_ends[None, :]).astype(jnp.int32), axis=1)


def group_advantage(rewards, groups):
    flat_reward = rewards.reshape(-1)
    flat_group = groups.reshape(-1)
    same_group = (flat_group[:, None] == flat_group[None, :]).astype(jnp.float32)
    group_mean = jnp.sum(same_group * flat_reward[None, :], axis=1) / jnp.sum(same_group, axis=1)
    return (flat_reward - group_mean).reshape(rewards.shape)


def token_coef(own_advantage, segment, policy_logp, sample_logp, frozen_logp, divisor):
    labels = jnp.arange(own_advantage.shape[0], dtype=jnp.int32)
    picked = jnp.sum(
        jnp.where(segment[:, None] == labels[None, :], own_advantage[None, :], 0.0), axis=1
    )
    return (
        -jnp.exp(policy_logp - sample_logp) * picked
        + kl_weight * (1.0 - jnp.exp(frozen_logp - policy_logp))
    ) / divisor


def decode_block(dec_query, dec_key, fresh_values, cache_keys, cache_values, cache_len):
    step_count = dec_query.shape[0]
    row_total = dec_query.shape[1]
    key_heads = cache_keys.shape[2] // HD
    group_size = HEADS // KV
    cache_rows = cache_keys.shape[1]
    score_scale = HD ** (-0.5)
    query_heads = dec_query.reshape(step_count, row_total, key_heads, group_size, HD)
    old_keys = cache_keys.reshape(row_total, cache_rows, key_heads, HD)
    old_values = cache_values.reshape(row_total, cache_rows, key_heads, HD)
    fresh_keys = dec_key.reshape(step_count, row_total, key_heads, HD)
    fresh_vals = fresh_values.reshape(step_count, row_total, key_heads, HD)
    old_scores = (
        jnp.einsum("srkgd,rckd->srkgc", query_heads, old_keys, preferred_element_type=jnp.float32)
        * score_scale
    )
    new_scores = (
        jnp.einsum("srkgd,jrkd->srkgj", query_heads, fresh_keys, preferred_element_type=jnp.float32)
        * score_scale
    )
    old_visible = (jnp.arange(cache_rows, dtype=jnp.int32)[None, :] < cache_len[:, None])[
        None, :, None, None, :
    ]
    step_ids = jnp.arange(step_count, dtype=jnp.int32)
    new_visible = (step_ids[None, :] <= step_ids[:, None])[:, None, None, None, :]
    row_max = jnp.maximum(
        jnp.max(jnp.where(old_visible, old_scores, -jnp.inf), axis=4),
        jnp.max(jnp.where(new_visible, new_scores, -jnp.inf), axis=4),
    )[..., None]
    old_exp = jnp.where(old_visible, jnp.exp(old_scores - row_max), 0.0)
    new_exp = jnp.where(new_visible, jnp.exp(new_scores - row_max), 0.0)
    denom = jnp.sum(old_exp, axis=4, keepdims=True) + jnp.sum(new_exp, axis=4, keepdims=True)
    old_weights = (old_exp / denom).astype(jnp.bfloat16)
    new_weights = (new_exp / denom).astype(jnp.bfloat16)
    attended = jnp.einsum(
        "srkgc,rckd->srkgd", old_weights, old_values, preferred_element_type=jnp.float32
    )
    attended = attended + jnp.einsum(
        "srkgj,jrkd->srkgd", new_weights, fresh_vals, preferred_element_type=jnp.float32
    )
    return attended.reshape(step_count, row_total, key_heads * group_size * HD).astype(jnp.bfloat16)


def shards(
    queries,
    attn_keys,
    hidden,
    out_grad,
    logp_new,
    logp_old,
    logp_ref,
    lengths,
    rewards,
    groups,
    master,
    first_moment,
    second_moment,
    dec_hidden,
    dec_query,
    dec_key,
    cache_keys,
    cache_values,
    cache_len,
    out_weight,
):
    tok_rows = queries.shape[1]
    group_size = HEADS // KV
    score_scale = HD ** (-0.5)
    shard_index = lax.axis_index("ctx")
    slab_index = lax.axis_index("tp")
    query_position = shard_index * tok_rows + jnp.arange(tok_rows, dtype=jnp.int32)
    own_lengths = lengths[0]
    query_segment = segment_ids(own_lengths, query_position)
    advantage = group_advantage(rewards, groups)
    own_advantage = lax.dynamic_index_in_dim(advantage, slab_index, 0, keepdims=False)
    token_weight = token_coef(
        own_advantage, query_segment, logp_new[0], logp_old[0], logp_ref[0], float(rewards.size)
    )
    dout_rows = (token_weight[:, None] * out_grad[0].astype(jnp.float32)).astype(jnp.bfloat16)
    all_keys = lax.all_gather(attn_keys[0], "ctx", axis=0, tiled=True)
    slab_rows = all_keys.shape[0]
    key_segment = segment_ids(own_lengths, jnp.arange(slab_rows, dtype=jnp.int32))
    query_heads = queries[0].reshape(tok_rows, KV, group_size, HD)
    dout_heads = dout_rows.reshape(tok_rows, KV, group_size, HD)

    def block_scores(first_row, row_count):
        key_block = lax.dynamic_slice_in_dim(all_keys, first_row, row_count, 0).reshape(
            row_count, KV, HD
        )
        scores = (
            jnp.einsum("tkgd,ckd->tkgc", query_heads, key_block, preferred_element_type=jnp.float32)
            * score_scale
        )
        key_position = first_row + jnp.arange(row_count, dtype=jnp.int32)
        segment_part = lax.dynamic_slice_in_dim(key_segment, first_row, row_count, 0)
        visible = (key_position[None, :] <= query_position[:, None]) & (
            segment_part[None, :] == query_segment[:, None]
        )
        return (scores, visible[:, None, None, :])

    block_rows = math.gcd(slab_rows, 512)

    def softmax_pass(state_pair, block_index):
        running_max, running_sum = state_pair
        scores, visible = block_scores(block_index * block_rows, block_rows)
        new_max = jnp.maximum(running_max, jnp.max(jnp.where(visible, scores, -1e30), axis=3))
        running_sum = running_sum * jnp.exp(running_max - new_max) + jnp.sum(
            jnp.where(visible, jnp.exp(scores - new_max[..., None]), 0.0), axis=3
        )
        return ((new_max, running_sum), None)

    start_state = (
        jnp.full((tok_rows, KV, group_size), -1e30, jnp.float32),
        jnp.zeros((tok_rows, KV, group_size), jnp.float32),
    )
    (row_max, summed), _ = lax.scan(
        softmax_pass, start_state, jnp.arange(slab_rows // block_rows, dtype=jnp.int32)
    )
    log_total = row_max + jnp.log(summed)

    def value_rows(first_row, row_count):
        scores, visible = block_scores(first_row, row_count)
        weights = jnp.where(visible, jnp.exp(scores - log_total[..., None]), 0.0).astype(
            jnp.bfloat16
        )
        return jnp.einsum(
            "tkgc,tkgd->ckd", weights, dout_heads, preferred_element_type=jnp.float32
        ).reshape(row_count, KV * HD)

    piece_rows = math.gcd(lax.axis_size("ctx") * tok_rows, 512)

    def one_piece(block_index):
        return value_rows(block_index * piece_rows, piece_rows)

    pieces = lax.map(
        one_piece, jnp.arange(lax.axis_size("ctx") * tok_rows // piece_rows, dtype=jnp.int32)
    )
    dvalue = lax.psum_scatter(
        pieces.reshape(lax.axis_size("ctx") * tok_rows, KV * HD),
        "ctx",
        scatter_dimension=0,
        tiled=True,
    ).astype(jnp.bfloat16)
    local_hidden = hidden[0]
    gradient = lax.psum_scatter(
        lax.dot_general(
            local_hidden, dvalue, (((0,), (0,)), ((), ())), preferred_element_type=jnp.float32
        ),
        ("ctx", "tp"),
        scatter_dimension=0,
        tiled=True,
    )
    new_first = first_decay * first_moment + (1.0 - first_decay) * gradient
    new_second = second_decay * second_moment + (1.0 - second_decay) * gradient * gradient
    new_master = master - learn_rate * (
        new_first / (jnp.sqrt(new_second) + adam_eps) + decay_weight * master
    )
    master_bf = new_master.astype(jnp.bfloat16)
    all_rows = lax.all_gather(master_bf, ("ctx", "tp"), axis=0, tiled=True)
    col_width = master_bf.shape[1] // lax.axis_size("tp")
    rollout = lax.dynamic_slice_in_dim(all_rows, slab_index * col_width, col_width, 1)
    step_count = dec_hidden.shape[0]
    dec_rows = dec_hidden.shape[1]
    fresh_values = jnp.dot(
        dec_hidden.reshape(step_count * dec_rows, dec_hidden.shape[2]),
        rollout,
        preferred_element_type=jnp.float32,
    )
    fresh_values = fresh_values.reshape(step_count, dec_rows, rollout.shape[1]).astype(jnp.bfloat16)
    attended = decode_block(dec_query, dec_key, fresh_values, cache_keys, cache_values, cache_len)
    partial_out = jnp.dot(
        attended.reshape(step_count * dec_rows, attended.shape[2]),
        out_weight,
        preferred_element_type=jnp.float32,
    )
    partial_out = partial_out.reshape(step_count, dec_rows, out_weight.shape[1])
    step_outs = []
    for step_index in range(step_count):
        step_outs.append(lax.psum(partial_out[step_index], "tp"))
    dec_out = jnp.stack(step_outs, axis=0).astype(jnp.bfloat16)
    return (new_master, new_first, new_second, rollout, dec_out)


def solution(mesh):
    return jax.shard_map(
        shards,
        mesh=mesh,
        in_specs=(
            P("tp", "ctx", None),
            P("tp", "ctx", None),
            P("tp", "ctx", None),
            P("tp", "ctx", None),
            P("tp", "ctx"),
            P("tp", "ctx"),
            P("tp", "ctx"),
            P("tp", None),
            P(),
            P(),
            P(("ctx", "tp"), None),
            P(("ctx", "tp"), None),
            P(("ctx", "tp"), None),
            P(None, "ctx", None),
            P(None, "ctx", "tp"),
            P(None, "ctx", "tp"),
            P("ctx", None, "tp"),
            P("ctx", None, "tp"),
            P("ctx"),
            P("tp", None),
        ),
        out_specs=(
            P(("ctx", "tp"), None),
            P(("ctx", "tp"), None),
            P(("ctx", "tp"), None),
            P(None, "tp"),
            P(None, "ctx", None),
        ),
        check_vma=False,
    )
```

profile of v0, /device:TPU:1, one launch (start us, length us, event | category | flops | bytes accessed | tf_op | source)
XLA Modules:
  0.0 1287.5 jit_solution(16659602423198218182)
XLA Ops:
  7.2 1.8 copy.144
  9.9 1.6 copy.145
  12.9 2.7 copy.150
  15.9 2.9 multiply_convert_fusion
  18.8 76.6 %all-gather.6.cloned.1.call-done = bf16[1,4096,512]{1,2,0:T(8,128)(2,1)} async-done(((bf16[1,128,512]{1,2,0:T(8,128)(2,1)}), bf16[1,4096,512]{1,2,0:T(8,128)(2,1)}) %all-gather.6.cloned.1.call-update) | async-done | bytes 4194320 | tf_op jit(solution)/shard_map/all_gather | solution.py:124
  95.4 99.8 %while.25 = (s32[]{:T(128)}, f32[128,4,8]{0,2,1:T(8,128)S(1)}, f32[128,4,8]{0,2,1:T(8,128)S(1)}, s32[8]{0:T(128)S(1)}, s32[4096]{0:T(1024)S(1)}, /*index=5*/s32[...) while((s32[]{:T(128)}, f32[128,4,8]{0,2,1:T(8,128)S(1)}, ...), condition=%wide.region_6.7_spmd.clone, body=%wide.region_3.0_spmd.clone.sunk | while | flops 551768704 | bytes 19820240 | solution.py:160
  98.0 4.7 fusion.92
  102.7 5.1 fusion.93
  110.5 4.7 fusion.92
  115.2 5.1 fusion.93
  123.0 4.7 fusion.92
  127.7 5.1 fusion.93
  135.5 4.7 fusion.92
  140.1 5.1 fusion.93
  147.9 4.7 fusion.92
  152.6 5.1 fusion.93
  160.4 4.7 fusion.92
  165.1 5.1 fusion.93
  172.9 4.7 fusion.92
  177.5 5.1 fusion.93
  185.3 4.7 fusion.92
  190.0 5.1 fusion.93
  195.2 84.1 %while.24 = (s32[]{:T(128)}, f32[8,512,512]{2,1,0:T(8,128)}, s32[8]{0:T(128)S(1)}, s32[4096]{0:T(1024)S(1)}, s32[128]{0:T(128)S(1)}, /*index=5*/bf16[4096,512]{0...) while((s32[]{:T(128)}, f32[8,512,512]{2,1,0:T(8,128)}, ...), condition=%wide.region_11.12_spmd.clone, body=%wide.region_10.11_spmd.clone.sunk | while | flops 1082327680 | bytes 9072847 | solution.py:179
  197.9 5.3 fusion.89
  203.1 1.6 copy.207
  208.4 5.3 fusion.89
  213.6 1.6 copy.207
  218.9 5.3 fusion.89
  224.2 1.6 copy.207
  229.4 5.3 fusion.89
  234.7 1.6 copy.207
  239.9 5.3 fusion.89
  245.2 1.6 copy.207
  250.4 5.3 fusion.89
  255.6 1.6 copy.207
  260.9 5.3 fusion.89
  271.4 5.3 fusion.89
  276.7 1.6 copy.207
  279.4 183.9 %reduce-scatter.5.cloned.1.call-done = f32[128,512]{1,0:T(8,128)} async-done(((f32[4096,512]{1,0:T(8,128)}), f32[128,512]{1,0:T(8,128)}) %reduce-scatter.5.cloned.1.call-update) | async-done | bytes 262160 | tf_op jit(solution)/shard_map/reduce_scatter | solution.py:182
  463.2 6.5 convolution_bitcast_fusion
  469.7 11.4 copy.177
  481.4 665.6 %reduce-scatter.7.cloned.1.call-done = f32[40,512]{1,0:T(8,128)} async-done(((f32[5120,512]{1,0:T(8,128)}), f32[40,512]{1,0:T(8,128)}) %reduce-scatter.7.cloned.1.call-update) | async-done | bytes 81936 | tf_op jit(solution)/shard_map/reduce_scatter | solution.py:189
  1147.1 1.6 fusion.62
  1150.2 3.9 fusion.23
  1156.0 63.0 %all-gather.4.cloned.1.call-done = bf16[5120,512]{1,0:T(8,128)(2,1)} async-done(((bf16[40,512]{1,0:T(8,128)(2,1)}), bf16[5120,512]{1,0:T(8,128)(2,1)}) %all-gather.4.cloned.1.call-update) | async-done | bytes 5242896 | tf_op jit(solution)/shard_map/all_gather | solution.py:203
  1221.6 5.5 fusion.39
  1228.4 50.3 %all-reduce.2 = (bf16[32,5120]{1,0:T(8,128)(2,1)S(1)}, bf16[32,5120]{1,0:T(8,128)(2,1)S(1)}, bf16[32,5120]{1,0:T(8,128)(2,1)}, bf16[32,5120]{1,0:T(8,128)(2,1)}) all-reduce(f32[32,5120]{1,0:T(8,128)S(1)} %get-tuple-element.345, f32[32,5120]{1,0:T(8,128)} %get-tuple-element.346, ...), channel_id=1, replica_groups=mesh['ctx'=32,'tp'=4] {'tp'}, use_global_device_ids=true, to_apply=%region_21.22 | all-reduce | flops 655360 | bytes 3932160 | tf_op jit(solution)/shard_map/psum | solution.py:223
  1278.7 2.3 pad_maximum_fusion
  (203 shorter events, 51.7 us)
Async XLA Ops:
  7.2 456.1 %copy-start = (bf16[1,128,5120]{2,1,0:T(8,128)(2,1)S(1)}, bf16[1,128,5120]{2,1,0:T(8,128)(2,1)}, u32[]{:S(2)}) copy-start(bf16[1,128,5120]{2,1,0:T(8,128)(2,1)} %param.26) | copy-start | bytes 3932164
  7.2 5.1 copy-start.7
  7.2 5.3 copy-start.8
  7.2 88.2 %all-gather.6.cloned.1.call-start = ((), (), s32[]{:S(2)}) async-start(), calls=%async_computation.4 | async-start | bytes 4325376 | tf_op jit(solution)/shard_map/all_gather | solution.py:124
  9.0 454.2 %reduce-scatter.5.cloned.1.call-start = ((), (), s32[]{:S(2)}) async-start(), calls=%async_computation.2 | async-start | bytes 8650752 | tf_op jit(solution)/shard_map/reduce_scatter | solution.py:182
  11.6 4.3 copy-start.9
  11.6 4.3 copy-start.10
  11.6 4.3 copy-start.11
  279.3 867.7 %reduce-scatter.7.cloned.1.call-start = ((), (), s32[]{:S(2)}) async-start(), calls=%async_computation.5 | async-start | bytes 10567680 | tf_op jit(solution)/shard_map/reduce_scatter | solution.py:189
  481.1 665.9 %copy-start.4 = (f32[40,512]{1,0:T(8,128)S(1)}, f32[40,512]{1,0:T(8,128)}, u32[]{:S(2)}) copy-start(f32[40,512]{1,0:T(8,128)} %param.34) | copy-start | bytes 245764
  481.1 665.9 %copy-start.5 = (f32[40,512]{1,0:T(8,128)S(1)}, f32[40,512]{1,0:T(8,128)}, u32[]{:S(2)}) copy-start(f32[40,512]{1,0:T(8,128)} %param.36) | copy-start | bytes 245764
  481.1 665.9 %copy-start.6 = (f32[40,512]{1,0:T(8,128)S(1)}, f32[40,512]{1,0:T(8,128)}, u32[]{:S(2)}) copy-start(f32[40,512]{1,0:T(8,128)} %param.35) | copy-start | bytes 245764
  481.1 667.6 %copy-start.3 = (bf16[4,32,1024]{2,1,0:T(8,128)(2,1)S(1)}, bf16[4,32,1024]{2,1,0:T(8,128)(2,1)}, u32[]{:S(2)}) copy-start(bf16[4,32,1024]{2,1,0:T(8,128)(2,1)} %param.38) | copy-start | bytes 786436
  481.1 667.6 %copy-start.14 = (bf16[4,32,128]{2,1,0:T(8,128)(2,1)S(1)}, bf16[4,32,128]{2,1,0:T(8,128)(2,1)}, u32[]{:S(2)}) copy-start(bf16[4,32,128]{2,1,0:T(8,128)(2,1)} %param.39) | copy-start | bytes 98308
  481.2 668.9 %copy-start.12 = (s32[32]{0:T(128)S(1)}, s32[32]{0:T(128)}, u32[]{:S(2)}) copy-start(s32[32]{0:T(128)} %param.42) | copy-start | bytes 388
  481.2 737.8 %all-gather.4.cloned.1.call-start = ((), (), s32[]{:S(2)}) async-start(), calls=%async_computation.3 | async-start | bytes 5283840 | tf_op jit(solution)/shard_map/all_gather | solution.py:203
  1150.2 5.0 copy-start.13
  1219.0 1.7 copy-start.2
  1220.5 1.2 copy-start.1
Sparse Core Ops, SparseCore 0:
  11.4 83.9 all-gather.5
  279.5 183.7 reduce-scatter.4
  481.3 665.6 reduce-scatter.6
  1150.5 68.4 all-gather.3
where the time goes:
time: 1290 us
  waiting for transfers between devices  989 us (77%)
  matrix products  98.2 us (8%)
  local copies, waits for them, and re-layouts  70.6 us (5%)
  other arithmetic  53.8 us (4%)
  blocking collectives  50.3 us (4%)
  between operations  14.1 us (1%)
    reduce_scatter x1, waiting for transfers between devices, shards(): lax.psum_scatter(lax.dot_general(local_hidden, dvalue, (((0,), (0,)), (()...  666 us
    reduce_scatter x1, waiting for transfers between devices, shards(): lax.psum_scatter(pieces.reshape(lax.axis_size('ctx') * tok_rows, KV * HD)...  184 us
    all_gather x1, waiting for transfers between devices, shards(): all_keys = lax.all_gather(attn_keys[0], 'ctx', axis=0, tiled=True)  76.6 us
    all_gather x1, waiting for transfers between devices, shards(): all_rows = lax.all_gather(master_bf, ('ctx', 'tp'), axis=0, tiled=True)  63 us
    psum x1, blocking collectives, shards(): step_outs.append(lax.psum(partial_out[step_index], 'tp'))  50.3 us
    dot_general x8, matrix products, value_rows(): jnp.einsum('tkgc,tkgd->ckd', weights, dout_heads, preferred_element_type=...  42.1 us
    reduce_sum x8, other arithmetic, softmax_pass(): jnp.sum(jnp.where(visible, jnp.exp(scores - new_max[..., None]), 0.0), ax...  41 us
    dot_general x8, matrix products, block_scores(): jnp.einsum('tkgd,ckd->tkgc', query_heads, key_block, preferred_element_ty...  37.3 us
  transfers between devices with their start and end apart: 4, of which 4 were waited for; matrix products, arithmetic and copies ran while one was open for 1% of the time, Pallas kernels for 0%

commit v1 on v0

v1 whole, which is shorter than its diff:
```python
import math

import jax
import jax.numpy as jnp
from jax import lax
from jax.experimental import pallas as pl
from jax.experimental.pallas import tpu as pltpu
from jax.sharding import PartitionSpec as P

HD = 128
HEADS = 32
KV = 4
GROUP = HEADS // KV
BLOCK = 128
NX, NZ, NY, NT = 4, 4, 2, 4
NG = NZ * NY
SLAB = NX * NG * BLOCK
CHUNK = 512
ROWS = GROUP * BLOCK
LOWEST = -1e30

first_decay = 0.9
second_decay = 0.95
adam_eps = 1e-08
learn_rate = 0.001
decay_weight = 0.1
kl_weight = 0.1
exp2_scale = HD ** (-0.5) * math.log2(math.e)


def route(value, target):
    pairs = []
    for source in range(NX * NG * NT):
        ctx, t = divmod(source, NT)
        x, g = divmod(ctx, NG)
        z, y = divmod(g, NY)
        nx, nz, ny, nt = target(x, z, y, t)
        pairs.append((source, (((nx % NX) * NZ + nz % NZ) * NY + ny % NY) * NT + nt % NT))
    return lax.ppermute(value, ("ctx", "tp"), pairs)


def pick(value, index, axis=0):
    return lax.dynamic_index_in_dim(value, index, axis, keepdims=False)


def segment_ids(lengths_row, position):
    doc_ends = jnp.cumsum(lengths_row)
    return jnp.sum((position[:, None] >= doc_ends[None, :]).astype(jnp.int32), axis=1)


def group_advantage(rewards, groups):
    flat_reward = rewards.reshape(-1)
    flat_group = groups.reshape(-1)
    same_group = (flat_group[:, None] == flat_group[None, :]).astype(jnp.float32)
    group_mean = jnp.sum(same_group * flat_reward[None, :], axis=1) / jnp.sum(same_group, axis=1)
    return (flat_reward - group_mean).reshape(rewards.shape)


def token_coef(own_advantage, segment, policy_logp, sample_logp, frozen_logp, divisor):
    labels = jnp.arange(own_advantage.shape[0], dtype=jnp.int32)
    picked = jnp.sum(
        jnp.where(segment[:, None] == labels[None, :], own_advantage[None, :], 0.0), axis=1
    )
    return (
        -jnp.exp(policy_logp - sample_logp) * picked
        + kl_weight * (1.0 - jnp.exp(frozen_logp - policy_logp))
    ) / divisor


def heads_as_rows(block):
    return jnp.concatenate([block[:, h * HD : (h + 1) * HD] for h in range(GROUP)], axis=0)


def chunk_range(block_start, bound):
    seen_from = jnp.where(block_start >= bound, bound, 0)
    first = seen_from // CHUNK
    stop = (block_start + BLOCK - 1) // CHUNK + 1
    return first, stop


def chunk_hidden(chunk_start, block_start, bound):
    key_at = chunk_start + lax.broadcasted_iota(jnp.int32, (CHUNK, ROWS), 0)
    query_at = block_start + (lax.broadcasted_iota(jnp.int32, (1, ROWS), 1) & (BLOCK - 1))
    from_at = jnp.where(query_at >= bound, bound, 0)
    return (key_at <= query_at) & (key_at >= from_at)


def chunk_whole(chunk_start, block_start, bound):
    latest_from = jnp.where(block_start + BLOCK - 1 >= bound, bound, 0)
    return (chunk_start + CHUNK - 1 <= block_start) & (chunk_start >= latest_from)


def fill_keys(where_ref, keys_ref, key_rows):
    head = where_ref[1]
    for x in range(NX):
        slot = lax.rem(head - x + NX, NX)
        for g in range(NG):
            key_rows[pl.ds((x * NG + g) * BLOCK, BLOCK), :] = keys_ref[g, slot]


def totals_kernel(where_ref, queries_ref, keys_ref, total_ref, key_rows, score_ref):
    g, head, bound = where_ref[0], where_ref[1], where_ref[2]
    fill_keys(where_ref, keys_ref, key_rows)

    def one_block(slot, _):
        block_start = (lax.rem(head - slot + NX, NX) * NG + g) * BLOCK
        query_rows = heads_as_rows(queries_ref[slot])
        first, stop = chunk_range(block_start, bound)

        def one_chunk(chunk, state):
            running_max, running_sum = state
            chunk_start = pl.multiple_of(chunk * CHUNK, CHUNK)
            score_ref[...] = lax.dot_general(
                key_rows[pl.ds(chunk_start, CHUNK), :],
                query_rows,
                (((1,), (1,)), ((), ())),
                preferred_element_type=jnp.float32,
            )

            @pl.when(jnp.logical_not(chunk_whole(chunk_start, block_start, bound)))
            def _():
                visible = chunk_hidden(chunk_start, block_start, bound)
                score_ref[...] = jnp.where(visible, score_ref[...], LOWEST)

            scores = score_ref[...]
            new_max = jnp.maximum(
                running_max, jnp.max(scores, axis=0, keepdims=True) * exp2_scale
            )
            running_sum = running_sum * jnp.exp2(running_max - new_max) + jnp.sum(
                jnp.exp2(scores * exp2_scale - new_max), axis=0, keepdims=True
            )
            return new_max, running_sum

        row_max, row_sum = lax.fori_loop(
            first,
            stop,
            one_chunk,
            (jnp.full((1, ROWS), LOWEST, jnp.float32), jnp.zeros((1, ROWS), jnp.float32)),
        )
        total_ref[slot] = row_max + jnp.log2(row_sum)
        return 0

    lax.fori_loop(0, NX, one_block, 0)


def values_kernel(where_ref, queries_ref, keys_ref, dout_ref, total_ref, out_ref, key_rows, sums):
    g, head, bound = where_ref[0], where_ref[1], where_ref[2]
    fill_keys(where_ref, keys_ref, key_rows)
    sums[...] = jnp.zeros_like(sums)

    def one_block(slot, _):
        block_start = (lax.rem(head - slot + NX, NX) * NG + g) * BLOCK
        query_rows = heads_as_rows(queries_ref[slot])
        dout_rows = heads_as_rows(dout_ref[slot])
        log_total = total_ref[slot]
        first, stop = chunk_range(block_start, bound)

        def one_chunk(chunk, _):
            chunk_start = pl.multiple_of(chunk * CHUNK, CHUNK)
            rows = pl.ds(chunk_start, CHUNK)
            scores = lax.dot_general(
                key_rows[rows, :],
                query_rows,
                (((1,), (1,)), ((), ())),
                preferred_element_type=jnp.float32,
            )
            whole = chunk_whole(chunk_start, block_start, bound)

            def add(weights):
                sums[rows, :] += jnp.dot(
                    weights.astype(jnp.bfloat16), dout_rows, preferred_element_type=jnp.float32
                )

            @pl.when(whole)
            def _():
                add(jnp.exp2(scores * exp2_scale - log_total))

            @pl.when(jnp.logical_not(whole))
            def _():
                visible = chunk_hidden(chunk_start, block_start, bound)
                add(jnp.where(visible, jnp.exp2(scores * exp2_scale - log_total), 0.0))

            return 0

        return lax.fori_loop(first, stop, one_chunk, 0)

    lax.fori_loop(0, NX, one_block, 0)
    for x in range(NX):
        for g_to in range(NG):
            out_ref[g_to, x] = sums[pl.ds((x * NG + g_to) * BLOCK, BLOCK), :].astype(out_ref.dtype)


def in_smem():
    return pl.BlockSpec(memory_space=pltpu.SMEM)


def in_vmem():
    return pl.BlockSpec(memory_space=pltpu.VMEM)


def attention_totals(where, queries, keys):
    return pl.pallas_call(
        totals_kernel,
        out_shape=jax.ShapeDtypeStruct((NX, 1, ROWS), jnp.float32),
        in_specs=[in_smem(), in_vmem(), in_vmem()],
        out_specs=in_vmem(),
        scratch_shapes=[
            pltpu.VMEM((SLAB, HD), jnp.bfloat16),
            pltpu.VMEM((CHUNK, ROWS), jnp.float32),
        ],
        compiler_params=pltpu.CompilerParams(vmem_limit_bytes=32 * 1024 * 1024),
        cost_estimate=pl.CostEstimate(
            flops=SLAB * SLAB * HD, bytes_accessed=2 << 20, transcendentals=SLAB * SLAB // 2
        ),
        name="attention_totals",
    )(where, queries, keys)


def attention_values(where, queries, keys, dout, totals):
    return pl.pallas_call(
        values_kernel,
        out_shape=jax.ShapeDtypeStruct((NG, NX, BLOCK, HD), jnp.bfloat16),
        in_specs=[in_smem(), in_vmem(), in_vmem(), in_vmem(), in_vmem()],
        out_specs=in_vmem(),
        scratch_shapes=[
            pltpu.VMEM((SLAB, HD), jnp.bfloat16),
            pltpu.VMEM((SLAB, HD), jnp.float32),
        ],
        compiler_params=pltpu.CompilerParams(vmem_limit_bytes=32 * 1024 * 1024),
        cost_estimate=pl.CostEstimate(
            flops=2 * SLAB * SLAB * HD, bytes_accessed=4 << 20, transcendentals=SLAB * SLAB // 2
        ),
        name="attention_values",
    )(where, queries, keys, dout, totals)


def decode_cached(dec_query, dec_key, cache_keys, cache_values, cache_len):
    step_count, row_total = dec_query.shape[:2]
    cache_rows = cache_keys.shape[1]
    score_scale = HD ** (-0.5)
    query_heads = dec_query.reshape(step_count, row_total, GROUP, HD)
    old_scores = (
        jnp.einsum("srgd,rcd->srgc", query_heads, cache_keys, preferred_element_type=jnp.float32)
        * score_scale
    )
    new_scores = (
        jnp.einsum("srgd,jrd->srgj", query_heads, dec_key, preferred_element_type=jnp.float32)
        * score_scale
    )
    old_visible = (jnp.arange(cache_rows, dtype=jnp.int32)[None, :] < cache_len[:, None])[
        None, :, None, :
    ]
    step_ids = jnp.arange(step_count, dtype=jnp.int32)
    new_visible = (step_ids[None, :] <= step_ids[:, None])[:, None, None, :]
    row_max = jnp.maximum(
        jnp.max(jnp.where(old_visible, old_scores, -jnp.inf), axis=3),
        jnp.max(jnp.where(new_visible, new_scores, -jnp.inf), axis=3),
    )[..., None]
    old_exp = jnp.where(old_visible, jnp.exp(old_scores - row_max), 0.0)
    new_exp = jnp.where(new_visible, jnp.exp(new_scores - row_max), 0.0)
    denom = jnp.sum(old_exp, axis=3, keepdims=True) + jnp.sum(new_exp, axis=3, keepdims=True)
    old_weights = (old_exp / denom).astype(jnp.bfloat16)
    new_weights = (new_exp / denom).astype(jnp.bfloat16)
    attended = jnp.einsum(
        "srgc,rcd->srgd", old_weights, cache_values, preferred_element_type=jnp.float32
    )
    return attended, new_weights


def sum_over_tp(value, core, bf=jnp.bfloat16):
    half = value.shape[1] // 2
    flip_core = lambda x, z, y, t: (x, z, y, t ^ 1)
    flip_chip = lambda x, z, y, t: (x, z, y, t ^ 2)
    mine = lax.dynamic_slice_in_dim(value, core * half, half, 1)
    other = lax.dynamic_slice_in_dim(value, (1 - core) * half, half, 1)
    on_chip = mine + route(other, flip_core)
    both = (on_chip + route(on_chip.astype(bf), flip_chip).astype(jnp.float32)).astype(bf)
    rest = route(both, flip_core)
    low = jnp.where(core == 0, both, rest)
    high = jnp.where(core == 0, rest, both)
    return jnp.concatenate([low, high], axis=1)


def shards(
    queries,
    attn_keys,
    hidden,
    out_grad,
    logp_new,
    logp_old,
    logp_ref,
    lengths,
    rewards,
    groups,
    master,
    first_moment,
    second_moment,
    dec_hidden,
    dec_query,
    dec_key,
    cache_keys,
    cache_values,
    cache_len,
    out_weight,
):
    bf, f32 = jnp.bfloat16, jnp.float32
    ctx = lax.axis_index("ctx")
    t = lax.axis_index("tp")
    x, g = ctx // NG, ctx % NG
    z, y = g // NY, g % NY

    def to_owner(r):
        return lambda x, z, y, s: (s + x + r, z, y, x + r)

    own_lengths = route(lengths, to_owner(0))[0]
    key_heads = attn_keys[0].reshape(BLOCK, KV, HD)
    query_heads = queries[0].reshape(BLOCK, KV, GROUP * HD)
    key_parts = jnp.stack(
        [route(pick(key_heads, (x + r) % KV, 1), to_owner(r)) for r in range(NX)]
    )
    query_parts = jnp.stack(
        [route(pick(query_heads, (x + r) % KV, 1), to_owner(r)) for r in range(NX)]
    )
    keys = lax.all_to_all(
        jnp.broadcast_to(key_parts[None], (NG, NX, BLOCK, HD)),
        "ctx",
        split_axis=0,
        concat_axis=0,
        axis_index_groups=[[a * NG + b for b in range(NG)] for a in range(NX)],
        tiled=True,
    )

    query_position = ctx * BLOCK + jnp.arange(BLOCK, dtype=jnp.int32)
    query_segment = segment_ids(lengths[0], query_position)
    own_advantage = pick(group_advantage(rewards, groups), t)
    token_weight = token_coef(
        own_advantage, query_segment, logp_new[0], logp_old[0], logp_ref[0], float(rewards.size)
    )
    dout_rows = (token_weight[:, None] * out_grad[0].astype(f32)).astype(bf)
    dout_heads = dout_rows.reshape(BLOCK, KV, GROUP * HD)
    dout_parts = jnp.stack(
        [route(pick(dout_heads, (x + r) % KV, 1), to_owner(r)) for r in range(NX)]
    )
    hidden_parts = [route(hidden[0], to_owner(r)) for r in range(NX)]

    state = jnp.stack([master, first_moment, second_moment]).reshape(3, 40, KV, HD)

    def over_tp(d):
        return lambda x, z, y, t: (x, z, y, t ^ d)

    moved = [pick(state, t, 2)] + [
        route(pick(state, t ^ d, 2), over_tp(d)) for d in range(1, NT)
    ]
    moved = jnp.stack(moved)
    by_row = jnp.stack([pick(moved, t ^ d) for d in range(NT)], axis=1)
    old_master, old_first, old_second = by_row.reshape(3, NT * 40, HD)

    cached, new_weights = decode_cached(dec_query, dec_key, cache_keys, cache_values, cache_len)

    where = jnp.stack([g, t, own_lengths[0]]).astype(jnp.int32)
    totals = attention_totals(where, query_parts, keys)
    partial = attention_values(where, query_parts, keys, dout_parts, totals)

    partial = partial.reshape(NZ, NY, NX, BLOCK, HD)

    def along_z(d):
        return lambda x, z, y, t: (x, z + d, y, t)

    over_z = pick(partial, z).astype(f32)
    for d in range(1, NZ):
        over_z = over_z + route(pick(partial, (z + d) % NZ), along_z(d)).astype(f32)
    flip_y = lambda x, z, y, t: (x, z, y + 1, t)
    dvalue = (pick(over_z, y) + route(pick(over_z, 1 - y), flip_y)).astype(bf)

    gradient = jnp.zeros((5120, HD), f32)
    for r in range(NX):
        gradient = gradient + lax.dot_general(
            hidden_parts[r],
            pick(dvalue, (t - r) % NX),
            (((0,), (0,)), ((), ())),
            preferred_element_type=f32,
        )
    terms = lax.all_to_all(
        gradient.astype(bf).reshape(NX * NG, NT * 40, HD),
        "ctx",
        split_axis=0,
        concat_axis=0,
        tiled=True,
    )
    gradient = jnp.sum(terms.astype(f32), axis=0)

    new_first = first_decay * old_first + (1.0 - first_decay) * gradient
    new_second = second_decay * old_second + (1.0 - second_decay) * gradient * gradient
    new_master = old_master - learn_rate * (
        new_first / (jnp.sqrt(new_second) + adam_eps) + decay_weight * old_master
    )
    rounded = new_master.astype(bf)
    rollout = lax.all_to_all(
        jnp.broadcast_to(rounded[None], (NX * NG, NT * 40, HD)),
        "ctx",
        split_axis=0,
        concat_axis=0,
        tiled=True,
    ).reshape(5120, HD)

    news = jnp.stack([new_master, new_first, new_second]).reshape(3, NT, 40, HD)
    back = [pick(news, t, 1)] + [
        route(pick(news, t ^ d, 1), over_tp(d)) for d in range(1, NT)
    ]
    back = jnp.stack(back)
    back = jnp.stack([pick(back, t ^ d) for d in range(NT)], axis=2)
    new_master, new_first, new_second = back.reshape(3, 40, KV * HD)

    step_count, dec_rows = dec_hidden.shape[:2]
    fresh = jnp.dot(
        dec_hidden.reshape(step_count * dec_rows, dec_hidden.shape[2]),
        rollout,
        preferred_element_type=f32,
    )
    fresh = fresh.reshape(step_count, dec_rows, HD).astype(bf).astype(f32)
    attended = cached
    for j in range(step_count):
        attended = attended + new_weights[..., j : j + 1].astype(f32) * fresh[j][None, :, None, :]
    attended = attended.astype(bf).reshape(step_count * dec_rows, GROUP * HD)
    partial_out = jnp.dot(attended, out_weight, preferred_element_type=f32)
    dec_out = sum_over_tp(partial_out, t % 2).reshape(step_count, dec_rows, out_weight.shape[1])
    return (new_master, new_first, new_second, rollout, dec_out)


def solution(mesh):
    return jax.shard_map(
        shards,
        mesh=mesh,
        in_specs=(
            P("tp", "ctx", None),
            P("tp", "ctx", None),
            P("tp", "ctx", None),
            P("tp", "ctx", None),
            P("tp", "ctx"),
            P("tp", "ctx"),
            P("tp", "ctx"),
            P("tp", None),
            P(),
            P(),
            P(("ctx", "tp"), None),
            P(("ctx", "tp"), None),
            P(("ctx", "tp"), None),
            P(None, "ctx", None),
            P(None, "ctx", "tp"),
            P(None, "ctx", "tp"),
            P("ctx", None, "tp"),
            P("ctx", None, "tp"),
            P("ctx"),
            P("tp", None),
        ),
        out_specs=(
            P(("ctx", "tp"), None),
            P(("ctx", "tp"), None),
            P(("ctx", "tp"), None),
            P(None, "tp"),
            P(None, "ctx", None),
        ),
        check_vma=False,
    )
```

time: 1290 us -> 364 us (0.28)
  waiting for transfers between devices: 989 us -> 115 us
  starting transfers between devices: 0.34 us -> 150 us
  matrix products: 98.2 us -> 18.9 us
  blocking collectives: 50.3 us -> 0 us
  local copies, waits for them, and re-layouts: 70.6 us -> 30.3 us
  other arithmetic: 53.8 us -> 19.1 us
  Pallas kernels: 0 us -> 27.1 us
    reduce_scatter x2 -> x0, waiting for transfers between devices: 849 us -> none  [the longest x1 666 us: shards(): lax.psum_scatter(lax.dot_general(local_hidden, dvalue, (((0,), (0,)), (()...]
    all_gather x2 -> x0, waiting for transfers between devices: 140 us -> none  [the longest x1 76.6 us: shards(): all_keys = lax.all_gather(attn_keys[0], 'ctx', axis=0, tiled=True)]
    ppermute x0 -> x30, waiting for transfers between devices: none -> 97.6 us  [route(): return lax.ppermute(value, ('ctx', 'tp'), pairs)]
    ppermute x0 -> x30, starting transfers between devices: none -> 80.4 us  [route(): return lax.ppermute(value, ('ctx', 'tp'), pairs)]
    dot_general x22 -> x8, matrix products: 97.7 us -> 18.4 us  [the longest x4 7.58 us: shards(): lax.dot_general(hidden_parts[r], pick(dvalue, (t - r) % NX), (((0,), (0,)...]
    all_to_all x0 -> x3, starting transfers between devices: none -> 69.6 us  [the longest x1 56.9 us: shards(): lax.all_to_all(gradient.astype(bf).reshape(NX * NG, NT * 40, HD), 'ctx',...]
    psum x1 -> x0, blocking collectives: 50.3 us -> none  [shards(): step_outs.append(lax.psum(partial_out[step_index], 'tp'))]
    reduce_sum x10 -> x3, other arithmetic: 42.1 us -> 1.19 us  [the longest x1 0.72 us: decode_cached(): jnp.sum(old_exp, axis=3, keepdims=True)]
  transfers between devices with their start and end apart: 4 -> 33, of which waited for: 4 -> 14; matrix products, arithmetic and copies ran while one was open for 1% -> 12% of each run, Pallas kernels for 0% -> 7%
where the time goes in v1:
time: 364 us; the launch traced here: 362 us
  starting transfers between devices  150 us (41%)
  waiting for transfers between devices  115 us (32%)
  local copies, waits for them, and re-layouts  30.3 us (8%)
  Pallas kernels  27.1 us (7%)
  other arithmetic  19.1 us (5%)
  matrix products  18.9 us (5%)
    ppermute x30, waiting for transfers between devices, route(): return lax.ppermute(value, ('ctx', 'tp'), pairs)  97.6 us
    ppermute x30, starting transfers between devices, route(): return lax.ppermute(value, ('ctx', 'tp'), pairs)  80.4 us
    all_to_all x1, starting transfers between devices, shards(): lax.all_to_all(gradient.astype(bf).reshape(NX * NG, NT * 40, HD), 'ctx',...  56.9 us
    pallas_call x1, Pallas kernels, attention_totals(): pl.pallas_call(totals_kernel, out_shape=jax.ShapeDtypeStruct((NX, 1, ROWS...  14 us
    unnamed x66, local copies, waits for them, and re-layouts  14 us
    pallas_call x1, Pallas kernels, attention_values(): pl.pallas_call(values_kernel, out_shape=jax.ShapeDtypeStruct((NG, NX, BLO...  13.1 us
    all_to_all x1, waiting for transfers between devices, shards(): lax.all_to_all(jnp.broadcast_to(rounded[None], (NX * NG, NT * 40, HD)), '...  13 us
    dot_general x4, matrix products, shards(): lax.dot_general(hidden_parts[r], pick(dvalue, (t - r) % NX), (((0,), (0,)...  7.58 us
  transfers between devices with their start and end apart: 33, of which 14 were waited for; matrix products, arithmetic and copies ran while one was open for 12% of the time, Pallas kernels for 7%

profile of v1, /device:TPU:1, one launch (start us, length us, event | category | flops | bytes accessed | tf_op | source)
XLA Modules:
  0.0 361.9 jit_solution(13345582991242109720)
XLA Ops:
  2.0 4.5 %collective-permute-start.8 = (bf16[128,128]{1,0:T(8,128)(2,1)S(1)}, bf16[128,128]{1,0:T(8,128)(2,1)}, u32[]{:S(2)}, u32[]{:S(2)}) collective-permute-start(bf16[128,128]{1,0:T(8,128)(2,1)S(1)} %bitcast.274), channel_id=1, source_target_pairs={{0,0},{1,32},{2,64},{3,96},{4,4},{5,36},{6,68},{7,100},{8,8},{9,40... | collective-permute-start | bytes 98312 | tf_op jit(solution)/shard_map/ppermute | solution.py:39
  6.7 5.4 %collective-permute-start.9 = (bf16[128,128]{1,0:T(8,128)(2,1)S(1)}, bf16[128,128]{1,0:T(8,128)(2,1)}, u32[]{:S(2)}, u32[]{:S(2)}) collective-permute-start(bf16[128,128]{1,0:T(8,128)(2,1)S(1)} %bitcast.273), channel_id=1, source_target_pairs={{0,33},{1,65},{2,97},{3,1},{4,37},{5,69},{6,101},{7,5},{8,41},{9,7... | collective-permute-start | bytes 98312 | tf_op jit(solution)/shard_map/ppermute | solution.py:39
  12.1 3.0 collective-permute-start.10
  15.3 2.1 collective-permute-start.11
  17.4 2.3 collective-permute-start.3
  19.6 1.9 reshape_squeeze.6
  21.5 3.1 constant_dynamic-slice_fusion.13
  30.9 2.0 collective-permute-start.4
  33.0 8.5 %collective-permute-start.5 = (bf16[128,1024]{1,0:T(8,128)(2,1)}, bf16[128,1024]{1,0:T(8,128)(2,1)}, u32[]{:S(2)}, u32[]{:S(2)}) collective-permute-start(bf16[128,1024]{1,0:T(8,128)(2,1)} %bitcast.226), channel_id=1, source_target_pairs={{0,33},{1,65},{2,97},{3,1},{4,37},{5,69},{6,101},{7,5},{8,41},{9,7... | collective-permute-start | bytes 786440 | tf_op jit(solution)/shard_map/ppermute | solution.py:39
  41.5 1.9 collective-permute-start.6
  43.5 1.9 collective-permute-start.7
  47.4 7.5 %all-to-all-start = ((bf16[8,4,128,128]{3,2,1,0:T(8,128)(2,1)}), bf16[8,4,128,128]{3,2,1,0:T(8,128)(2,1)S(1)}, u32[]{:S(2)}, u32[]{:S(2)}) async-start(bf16[8,4,128,128]{3,2,1,0:T(8,128)(2,1)} %broadcast_in_dim.79), calls=%async_computation | async-start | bytes 2097152 | tf_op jit(solution)/shard_map/all_to_all | solution.py:324
  55.0 2.7 reshape.290
  57.7 2.7 fusion.11
  61.4 2.8 collective-permute-start.12
  64.2 5.8 %collective-permute-start.13 = (bf16[128,1024]{1,0:T(8,128)(2,1)}, bf16[128,1024]{1,0:T(8,128)(2,1)}, u32[]{:S(2)}, u32[]{:S(2)}) collective-permute-start(bf16[128,1024]{1,0:T(8,128)(2,1)} %get-tuple-element.18), channel_id=1, source_target_pairs={{0,33},{1,65},{2,97},{3,1},{4,37},{5,69},{6,101},{7,5},{8,41},{9,7... | collective-permute-start | bytes 786440 | tf_op jit(solution)/shard_map/ppermute | solution.py:39
  70.0 2.6 collective-permute-start.14
  72.7 1.9 collective-permute-start.15
  75.3 6.3 %collective-permute-start.22 = (bf16[128,5120]{1,0:T(8,128)(2,1)}, bf16[128,5120]{1,0:T(8,128)(2,1)}, u32[]{:S(2)}, u32[]{:S(2)}) collective-permute-start(bf16[128,5120]{1,0:T(8,128)(2,1)} %bitcast.52), channel_id=1, source_target_pairs={{0,66},{1,98},{2,2},{3,34},{4,70},{5,102},{6,6},{7,38},{8,74},{9,1... | collective-permute-start | bytes 3932168 | tf_op jit(solution)/shard_map/ppermute | solution.py:39
  83.7 5.0 %collective-permute-done.15 = bf16[128,1024]{1,0:T(8,128)(2,1)} collective-permute-done((bf16[128,1024]{1,0:T(8,128)(2,1)}, bf16[128,1024]{1,0:T(8,128)(2,1)}, u32[]{:S(2)}, u32[]{:S(2)}) %collective-permute-start.15) | collective-permute-done | bytes 262176 | tf_op jit(solution)/shard_map/ppermute | solution.py:39
  88.7 2.3 pad_maximum_fusion.2.dout_ref
  91.0 14.0 %attention_totals.1.total_ref = f32[4,1,1024]{2,1,0:T(1,128)S(1)} custom-call(s32[3]{0:T(128)S(1)} %pad_add_fusion.where_ref, bf16[4,128,1024]{2,1,0:T(8,128)(2,1)S(1)} %pad_maximum_fusion.1.queries_ref, bf16[8,4,128,128]{3,2,1,0:T(8,128)(2,1)S(1)} %all-to-all-done.keys_ref), custom_call_target="tpu_custom_call" | custom-call | flops 2147483648 | bytes 2097152 | tf_op jit(solution)/shard_map/attention_totals/pallas_call | solution.py:202
  106.3 13.1 %attention_values.1 = bf16[8,4,128,128]{3,2,1,0:T(8,128)(2,1)S(1)} custom-call(s32[3]{0:T(128)S(1)} %pad_add_fusion.where_ref, bf16[4,128,1024]{2,1,0:T(8,128)(2,1)S(1)} %copy-done.2, bf16[8,4,128,128]{3,2,1,0:T(8,128)(2,1)S(1)} %all-to-all-done.keys_ref, bf16[4,128,1024]{2,1,0:T(8,128)(2,1)S(1)} %copy-done.3, f32[4,1,1024]{2,1,0:T(1,128)S(1)} %attention_totals.1.total_ref), custom_call_target="tpu_custom_call" | custom-call | flops 4294967296 | bytes 4194304 | tf_op jit(solution)/shard_map/attention_values/pallas_call | solution.py:220
  119.5 7.5 %collective-permute-start.17 = (bf16[2,4,128,128]{3,2,1,0:T(8,128)(2,1)S(1)}, bf16[2,4,128,128]{3,2,1,0:T(8,128)(2,1)}, u32[]{:S(2)}, u32[]{:S(2)}) collective-permute-start(bf16[2,4,128,128]{3,2,1,0:T(8,128)(2,1)S(1)} %get-tuple-element.14), channel_id=1, source_target_pairs={{0,16},{1,17},{2,18},{3,19},{4,20},{5,21},{6,22},{7,23},{8,24},{9,... | collective-permute-start | bytes 786440 | tf_op jit(solution)/shard_map/ppermute | solution.py:39
  128.2 2.1 collective-permute-start.21
  130.4 3.4 collective-permute-start.23
  133.7 3.6 collective-permute-done.17
  138.7 2.5 collective-permute-start.19
  141.3 4.7 %collective-permute-start.20 = (bf16[128,5120]{1,0:T(8,128)(2,1)}, bf16[128,5120]{1,0:T(8,128)(2,1)}, u32[]{:S(2)}, u32[]{:S(2)}) collective-permute-start(bf16[128,5120]{1,0:T(8,128)(2,1)} %bitcast.52), channel_id=1, source_target_pairs={{0,0},{1,32},{2,64},{3,96},{4,4},{5,36},{6,68},{7,100},{8,8},{9,40... | collective-permute-start | bytes 3932168 | tf_op jit(solution)/shard_map/ppermute | solution.py:39
  146.1 18.0 %collective-permute-done.19 = f32[4,128,128]{2,1,0:T(8,128)S(1)} collective-permute-done((f32[4,128,128]{2,1,0:T(8,128)S(1)}, f32[4,128,128]{2,1,0:T(8,128)S(1)}, u32[]{:S(2)}, u32[]{:S(2)}) %collective-permute-start.19) | collective-permute-done | bytes 262176 | tf_op jit(solution)/shard_map/ppermute | solution.py:39
  167.8 1.9 fusion.59
  169.7 44.1 %collective-permute-done.20 = bf16[128,5120]{1,0:T(8,128)(2,1)} collective-permute-done((bf16[128,5120]{1,0:T(8,128)(2,1)}, bf16[128,5120]{1,0:T(8,128)(2,1)}, u32[]{:S(2)}, u32[]{:S(2)}) %collective-permute-start.20) | collective-permute-done | bytes 1310752 | tf_op jit(solution)/shard_map/ppermute | solution.py:39
  213.8 2.0 fusion.3
  217.3 56.9 %all-to-all-start.1 = ((bf16[32,160,128]{2,1,0:T(8,128)(2,1)}), bf16[32,160,128]{2,1,0:T(8,128)(2,1)S(1)}, u32[]{:S(2)}, u32[]{:S(2)}) async-start(bf16[32,160,128]{2,1,0:T(8,128)(2,1)} %bitcast.243), calls=%async_computation.1 | async-start | bytes 2621440 | tf_op jit(solution)/shard_map/all_to_all | solution.py:383
  274.9 2.0 collective-permute-start.2
  277.0 1.9 select_reduce_fusion
  278.9 5.6 %collective-permute-done.1 = f32[3,40,128]{2,1,0:T(8,128)S(1)} collective-permute-done((f32[3,40,128]{2,1,0:T(8,128)S(1)}, f32[3,40,128]{2,1,0:T(8,128)S(1)}, u32[]{:S(2)}, u32[]{:S(2)}) %collective-permute-start.1) | collective-permute-done | bytes 61472 | tf_op jit(solution)/shard_map/ppermute | solution.py:39
  285.2 4.0 %all-to-all-done.1 = bf16[32,160,128]{2,1,0:T(8,128)(2,1)S(1)} async-done(((bf16[32,160,128]{2,1,0:T(8,128)(2,1)}), bf16[32,160,128]{2,1,0:T(8,128)(2,1)S(1)}, u32[]{:S(2)}, u32[]{:S(2)}) %all-to-all-start.1) | async-done | bytes 1310752 | tf_op jit(solution)/shard_map/all_to_all | solution.py:383
  291.4 5.2 %all-to-all-start.2 = ((bf16[32,160,128]{2,1,0:T(8,128)(2,1)}), bf16[32,160,128]{2,1,0:T(8,128)(2,1)S(1)}, u32[]{:S(2)}, u32[]{:S(2)}) async-start(bf16[32,160,128]{2,1,0:T(8,128)(2,1)} %broadcast_in_dim.83), calls=%async_computation.2 | async-start | bytes 2621440 | tf_op jit(solution)/shard_map/all_to_all | solution.py:398
  296.8 3.8 %fusion.8 = (f32[4,32,8]{2,0,1:T(4,128)S(1)}, f32[32,512,4,8]{1,3,2,0:T(8,128)S(1)}) fusion(pred[32,512]{1,0:T(8,128)(4,1)S(1)} %iota_compare_fusion, bf16[32,512,128]{2,1,0:T(8,128)(2,1)} %param.36, bf16[4,32,8,128]{3,2,1,0:T(8,128)(2,1)S(1)} %bitcast.247), kind=kOutput, calls=%fused_computation.12 | convolution fusion | flops 135789568 | bytes 6574080 | tf_op jit(solution)/shard_map/srgd,rcd->srgc/dot_general | solution.py:243
  303.1 13.0 %all-to-all-done.2 = bf16[32,160,128]{2,1,0:T(8,128)(2,1)S(1)} async-done(((bf16[32,160,128]{2,1,0:T(8,128)(2,1)}), bf16[32,160,128]{2,1,0:T(8,128)(2,1)S(1)}, u32[]{:S(2)}, u32[]{:S(2)}) %all-to-all-start.2) | async-done | bytes 1310752 | tf_op jit(solution)/shard_map/all_to_all | solution.py:398
  317.6 3.7 %fusion.28 = bf16[4,32,8,128]{3,2,0,1:T(8,128)(2,1)S(1)} fusion(bf16[32,512,128]{2,1,0:T(8,128)(2,1)} %param.37, f32[32,512,4,8]{1,3,2,0:T(8,128)S(1)} %copy-done.6, f32[4,32,8]{2,0,1:T(4,128)S(1)} %add.349, f32[4,32,8]{2,0,1:T(4,128)S(1)} %max.7, pred[32,512]{1,0:T(8,128)(4,1)S(1)} %iota_compare_fusion, f32[32,128]{1,0:T(8,128)S(1)} %get-tuple-element.54, ...), kind=kOutput, calls=%fused_computation.27 | convolution fusion | flops 138018816 | bytes 6660096 | tf_op jit(solution)/shard_map/srgc,rcd->srgd/dot_general | solution.py:264
  326.3 3.1 collective-permute-start.27
  329.5 3.0 collective-permute-done.27
  332.5 2.7 fusion.41
  338.3 14.3 %collective-permute-done.25 = f32[3,40,128]{2,1,0:T(8,128)} collective-permute-done((f32[3,40,128]{2,1,0:T(8,128)S(1)}, f32[3,40,128]{2,1,0:T(8,128)}, u32[]{:S(2)}, u32[]{:S(2)}) %collective-permute-start.25) | collective-permute-done | bytes 61472 | tf_op jit(solution)/shard_map/ppermute | solution.py:39
  352.6 1.9 collective-permute-done.26
  355.4 1.9 add_convert_fusion
  (162 shorter events, 43.8 us)
Async XLA Ops:
  0.6 315.4 %copy-start = (bf16[4,32,5120]{2,1,0:T(8,128)(2,1)S(1)}, bf16[4,32,5120]{2,1,0:T(8,128)(2,1)}, u32[]{:S(2)}) copy-start(bf16[4,32,5120]{2,1,0:T(8,128)(2,1)} %param.33) | copy-start | bytes 3932164
  2.0 28.9 %collective-permute-start.8 = (bf16[128,128]{1,0:T(8,128)(2,1)S(1)}, bf16[128,128]{1,0:T(8,128)(2,1)}, u32[]{:S(2)}, u32[]{:S(2)}) collective-permute-start(bf16[128,128]{1,0:T(8,128)(2,1)S(1)} %bitcast.274), channel_id=1, source_target_pairs={{0,0},{1,32},{2,64},{3,96},{4,4},{5,36},{6,68},{7,100},{8,8},{9,40... | collective-permute-start | bytes 98312 | tf_op jit(solution)/shard_map/ppermute | solution.py:39
  6.7 26.3 %collective-permute-start.9 = (bf16[128,128]{1,0:T(8,128)(2,1)S(1)}, bf16[128,128]{1,0:T(8,128)(2,1)}, u32[]{:S(2)}, u32[]{:S(2)}) collective-permute-start(bf16[128,128]{1,0:T(8,128)(2,1)S(1)} %bitcast.273), channel_id=1, source_target_pairs={{0,33},{1,65},{2,97},{3,1},{4,37},{5,69},{6,101},{7,5},{8,41},{9,7... | collective-permute-start | bytes 98312 | tf_op jit(solution)/shard_map/ppermute | solution.py:39
  12.1 29.4 %collective-permute-start.10 = (bf16[128,128]{1,0:T(8,128)(2,1)S(1)}, bf16[128,128]{1,0:T(8,128)(2,1)}, u32[]{:S(2)}, u32[]{:S(2)}) collective-permute-start(bf16[128,128]{1,0:T(8,128)(2,1)S(1)} %bitcast.272), channel_id=1, source_target_pairs={{0,66},{1,98},{2,2},{3,34},{4,70},{5,102},{6,6},{7,38},{8,74},{9,1... | collective-permute-start | bytes 98312 | tf_op jit(solution)/shard_map/ppermute | solution.py:39
  15.3 28.2 %collective-permute-start.11 = (bf16[128,128]{1,0:T(8,128)(2,1)S(1)}, bf16[128,128]{1,0:T(8,128)(2,1)}, u32[]{:S(2)}, u32[]{:S(2)}) collective-permute-start(bf16[128,128]{1,0:T(8,128)(2,1)S(1)} %bitcast.271), channel_id=1, source_target_pairs={{0,99},{1,3},{2,35},{3,67},{4,103},{5,7},{6,39},{7,71},{8,107},{9,... | collective-permute-start | bytes 98312 | tf_op jit(solution)/shard_map/ppermute | solution.py:39
  17.4 44.0 %collective-permute-start.3 = (s32[1,2]{1,0:T(1,128)}, s32[1,2]{1,0:T(1,128)}, u32[]{:S(2)}, u32[]{:S(2)}) collective-permute-start(s32[1,2]{1,0:T(1,128)} %param.27), channel_id=1, source_target_pairs={{0,0},{1,32},{2,64},{3,96},{4,4},{5,36},{6,68},{7,100},{8,8},{9,40... | collective-permute-start | bytes 32 | tf_op jit(solution)/shard_map/ppermute | solution.py:39
  30.1 24.8 %copy-start.18 = (f32[1,128]{1,0:T(1,128)S(1)}, f32[1,128]{1,0:T(1,128)}, u32[]{:S(2)}) copy-start(f32[1,128]{1,0:T(1,128)} %param.26) | copy-start | bytes 1540
  30.1 24.8 %copy-start.19 = (f32[1,128]{1,0:T(1,128)S(1)}, f32[1,128]{1,0:T(1,128)}, u32[]{:S(2)}) copy-start(f32[1,128]{1,0:T(1,128)} %param.24) | copy-start | bytes 1540
  30.1 24.8 %copy-start.20 = (f32[1,128]{1,0:T(1,128)S(1)}, f32[1,128]{1,0:T(1,128)}, u32[]{:S(2)}) copy-start(f32[1,128]{1,0:T(1,128)} %param.25) | copy-start | bytes 1540
  30.9 24.0 %copy-start.7 = (bf16[1,128,4096]{2,1,0:T(8,128)(2,1)S(1)}, bf16[1,128,4096]{2,1,0:T(8,128)(2,1)}, u32[]{:S(2)}) copy-start(bf16[1,128,4096]{2,1,0:T(8,128)(2,1)} %param.23) | copy-start | bytes 3145732
  30.9 33.3 %collective-permute-start.4 = (bf16[128,1024]{1,0:T(8,128)(2,1)}, bf16[128,1024]{1,0:T(8,128)(2,1)}, u32[]{:S(2)}, u32[]{:S(2)}) collective-permute-start(bf16[128,1024]{1,0:T(8,128)(2,1)} %bitcast.227), channel_id=1, source_target_pairs={{0,0},{1,32},{2,64},{3,96},{4,4},{5,36},{6,68},{7,100},{8,8},{9,40... | collective-permute-start | bytes 786440 | tf_op jit(solution)/shard_map/ppermute | solution.py:39
  33.0 37.0 %collective-permute-start.5 = (bf16[128,1024]{1,0:T(8,128)(2,1)}, bf16[128,1024]{1,0:T(8,128)(2,1)}, u32[]{:S(2)}, u32[]{:S(2)}) collective-permute-start(bf16[128,1024]{1,0:T(8,128)(2,1)} %bitcast.226), channel_id=1, source_target_pairs={{0,33},{1,65},{2,97},{3,1},{4,37},{5,69},{6,101},{7,5},{8,41},{9,7... | collective-permute-start | bytes 786440 | tf_op jit(solution)/shard_map/ppermute | solution.py:39
  41.5 31.1 %collective-permute-start.6 = (bf16[128,1024]{1,0:T(8,128)(2,1)}, bf16[128,1024]{1,0:T(8,128)(2,1)}, u32[]{:S(2)}, u32[]{:S(2)}) collective-permute-start(bf16[128,1024]{1,0:T(8,128)(2,1)} %bitcast.225), channel_id=1, source_target_pairs={{0,66},{1,98},{2,2},{3,34},{4,70},{5,102},{6,6},{7,38},{8,74},{9,1... | collective-permute-start | bytes 786440 | tf_op jit(solution)/shard_map/ppermute | solution.py:39
  43.5 31.9 %collective-permute-start.7 = (bf16[128,1024]{1,0:T(8,128)(2,1)}, bf16[128,1024]{1,0:T(8,128)(2,1)}, u32[]{:S(2)}, u32[]{:S(2)}) collective-permute-start(bf16[128,1024]{1,0:T(8,128)(2,1)} %bitcast.224), channel_id=1, source_target_pairs={{0,99},{1,3},{2,35},{3,67},{4,103},{5,7},{6,39},{7,71},{8,107},{9,... | collective-permute-start | bytes 786440 | tf_op jit(solution)/shard_map/ppermute | solution.py:39
  47.4 43.6 %all-to-all-start = ((bf16[8,4,128,128]{3,2,1,0:T(8,128)(2,1)}), bf16[8,4,128,128]{3,2,1,0:T(8,128)(2,1)S(1)}, u32[]{:S(2)}, u32[]{:S(2)}) async-start(bf16[8,4,128,128]{3,2,1,0:T(8,128)(2,1)} %broadcast_in_dim.79), calls=%async_computation | async-start | bytes 2097152 | tf_op jit(solution)/shard_map/all_to_all | solution.py:324
  61.4 21.6 %collective-permute-start.12 = (bf16[128,1024]{1,0:T(8,128)(2,1)}, bf16[128,1024]{1,0:T(8,128)(2,1)}, u32[]{:S(2)}, u32[]{:S(2)}) collective-permute-start(bf16[128,1024]{1,0:T(8,128)(2,1)} %get-tuple-element.15), channel_id=1, source_target_pairs={{0,0},{1,32},{2,64},{3,96},{4,4},{5,36},{6,68},{7,100},{8,8},{9,40... | collective-permute-start | bytes 786440 | tf_op jit(solution)/shard_map/ppermute | solution.py:39
  64.2 18.8 %collective-permute-start.13 = (bf16[128,1024]{1,0:T(8,128)(2,1)}, bf16[128,1024]{1,0:T(8,128)(2,1)}, u32[]{:S(2)}, u32[]{:S(2)}) collective-permute-start(bf16[128,1024]{1,0:T(8,128)(2,1)} %get-tuple-element.18), channel_id=1, source_target_pairs={{0,33},{1,65},{2,97},{3,1},{4,37},{5,69},{6,101},{7,5},{8,41},{9,7... | collective-permute-start | bytes 786440 | tf_op jit(solution)/shard_map/ppermute | solution.py:39
  70.0 13.7 %collective-permute-start.14 = (bf16[128,1024]{1,0:T(8,128)(2,1)}, bf16[128,1024]{1,0:T(8,128)(2,1)}, u32[]{:S(2)}, u32[]{:S(2)}) collective-permute-start(bf16[128,1024]{1,0:T(8,128)(2,1)} %get-tuple-element.17), channel_id=1, source_target_pairs={{0,66},{1,98},{2,2},{3,34},{4,70},{5,102},{6,6},{7,38},{8,74},{9,1... | collective-permute-start | bytes 786440 | tf_op jit(solution)/shard_map/ppermute | solution.py:39
  72.7 16.1 %collective-permute-start.15 = (bf16[128,1024]{1,0:T(8,128)(2,1)}, bf16[128,1024]{1,0:T(8,128)(2,1)}, u32[]{:S(2)}, u32[]{:S(2)}) collective-permute-start(bf16[128,1024]{1,0:T(8,128)(2,1)} %get-tuple-element.16), channel_id=1, source_target_pairs={{0,99},{1,3},{2,35},{3,67},{4,103},{5,7},{6,39},{7,71},{8,107},{9,... | collective-permute-start | bytes 786440 | tf_op jit(solution)/shard_map/ppermute | solution.py:39
  75.3 88.8 %collective-permute-start.22 = (bf16[128,5120]{1,0:T(8,128)(2,1)}, bf16[128,5120]{1,0:T(8,128)(2,1)}, u32[]{:S(2)}, u32[]{:S(2)}) collective-permute-start(bf16[128,5120]{1,0:T(8,128)(2,1)} %bitcast.52), channel_id=1, source_target_pairs={{0,66},{1,98},{2,2},{3,34},{4,70},{5,102},{6,6},{7,38},{8,74},{9,1... | collective-permute-start | bytes 3932168 | tf_op jit(solution)/shard_map/ppermute | solution.py:39
  83.0 8.0 %copy-start.1 = (bf16[4,128,1024]{2,1,0:T(8,128)(2,1)}, bf16[4,128,1024]{2,1,0:T(8,128)(2,1)S(1)}, u32[]{:S(2)}) copy-start(bf16[4,128,1024]{2,1,0:T(8,128)(2,1)S(1)} %pad_maximum_fusion.1.queries_ref) | copy-start | bytes 3145732
  91.0 14.0 %copy-start.3 = (bf16[4,128,1024]{2,1,0:T(8,128)(2,1)S(1)}, bf16[4,128,1024]{2,1,0:T(8,128)(2,1)}, u32[]{:S(2)}) copy-start(bf16[4,128,1024]{2,1,0:T(8,128)(2,1)} %pad_maximum_fusion.2.dout_ref) | copy-start | bytes 3145732
  119.5 10.9 %collective-permute-start.16 = (bf16[2,4,128,128]{3,2,1,0:T(8,128)(2,1)S(1)}, bf16[2,4,128,128]{3,2,1,0:T(8,128)(2,1)S(1)}, u32[]{:S(2)}, u32[]{:S(2)}) collective-permute-start(bf16[2,4,128,128]{3,2,1,0:T(8,128)(2,1)S(1)} %get-tuple-element.12), channel_id=1, source_target_pairs={{0,8},{1,9},{2,10},{3,11},{4,12},{5,13},{6,14},{7,15},{8,16},{9,17... | collective-permute-start | bytes 786440 | tf_op jit(solution)/shard_map/ppermute | solution.py:39
  119.5 17.8 %collective-permute-start.17 = (bf16[2,4,128,128]{3,2,1,0:T(8,128)(2,1)S(1)}, bf16[2,4,128,128]{3,2,1,0:T(8,128)(2,1)}, u32[]{:S(2)}, u32[]{:S(2)}) collective-permute-start(bf16[2,4,128,128]{3,2,1,0:T(8,128)(2,1)S(1)} %get-tuple-element.14), channel_id=1, source_target_pairs={{0,16},{1,17},{2,18},{3,19},{4,20},{5,21},{6,22},{7,23},{8,24},{9,... | collective-permute-start | bytes 786440 | tf_op jit(solution)/shard_map/ppermute | solution.py:39
  127.0 10.5 %collective-permute-start.18 = (bf16[2,4,128,128]{3,2,1,0:T(8,128)(2,1)S(1)}, bf16[2,4,128,128]{3,2,1,0:T(8,128)(2,1)}, u32[]{:S(2)}, u32[]{:S(2)}) collective-permute-start(bf16[2,4,128,128]{3,2,1,0:T(8,128)(2,1)S(1)} %get-tuple-element.13), channel_id=1, source_target_pairs={{0,24},{1,25},{2,26},{3,27},{4,28},{5,29},{6,30},{7,31},{8,0},{9,1... | collective-permute-start | bytes 786440 | tf_op jit(solution)/shard_map/ppermute | solution.py:39
  128.2 37.7 %collective-permute-start.21 = (bf16[128,5120]{1,0:T(8,128)(2,1)}, bf16[128,5120]{1,0:T(8,128)(2,1)}, u32[]{:S(2)}, u32[]{:S(2)}) collective-permute-start(bf16[128,5120]{1,0:T(8,128)(2,1)} %bitcast.52), channel_id=1, source_target_pairs={{0,33},{1,65},{2,97},{3,1},{4,37},{5,69},{6,101},{7,5},{8,41},{9,7... | collective-permute-start | bytes 3932168 | tf_op jit(solution)/shard_map/ppermute | solution.py:39
  130.4 37.5 %collective-permute-start.23 = (bf16[128,5120]{1,0:T(8,128)(2,1)}, bf16[128,5120]{1,0:T(8,128)(2,1)}, u32[]{:S(2)}, u32[]{:S(2)}) collective-permute-start(bf16[128,5120]{1,0:T(8,128)(2,1)} %bitcast.52), channel_id=1, source_target_pairs={{0,99},{1,3},{2,35},{3,67},{4,103},{5,7},{6,39},{7,71},{8,107},{9,... | collective-permute-start | bytes 3932168 | tf_op jit(solution)/shard_map/ppermute | solution.py:39
  138.7 25.3 %collective-permute-start.19 = (f32[4,128,128]{2,1,0:T(8,128)S(1)}, f32[4,128,128]{2,1,0:T(8,128)S(1)}, u32[]{:S(2)}, u32[]{:S(2)}) collective-permute-start(f32[4,128,128]{2,1,0:T(8,128)S(1)} %dynamic-slice_bitcast_fusion), channel_id=1, source_target_pairs={{0,4},{1,5},{2,6},{3,7},{4,0},{5,1},{6,2},{7,3},{8,12},{9,13},{10,... | collective-permute-start | bytes 786440 | tf_op jit(solution)/shard_map/ppermute | solution.py:39
  141.3 72.5 %collective-permute-start.20 = (bf16[128,5120]{1,0:T(8,128)(2,1)}, bf16[128,5120]{1,0:T(8,128)(2,1)}, u32[]{:S(2)}, u32[]{:S(2)}) collective-permute-start(bf16[128,5120]{1,0:T(8,128)(2,1)} %bitcast.52), channel_id=1, source_target_pairs={{0,0},{1,32},{2,64},{3,96},{4,4},{5,36},{6,68},{7,100},{8,8},{9,40... | collective-permute-start | bytes 3932168 | tf_op jit(solution)/shard_map/ppermute | solution.py:39
  215.8 58.4 %copy-start.10 = (f32[40,512]{1,0:T(8,128)S(1)}, f32[40,512]{1,0:T(8,128)}, u32[]{:S(2)}) copy-start(f32[40,512]{1,0:T(8,128)} %param.30) | copy-start | bytes 245764
  215.9 58.4 %copy-start.11 = (f32[40,512]{1,0:T(8,128)S(1)}, f32[40,512]{1,0:T(8,128)}, u32[]{:S(2)}) copy-start(f32[40,512]{1,0:T(8,128)} %param.31) | copy-start | bytes 245764
  217.3 57.0 %copy-start.12 = (f32[40,512]{1,0:T(8,128)S(1)}, f32[40,512]{1,0:T(8,128)}, u32[]{:S(2)}) copy-start(f32[40,512]{1,0:T(8,128)} %param.32) | copy-start | bytes 245764
  217.3 59.6 %copy-start.9 = (bf16[4,32,1024]{2,1,0:T(8,128)(2,1)S(1)}, bf16[4,32,1024]{2,1,0:T(8,128)(2,1)}, u32[]{:S(2)}) copy-start(bf16[4,32,1024]{2,1,0:T(8,128)(2,1)} %param.34) | copy-start | bytes 786436
  217.3 59.7 %copy-start.22 = (bf16[4,32,128]{2,1,0:T(8,128)(2,1)S(1)}, bf16[4,32,128]{2,1,0:T(8,128)(2,1)}, u32[]{:S(2)}) copy-start(bf16[4,32,128]{2,1,0:T(8,128)(2,1)} %param.35) | copy-start | bytes 98308
  217.3 71.9 %all-to-all-start.1 = ((bf16[32,160,128]{2,1,0:T(8,128)(2,1)}), bf16[32,160,128]{2,1,0:T(8,128)(2,1)S(1)}, u32[]{:S(2)}, u32[]{:S(2)}) async-start(bf16[32,160,128]{2,1,0:T(8,128)(2,1)} %bitcast.243), calls=%async_computation.1 | async-start | bytes 2621440 | tf_op jit(solution)/shard_map/all_to_all | solution.py:383
  274.7 4.2 %collective-permute-start = (f32[3,40,128]{2,1,0:T(8,128)S(1)}, f32[3,40,128]{2,1,0:T(8,128)S(1)}, u32[]{:S(2)}, u32[]{:S(2)}) collective-permute-start(f32[3,40,128]{2,1,0:T(8,128)S(1)} %bitcast.269), channel_id=1, source_target_pairs={{0,1},{1,0},{2,3},{3,2},{4,5},{5,4},{6,7},{7,6},{8,9},{9,8},{10,11... | collective-permute-start | bytes 184328 | tf_op jit(solution)/shard_map/ppermute | solution.py:39
  274.8 9.7 %collective-permute-start.1 = (f32[3,40,128]{2,1,0:T(8,128)S(1)}, f32[3,40,128]{2,1,0:T(8,128)S(1)}, u32[]{:S(2)}, u32[]{:S(2)}) collective-permute-start(f32[3,40,128]{2,1,0:T(8,128)S(1)} %bitcast.267), channel_id=1, source_target_pairs={{0,2},{1,3},{2,0},{3,1},{4,6},{5,7},{6,4},{7,5},{8,10},{9,11},{10,... | collective-permute-start | bytes 184328 | tf_op jit(solution)/shard_map/ppermute | solution.py:39
  274.9 10.3 %collective-permute-start.2 = (f32[3,40,128]{2,1,0:T(8,128)S(1)}, f32[3,40,128]{2,1,0:T(8,128)S(1)}, u32[]{:S(2)}, u32[]{:S(2)}) collective-permute-start(f32[3,40,128]{2,1,0:T(8,128)S(1)} %bitcast.264), channel_id=1, source_target_pairs={{0,3},{1,2},{2,1},{3,0},{4,7},{5,6},{6,5},{7,4},{8,11},{9,10},{10,... | collective-permute-start | bytes 184328 | tf_op jit(solution)/shard_map/ppermute | solution.py:39
  277.0 8.2 %copy-start.14 = (pred[4,4]{1,0:T(4,128)(4,1)}, pred[4,4]{1,0:T(4,128)(4,1)S(1)}, u32[]{:S(2)}) copy-start(pred[4,4]{1,0:T(4,128)(4,1)S(1)} %iota_compare_fusion.1) | copy-start | bytes 52
  290.1 6.6 %copy-start.21 = (s32[32]{0:T(128)S(1)}, s32[32]{0:T(128)}, u32[]{:S(2)}) copy-start(s32[32]{0:T(128)} %param.38) | copy-start | bytes 388
  291.4 24.6 %all-to-all-start.2 = ((bf16[32,160,128]{2,1,0:T(8,128)(2,1)}), bf16[32,160,128]{2,1,0:T(8,128)(2,1)S(1)}, u32[]{:S(2)}, u32[]{:S(2)}) async-start(bf16[32,160,128]{2,1,0:T(8,128)(2,1)} %broadcast_in_dim.83), calls=%async_computation.2 | async-start | bytes 2621440 | tf_op jit(solution)/shard_map/all_to_all | solution.py:398
  326.3 9.0 %copy-start.8 = (f32[1,4,40,128]{3,2,1,0:T(8,128)S(1)}, f32[1,4,40,128]{3,2,1,0:T(8,128)}, u32[]{:S(2)}) copy-start(f32[1,4,40,128]{3,2,1,0:T(8,128)} %get-tuple-element.9) | copy-start | bytes 245764
  326.3 6.1 %collective-permute-start.27 = (f32[128,2560]{1,0:T(8,128)}, f32[128,2560]{1,0:T(8,128)}, u32[]{:S(2)}, u32[]{:S(2)}) collective-permute-start(f32[128,2560]{1,0:T(8,128)} %constant_dynamic-slice_fusion), channel_id=1, source_target_pairs={{0,1},{1,0},{2,3},{3,2},{4,5},{5,4},{6,7},{7,6},{8,9},{9,8},{10,11... | collective-permute-start | bytes 3932168 | tf_op jit(solution)/shard_map/ppermute | solution.py:39
  335.1 20.3 %collective-permute-start.28 = (bf16[128,2560]{1,0:T(8,128)(2,1)}, bf16[128,2560]{1,0:T(8,128)(2,1)S(1)}, u32[]{:S(2)}, u32[]{:S(2)}) collective-permute-start(bf16[128,2560]{1,0:T(8,128)(2,1)} %fusion.41), channel_id=1, source_target_pairs={{0,2},{1,3},{2,0},{3,1},{4,6},{5,7},{6,4},{7,5},{8,10},{9,11},{10,... | collective-permute-start | bytes 1966088 | tf_op jit(solution)/shard_map/ppermute | solution.py:39
  336.0 2.3 collective-permute-start.24
  336.6 16.0 %collective-permute-start.25 = (f32[3,40,128]{2,1,0:T(8,128)S(1)}, f32[3,40,128]{2,1,0:T(8,128)}, u32[]{:S(2)}, u32[]{:S(2)}) collective-permute-start(f32[3,40,128]{2,1,0:T(8,128)S(1)} %get-tuple-element.35), channel_id=1, source_target_pairs={{0,2},{1,3},{2,0},{3,1},{4,6},{5,7},{6,4},{7,5},{8,10},{9,11},{10,... | collective-permute-start | bytes 184328 | tf_op jit(solution)/shard_map/ppermute | solution.py:39
  337.9 16.6 %collective-permute-start.26 = (f32[3,40,128]{2,1,0:T(8,128)S(1)}, f32[3,40,128]{2,1,0:T(8,128)}, u32[]{:S(2)}, u32[]{:S(2)}) collective-permute-start(f32[3,40,128]{2,1,0:T(8,128)S(1)} %get-tuple-element.34), channel_id=1, source_target_pairs={{0,3},{1,2},{2,1},{3,0},{4,7},{5,6},{6,5},{7,4},{8,11},{9,10},{10,... | collective-permute-start | bytes 184328 | tf_op jit(solution)/shard_map/ppermute | solution.py:39
  357.3 2.2 collective-permute-start.29
  (12 other events, 37.4 us)

commit v2 on v0

v2 whole, which is shorter than its diff:
```python
import math

import jax
import jax.numpy as jnp
from jax import lax
from jax.experimental import pallas as pl
from jax.experimental.pallas import tpu as pltpu
from jax.sharding import PartitionSpec as P

HD = 128
HEADS = 32
KV = 4
GROUP = HEADS // KV
BLOCK = 128
NX, NZ, NY, NT = 4, 4, 2, 4
NG = NZ * NY
SLAB = NX * NG * BLOCK
CHUNK = 512
ROWS = GROUP * BLOCK
LOWEST = -1e30

first_decay = 0.9
second_decay = 0.95
adam_eps = 1e-08
learn_rate = 0.001
decay_weight = 0.1
kl_weight = 0.1
exp2_scale = HD ** (-0.5) * math.log2(math.e)


def route(value, target):
    pairs = []
    for source in range(NX * NG * NT):
        ctx, t = divmod(source, NT)
        x, g = divmod(ctx, NG)
        z, y = divmod(g, NY)
        nx, nz, ny, nt = target(x, z, y, t)
        pairs.append((source, (((nx % NX) * NZ + nz % NZ) * NY + ny % NY) * NT + nt % NT))
    return lax.ppermute(value, ("ctx", "tp"), pairs)


def together(*values):
    return lax.optimization_barrier(values)


def pick(value, index, axis=0):
    return lax.dynamic_index_in_dim(value, index, axis, keepdims=False)


def segment_ids(lengths_row, position):
    doc_ends = jnp.cumsum(lengths_row)
    return jnp.sum((position[:, None] >= doc_ends[None, :]).astype(jnp.int32), axis=1)


def group_advantage(rewards, groups):
    flat_reward = rewards.reshape(-1)
    flat_group = groups.reshape(-1)
    same_group = (flat_group[:, None] == flat_group[None, :]).astype(jnp.float32)
    group_mean = jnp.sum(same_group * flat_reward[None, :], axis=1) / jnp.sum(same_group, axis=1)
    return (flat_reward - group_mean).reshape(rewards.shape)


def token_coef(own_advantage, segment, policy_logp, sample_logp, frozen_logp, divisor):
    labels = jnp.arange(own_advantage.shape[0], dtype=jnp.int32)
    picked = jnp.sum(
        jnp.where(segment[:, None] == labels[None, :], own_advantage[None, :], 0.0), axis=1
    )
    return (
        -jnp.exp(policy_logp - sample_logp) * picked
        + kl_weight * (1.0 - jnp.exp(frozen_logp - policy_logp))
    ) / divisor


def in_smem():
    return pl.BlockSpec(memory_space=pltpu.SMEM)


def in_vmem():
    return pl.BlockSpec(memory_space=pltpu.VMEM)


def attention_kernel(where_ref, *refs):
    block_refs, refs = refs[:NX], refs[NX:]
    keys_ref, out_ref, query_rows, dout_rows, scores, sums = refs
    g, bound, own = where_ref[0], where_ref[1], where_ref[2]
    for slot in range(NX):
        for h in range(GROUP):
            rows = pl.ds(h * BLOCK, BLOCK)
            query_rows[slot, rows, :] = block_refs[slot][:, pl.ds(h * HD, HD)]
            dout_rows[slot, rows, :] = block_refs[slot][:, pl.ds((GROUP + h) * HD, HD)]
    sums[...] = jnp.zeros_like(sums)

    def one_block(slot, _):
        block_start = (lax.rem(own - slot + NX, NX) * NG + g) * BLOCK
        latest_from = jnp.where(block_start + BLOCK - 1 >= bound, bound, 0)
        first = jnp.where(block_start >= bound, bound, 0) // CHUNK
        stop = (block_start + BLOCK - 1) // CHUNK + 1
        block_queries, block_douts = query_rows[slot], dout_rows[slot]

        def scored(chunk, row_max):
            start = pl.multiple_of(chunk * CHUNK, CHUNK)
            rows = pl.ds(start, CHUNK)
            scores[rows, :] = lax.dot_general(
                keys_ref[rows, :],
                block_queries,
                (((1,), (1,)), ((), ())),
                preferred_element_type=jnp.float32,
            )
            whole = (start + CHUNK - 1 <= block_start) & (start >= latest_from)

            @pl.when(jnp.logical_not(whole))
            def _():
                key_at = start + lax.broadcasted_iota(jnp.int32, (CHUNK, ROWS), 0)
                query_at = block_start + (
                    lax.broadcasted_iota(jnp.int32, (1, ROWS), 1) & (BLOCK - 1)
                )
                from_at = jnp.where(query_at >= bound, bound, 0)
                visible = (key_at <= query_at) & (key_at >= from_at)
                scores[rows, :] = jnp.where(visible, scores[rows, :], LOWEST)

            by_tile = scores[rows, :].reshape(CHUNK // 8, 8, ROWS)
            return jnp.maximum(row_max, jnp.max(by_tile, axis=0))

        row_max = lax.fori_loop(first, stop, scored, jnp.full((8, ROWS), LOWEST, jnp.float32))
        row_max = jnp.max(row_max, axis=0, keepdims=True) * exp2_scale

        def summed(chunk, row_sum):
            rows = pl.ds(pl.multiple_of(chunk * CHUNK, CHUNK), CHUNK)
            powers = jnp.exp2(scores[rows, :] * exp2_scale - row_max)
            scores[rows, :] = powers
            return row_sum + jnp.sum(powers.reshape(CHUNK // 8, 8, ROWS), axis=0)

        row_sum = lax.fori_loop(first, stop, summed, jnp.zeros((8, ROWS), jnp.float32))
        inverse = 1.0 / jnp.sum(row_sum, axis=0, keepdims=True)

        def added(chunk, _):
            rows = pl.ds(pl.multiple_of(chunk * CHUNK, CHUNK), CHUNK)
            sums[rows, :] += jnp.dot(
                (scores[rows, :] * inverse).astype(jnp.bfloat16),
                block_douts,
                preferred_element_type=jnp.float32,
            )
            return 0

        return lax.fori_loop(first, stop, added, 0)

    lax.fori_loop(0, NX, one_block, 0)
    for x in range(NX):
        for g_to in range(NG):
            out_ref[g_to, x] = sums[pl.ds((x * NG + g_to) * BLOCK, BLOCK), :].astype(out_ref.dtype)


def attention_terms(where, blocks, keys):
    return pl.pallas_call(
        attention_kernel,
        out_shape=jax.ShapeDtypeStruct((NG, NX, BLOCK, HD), jnp.bfloat16),
        in_specs=[in_smem()] + [in_vmem()] * (NX + 1),
        out_specs=in_vmem(),
        scratch_shapes=[
            pltpu.VMEM((NX, ROWS, HD), jnp.bfloat16),
            pltpu.VMEM((NX, ROWS, HD), jnp.bfloat16),
            pltpu.VMEM((SLAB, ROWS), jnp.float32),
            pltpu.VMEM((SLAB, HD), jnp.float32),
        ],
        compiler_params=pltpu.CompilerParams(vmem_limit_bytes=48 * 1024 * 1024),
        cost_estimate=pl.CostEstimate(
            flops=4 * SLAB * SLAB * HD, bytes_accessed=6 << 20, transcendentals=SLAB * SLAB // 2
        ),
        name="attention_terms",
    )(where, *blocks, keys)


def gradient_kernel(where_ref, dvalue_ref, h0_ref, h1_ref, h2_ref, h3_ref, out_ref):
    t = where_ref[3]
    hidden = jnp.concatenate([h0_ref[...], h1_ref[...], h2_ref[...], h3_ref[...]], axis=0)
    matching = jnp.concatenate([dvalue_ref[t ^ d].T for d in range(NX)], axis=1)
    by_column = jnp.dot(matching, hidden, preferred_element_type=jnp.float32)
    out_ref[...] = by_column.T.astype(out_ref.dtype)


def gradient_terms(where, dvalue, hidden_parts):
    width, tile = hidden_parts[0].shape[1], 1280
    columns = pl.BlockSpec((BLOCK, tile), lambda i: (0, i))
    return pl.pallas_call(
        gradient_kernel,
        grid=(width // tile,),
        out_shape=jax.ShapeDtypeStruct((width, HD), jnp.bfloat16),
        in_specs=[
            in_smem(),
            pl.BlockSpec((NX, BLOCK, HD), lambda i: (0, 0, 0)),
        ]
        + [columns] * NX,
        out_specs=pl.BlockSpec((tile, HD), lambda i: (i, 0)),
        cost_estimate=pl.CostEstimate(
            flops=2 * NX * BLOCK * width * HD, bytes_accessed=7 << 20, transcendentals=0
        ),
        name="gradient_terms",
    )(where, dvalue, *hidden_parts)


def decode_weights(dec_query, dec_key, cache_keys, cache_len):
    step_count, row_total = dec_query.shape[:2]
    cache_rows = cache_keys.shape[1]
    score_scale = HD ** (-0.5)
    query_heads = dec_query.reshape(step_count, row_total, GROUP, HD)
    old_scores = (
        jnp.einsum("srgd,rcd->srgc", query_heads, cache_keys, preferred_element_type=jnp.float32)
        * score_scale
    )
    new_scores = (
        jnp.einsum("srgd,jrd->srgj", query_heads, dec_key, preferred_element_type=jnp.float32)
        * score_scale
    )
    old_visible = (jnp.arange(cache_rows, dtype=jnp.int32)[None, :] < cache_len[:, None])[
        None, :, None, :
    ]
    step_ids = jnp.arange(step_count, dtype=jnp.int32)
    new_visible = (step_ids[None, :] <= step_ids[:, None])[:, None, None, :]
    row_max = jnp.maximum(
        jnp.max(jnp.where(old_visible, old_scores, -jnp.inf), axis=3),
        jnp.max(jnp.where(new_visible, new_scores, -jnp.inf), axis=3),
    )[..., None]
    old_exp = jnp.where(old_visible, jnp.exp(old_scores - row_max), 0.0)
    new_exp = jnp.where(new_visible, jnp.exp(new_scores - row_max), 0.0)
    denom = jnp.sum(old_exp, axis=3, keepdims=True) + jnp.sum(new_exp, axis=3, keepdims=True)
    old_weights = (old_exp / denom).astype(jnp.bfloat16)
    new_weights = (new_exp / denom).astype(jnp.bfloat16)
    return old_weights, new_weights


def decode_kernel(where_ref, hidden_ref, rollout_ref, cached_ref, weights_ref, out_weight_ref, out_ref, attended_ref):
    steps = weights_ref.shape[1] // GROUP
    rows = hidden_ref.shape[0] // steps

    @pl.when(pl.program_id(0) == 0)
    def _():
        fresh = jnp.dot(hidden_ref[...], rollout_ref[...], preferred_element_type=jnp.float32)
        fresh = fresh.astype(jnp.bfloat16).astype(jnp.float32)
        repeated = [
            jnp.concatenate([fresh[j * rows : (j + 1) * rows]] * steps, axis=0)
            for j in range(steps)
        ]
        for h in range(GROUP):
            columns = pl.ds(h * HD, HD)
            total = cached_ref[:, columns]
            for j in range(steps):
                at = h * steps + j
                total = total + weights_ref[:, at : at + 1] * repeated[j]
            attended_ref[:, columns] = total.astype(attended_ref.dtype)

    out_ref[...] = jnp.dot(
        attended_ref[...], out_weight_ref[...], preferred_element_type=jnp.float32
    )


def decode_outputs(where, dec_hidden, rollout, cached, weights, out_weight):
    rows, width = dec_hidden.shape
    tile = 640
    half_tiles = out_weight.shape[1] // tile // 2

    def whole(*shape):
        return pl.BlockSpec(shape, lambda i, where: (0, 0))

    return pl.pallas_call(
        decode_kernel,
        grid_spec=pltpu.PrefetchScalarGridSpec(
            num_scalar_prefetch=1,
            grid=(half_tiles,),
            in_specs=[
                whole(rows, width),
                whole(width, HD),
                whole(rows, GROUP * HD),
                whole(*weights.shape),
                pl.BlockSpec((GROUP * HD, tile), lambda i, where: (0, (1 - where[4]) * half_tiles + i)),
            ],
            out_specs=[
                pl.BlockSpec((rows, tile), lambda i, where: (0, i)),
                whole(rows, GROUP * HD),
            ],
        ),
        out_shape=[
            jax.ShapeDtypeStruct((rows, half_tiles * tile), jnp.float32),
            jax.ShapeDtypeStruct((rows, GROUP * HD), jnp.bfloat16),
        ],
        cost_estimate=pl.CostEstimate(
            flops=rows * width * HD * 2 + rows * GROUP * HD * 2560 * 2,
            bytes_accessed=9 << 20,
            transcendentals=0,
        ),
        compiler_params=pltpu.CompilerParams(vmem_limit_bytes=32 * 1024 * 1024),
        name="decode_outputs",
    )(where, dec_hidden, rollout, cached, weights, out_weight)


def own_kernel(where_ref, attended_ref, out_weight_ref, out_ref):
    out_ref[...] = jnp.dot(
        attended_ref[...], out_weight_ref[...], preferred_element_type=jnp.float32
    )


def own_outputs(where, attended, out_weight):
    rows, tile = attended.shape[0], 640
    half_tiles = out_weight.shape[1] // tile // 2
    return pl.pallas_call(
        own_kernel,
        grid_spec=pltpu.PrefetchScalarGridSpec(
            num_scalar_prefetch=1,
            grid=(half_tiles,),
            in_specs=[
                pl.BlockSpec((rows, GROUP * HD), lambda i, where: (0, 0)),
                pl.BlockSpec((GROUP * HD, tile), lambda i, where: (0, where[4] * half_tiles + i)),
            ],
            out_specs=pl.BlockSpec((rows, tile), lambda i, where: (0, i)),
        ),
        out_shape=jax.ShapeDtypeStruct((rows, half_tiles * tile), jnp.float32),
        cost_estimate=pl.CostEstimate(
            flops=rows * GROUP * HD * 2560 * 2, bytes_accessed=7 << 20, transcendentals=0
        ),
        name="own_outputs",
    )(where, attended, out_weight)


def join_kernel(where_ref, own_ref, rest_ref, out_ref):
    half = own_ref.shape[1]
    core = where_ref[4]
    out_ref[:, pl.ds(pl.multiple_of(core * half, half), half)] = own_ref[...]
    out_ref[:, pl.ds(pl.multiple_of((1 - core) * half, half), half)] = rest_ref[...]


def join_halves(where, own, rest):
    return pl.pallas_call(
        join_kernel,
        in_specs=[in_smem(), in_vmem(), in_vmem()],
        out_specs=in_vmem(),
        out_shape=jax.ShapeDtypeStruct((own.shape[0], 2 * own.shape[1]), own.dtype),
        name="join_halves",
    )(where, own, rest)


def shards(
    queries,
    attn_keys,
    hidden,
    out_grad,
    logp_new,
    logp_old,
    logp_ref,
    lengths,
    rewards,
    groups,
    master,
    first_moment,
    second_moment,
    dec_hidden,
    dec_query,
    dec_key,
    cache_keys,
    cache_values,
    cache_len,
    out_weight,
):
    bf, f32 = jnp.bfloat16, jnp.float32
    ctx = lax.axis_index("ctx")
    t = lax.axis_index("tp")
    x, g = ctx // NG, ctx % NG
    z, y = g // NY, g % NY

    def exchange(value, groups=None):
        return lax.all_to_all(
            value, "ctx", split_axis=0, concat_axis=0, axis_index_groups=groups, tiled=True
        )

    query_position = ctx * BLOCK + jnp.arange(BLOCK, dtype=jnp.int32)
    query_segment = segment_ids(lengths[0], query_position)
    own_advantage = pick(group_advantage(rewards, groups), t)
    token_weight = token_coef(
        own_advantage, query_segment, logp_new[0], logp_old[0], logp_ref[0], float(rewards.size)
    )
    dout_rows = (token_weight[:, None] * out_grad[0].astype(f32)).astype(bf)

    def along_x(d):
        return lambda x, z, y, t: (x + d, z, y, t)

    def for_head(head):
        width = GROUP * HD
        return jnp.concatenate(
            [
                lax.dynamic_slice_in_dim(queries[0], head * width, width, 1),
                lax.dynamic_slice_in_dim(dout_rows, head * width, width, 1),
            ],
            axis=1,
        )

    key_heads = attn_keys[0].reshape(BLOCK, KV, HD).transpose(1, 0, 2)
    key_heads = jnp.broadcast_to(key_heads[:, None], (NX, NG, BLOCK, HD))
    key_heads, *sent = together(key_heads, *[for_head((x + d) % NX) for d in range(NX)])
    blocks = [sent[0]] + [route(sent[d], along_x(d)) for d in range(1, NX)]
    keys = exchange(key_heads.reshape(NX * NG, BLOCK, HD)).reshape(SLAB, HD)

    def swap(x, z, y, t):
        return (t + 2 * (x // 2), z, y, x)

    def swap_and_flip(x, z, y, t):
        return (t + 2 * ((x ^ 2) // 2), z, y, x ^ 2)

    def flip_core(x, z, y, t):
        return (x, z, y, t ^ 1)

    def flip_chip(x, z, y, t):
        return (x, z, y, t ^ 2)

    state = jnp.stack([master, first_moment, second_moment]).reshape(3, 40, KV, HD)
    state, keys = together(state, keys)
    own_rows, keys, *blocks = together(hidden[0], keys, *blocks)
    hidden_parts = [route(own_rows, swap), None, route(own_rows, swap_and_flip), None]

    def over_tp(d):
        return lambda x, z, y, t: (x, z, y, t ^ d)

    moved = [pick(state, t, 2)] + [
        route(pick(state, t ^ d, 2), over_tp(d)) for d in range(1, NT)
    ]
    moved = jnp.stack(moved)
    by_row = jnp.stack([pick(moved, t ^ d) for d in range(NT)], axis=1)
    by_row = by_row.reshape(3, NT * 40, HD)

    old_weights, new_weights = decode_weights(dec_query, dec_key, cache_keys, cache_len)

    where = jnp.stack([g, lengths[0, 0], x, t, t % 2]).astype(jnp.int32)
    where, by_row, old_weights, new_weights = together(where, by_row, old_weights, new_weights)
    old_master, old_first, old_second = by_row
    partial = attention_terms(where, blocks, keys)

    along_zy = [[a * NG + b for b in range(NG)] for a in range(NX)]
    terms = exchange(partial.reshape(NG, NX * BLOCK, HD), along_zy)
    terms, hidden_parts[0], hidden_parts[2] = together(terms, hidden_parts[0], hidden_parts[2])
    dvalue = jnp.sum(terms.astype(f32), axis=0).astype(bf).reshape(NX, BLOCK, HD)
    dvalue = route(dvalue, swap)
    hidden_parts[1] = route(hidden_parts[0], flip_core)
    hidden_parts[3] = route(hidden_parts[2], flip_core)
    gradient = gradient_terms(where, dvalue, hidden_parts)
    terms = exchange(gradient.reshape(NX * NG, NT * 40, HD))
    gradient = jnp.sum(terms.astype(f32), axis=0)

    new_first = first_decay * old_first + (1.0 - first_decay) * gradient
    new_second = second_decay * old_second + (1.0 - second_decay) * gradient * gradient
    new_master = old_master - learn_rate * (
        new_first / (jnp.sqrt(new_second) + adam_eps) + decay_weight * old_master
    )
    cached = jnp.einsum(
        "srgc,rcd->srgd", old_weights, cache_values, preferred_element_type=f32
    ).reshape(-1, GROUP * HD)
    new_weights = new_weights.astype(f32).reshape(cached.shape[0], -1)
    rounded, cached, new_weights = together(new_master.astype(bf), cached, new_weights)
    rollout = exchange(jnp.broadcast_to(rounded[None], (NX * NG, NT * 40, HD))).reshape(5120, HD)

    news = jnp.stack([new_master, new_first, new_second]).reshape(3, NT, 40, HD)
    back = [pick(news, t, 1)] + [
        route(pick(news, t ^ d, 1), over_tp(d)) for d in range(1, NT)
    ]
    back = jnp.stack(back)
    back = jnp.stack([pick(back, t ^ d) for d in range(NT)], axis=2)
    rollout, back = together(rollout, back)
    new_master, new_first, new_second = back.reshape(3, 40, KV * HD)

    step_count, dec_rows = dec_hidden.shape[:2]
    rows = step_count * dec_rows
    other, attended = decode_outputs(
        where,
        dec_hidden.reshape(rows, dec_hidden.shape[2]),
        rollout,
        cached,
        new_weights,
        out_weight,
    )
    received = route(other, flip_core)
    on_chip = own_outputs(where, attended, out_weight) + received
    both = (on_chip + route(on_chip.astype(bf), flip_chip).astype(f32)).astype(bf)
    dec_out = join_halves(where, both, route(both, flip_core))
    dec_out = dec_out.reshape(step_count, dec_rows, out_weight.shape[1])
    return (new_master, new_first, new_second, rollout, dec_out)


def solution(mesh):
    return jax.shard_map(
        shards,
        mesh=mesh,
        in_specs=(
            P("tp", "ctx", None),
            P("tp", "ctx", None),
            P("tp", "ctx", None),
            P("tp", "ctx", None),
            P("tp", "ctx"),
            P("tp", "ctx"),
            P("tp", "ctx"),
            P("tp", None),
            P(),
            P(),
            P(("ctx", "tp"), None),
            P(("ctx", "tp"), None),
            P(("ctx", "tp"), None),
            P(None, "ctx", None),
            P(None, "ctx", "tp"),
            P(None, "ctx", "tp"),
            P("ctx", None, "tp"),
            P("ctx", None, "tp"),
            P("ctx"),
            P("tp", None),
        ),
        out_specs=(
            P(("ctx", "tp"), None),
            P(("ctx", "tp"), None),
            P(("ctx", "tp"), None),
            P(None, "tp"),
            P(None, "ctx", None),
        ),
        check_vma=False,
    )
```

time: 1290 us -> 246 us (0.19)
  waiting for transfers between devices: 989 us -> 57.2 us
  matrix products: 98.2 us -> 7.91 us
  starting transfers between devices: 0.34 us -> 81.1 us
  local copies, waits for them, and re-layouts: 70.6 us -> 24.1 us
  other arithmetic: 53.8 us -> 14.9 us
  Pallas kernels: 0 us -> 33.4 us
  blocking collectives: 50.3 us -> 24.2 us
  between operations: 14.1 us -> 1.16 us
    reduce_scatter x2 -> x0, waiting for transfers between devices: 849 us -> none  [the longest x1 666 us: shards(): lax.psum_scatter(lax.dot_general(local_hidden, dvalue, (((0,), (0,)), (()...]
    all_gather x2 -> x0, waiting for transfers between devices: 140 us -> none  [the longest x1 76.6 us: shards(): all_keys = lax.all_gather(attn_keys[0], 'ctx', axis=0, tiled=True)]
    dot_general x23 -> x3, matrix products: 98.2 us -> 7.91 us  [the longest x1 3.77 us: decode_weights(): jnp.einsum('srgd,rcd->srgc', query_heads, cache_keys, preferred_element_t...]
    psum x1 -> x0, blocking collectives: 50.3 us -> none  [shards(): step_outs.append(lax.psum(partial_out[step_index], 'tp'))]
    ppermute x0 -> x17, waiting for transfers between devices: none -> 41.9 us  [route(): return lax.ppermute(value, ('ctx', 'tp'), pairs)]
    ppermute x0 -> x17, starting transfers between devices: none -> 41 us  [route(): return lax.ppermute(value, ('ctx', 'tp'), pairs)]
    reduce_sum x10 -> x4, other arithmetic: 42.1 us -> 1.34 us  [the longest x1 0.73 us: decode_weights(): jnp.sum(old_exp, axis=3, keepdims=True)]
    all_to_all x0 -> x3, starting transfers between devices: none -> 40.2 us  [exchange(): lax.all_to_all(value, 'ctx', split_axis=0, concat_axis=0, axis_index_grou...]
  transfers between devices with their start and end apart: 4 -> 20, of which waited for: 4 -> 6; matrix products, arithmetic and copies ran while one was open for 1% -> 11% of each run, Pallas kernels for 0% -> 9%
where the time goes in v2:
time: 246 us; the launch traced here: 244 us
  starting transfers between devices  81.1 us (33%)
  waiting for transfers between devices  57.2 us (23%)
  Pallas kernels  33.4 us (14%)
  blocking collectives  24.2 us (10%)
  local copies, waits for them, and re-layouts  24.1 us (10%)
  other arithmetic  14.9 us (6%)
  matrix products  7.91 us (3%)
    ppermute x17, waiting for transfers between devices, route(): return lax.ppermute(value, ('ctx', 'tp'), pairs)  41.9 us
    ppermute x17, starting transfers between devices, route(): return lax.ppermute(value, ('ctx', 'tp'), pairs)  41 us
    all_to_all x3, starting transfers between devices, exchange(): lax.all_to_all(value, 'ctx', split_axis=0, concat_axis=0, axis_index_grou...  40.2 us
    all_to_all x1, blocking collectives, exchange(): lax.all_to_all(value, 'ctx', split_axis=0, concat_axis=0, axis_index_grou...  24.2 us
    pallas_call x1, Pallas kernels, attention_terms(): pl.pallas_call(attention_kernel, out_shape=jax.ShapeDtypeStruct((NG, NX,...  15.7 us
    all_to_all x3, waiting for transfers between devices, exchange(): lax.all_to_all(value, 'ctx', split_axis=0, concat_axis=0, axis_index_grou...  15.3 us
    unnamed x40, local copies, waits for them, and re-layouts  12.1 us
    pallas_call x1, Pallas kernels, own_outputs(): pl.pallas_call(own_kernel, grid_spec=pltpu.PrefetchScalarGridSpec(num_sca...  5.66 us
  transfers between devices with their start and end apart: 20, of which 6 were waited for; matrix products, arithmetic and copies ran while one was open for 11% of the time, Pallas kernels for 9%

profile of v2, /device:TPU:1, one launch (start us, length us, event | category | flops | bytes accessed | tf_op | source)
XLA Modules:
  0.0 244.0 jit_solution(12480771629668709981)
XLA Ops:
  0.7 0.9 reshape_squeeze.3
  5.4 1.6 fusion.4
  7.2 0.9 pad_maximum_fusion
  8.1 1.1 pad_maximum_fusion.2
  9.2 1.2 broadcast_in_dim.79
  10.4 11.3 %all-to-all-start = ((bf16[32,128,128]{2,1,0:T(8,128)(2,1)}), bf16[32,128,128]{2,1,0:T(8,128)(2,1)S(1)}, u32[]{:S(2)}, u32[]{:S(2)}) async-start(bf16[32,128,128]{2,1,0:T(8,128)(2,1)} %bitcast.16), calls=%async_computation | async-start | bytes 2097152 | tf_op jit(solution)/shard_map/all_to_all | solution.py:369
  21.7 1.3 collective-permute-start.3
  23.0 2.4 collective-permute-start.4
  25.5 1.1 collective-permute-start.5
  26.8 3.8 %fusion.5 = (f32[4,32,8]{2,0,1:T(4,128)S(1)}, f32[32,512,4,8]{1,3,2,0:T(8,128)S(1)}) fusion(pred[32,512]{1,0:T(8,128)(4,1)S(1)} %iota_compare_fusion, bf16[32,512,128]{2,1,0:T(8,128)(2,1)} %param.36, bf16[4,32,8,128]{3,2,1,0:T(8,128)(2,1)S(1)} %bitcast.179), kind=kOutput, calls=%fused_computation.9 | convolution fusion | flops 135789568 | bytes 6574080 | tf_op jit(solution)/shard_map/srgd,rcd->srgc/dot_general | solution.py:207
  30.6 1.3 select_reduce_fusion
  32.9 1.7 divide_convert_fusion
  34.6 1.5 stack.106
  36.1 1.5 stack.105
  37.7 1.5 stack.104
  39.2 1.7 pad_maximum_fusion.4
  41.0 2.3 constant_dynamic-slice_fusion.7
  43.2 2.4 collective-permute-start.2
  45.6 1.1 collective-permute-start.1
  46.9 2.6 %collective-permute-start = (f32[3,40,128]{2,1,0:T(8,128)}, f32[3,40,128]{2,1,0:T(8,128)}, u32[]{:S(2)}, u32[]{:S(2)}) collective-permute-start(f32[3,40,128]{2,1,0:T(8,128)} %bitcast.19), channel_id=1, source_target_pairs={{0,1},{1,0},{2,3},{3,2},{4,5},{5,4},{6,7},{7,6},{8,9},{9,8},{10,11... | collective-permute-start | bytes 184328 | tf_op jit(solution)/shard_map/ppermute | solution.py:39
  50.5 7.6 %collective-permute-done.4.refs_2_ = bf16[128,2048]{1,0:T(8,128)(2,1)S(1)} collective-permute-done((bf16[128,2048]{1,0:T(8,128)(2,1)}, bf16[128,2048]{1,0:T(8,128)(2,1)S(1)}, u32[]{:S(2)}, u32[]{:S(2)}) %collective-permute-start.4) | collective-permute-done | bytes 524320 | tf_op jit(solution)/shard_map/ppermute | solution.py:39
  58.1 3.3 %collective-permute-start.6 = (bf16[128,5120]{1,0:T(8,128)(2,1)}, bf16[128,5120]{1,0:T(8,128)(2,1)}, u32[]{:S(2)}, u32[]{:S(2)}) collective-permute-start(bf16[128,5120]{1,0:T(8,128)(2,1)} %bitcast.202), channel_id=1, source_target_pairs={{0,0},{1,32},{2,64},{3,96},{4,4},{5,36},{6,68},{7,100},{8,8},{9,40... | collective-permute-start | bytes 3932168 | tf_op jit(solution)/shard_map/ppermute | solution.py:39
  61.4 3.6 %collective-permute-start.7 = (bf16[128,5120]{1,0:T(8,128)(2,1)}, bf16[128,5120]{1,0:T(8,128)(2,1)}, u32[]{:S(2)}, u32[]{:S(2)}) collective-permute-start(bf16[128,5120]{1,0:T(8,128)(2,1)} %bitcast.203), channel_id=1, source_target_pairs={{0,66},{1,98},{2,2},{3,34},{4,70},{5,102},{6,6},{7,38},{8,74},{9,1... | collective-permute-start | bytes 3932168 | tf_op jit(solution)/shard_map/ppermute | solution.py:39
  65.0 0.9 pad_maximum_fusion.5
  66.0 15.7 %attention_terms.1 = bf16[8,4,128,128]{3,2,1,0:T(8,128)(2,1)S(1)} custom-call(s32[5]{0:T(128)S(1)} %stack.103.where_ref, bf16[128,2048]{1,0:T(8,128)(2,1)S(1)} %get-tuple-element.41.refs_0_, bf16[128,2048]{1,0:T(8,128)(2,1)S(1)} %collective-permute-done.3.refs_1_, bf16[128,2048]{1,0:T(8,128)(2,1)S(1)} %collective-permute-done.4.refs_2_, ...), custom_call_target="tpu_custom_call" | custom-call | flops 8589934592 | bytes 6291456 | tf_op jit(solution)/shard_map/attention_terms/pallas_call | solution.py:154
  81.7 24.2 %all_to_all.20 = bf16[8,512,128]{2,1,0:T(8,128)(2,1)S(1)} all-to-all(bf16[8,512,128]{2,1,0:T(8,128)(2,1)S(1)} %bitcast.173), channel_id=1, replica_groups={{0,4,8,12,16,20,24,28},{32,36,40,44,48,52,56,60},{64,68,72,76,80,84,88,..., dimensions={0} | all-to-all | bytes 2097152 | tf_op jit(solution)/shard_map/all_to_all | solution.py:369
  106.0 10.6 %collective-permute-start.9 = (bf16[128,5120]{1,0:T(8,128)(2,1)}, bf16[128,5120]{1,0:T(8,128)(2,1)S(1)}, u32[]{:S(2)}, u32[]{:S(2)}) collective-permute-start(bf16[128,5120]{1,0:T(8,128)(2,1)} %collective-permute-done.6.h0_ref), channel_id=1, source_target_pairs={{0,1},{1,0},{2,3},{3,2},{4,5},{5,4},{6,7},{7,6},{8,9},{9,8},{10,11... | collective-permute-start | bytes 3932168 | tf_op jit(solution)/shard_map/ppermute | solution.py:39
  116.8 1.9 collective-permute-start.8
  118.7 4.4 %collective-permute-done.8.dvalue_ref = bf16[4,128,128]{2,1,0:T(8,128)(2,1)S(1)} collective-permute-done((bf16[4,128,128]{2,1,0:T(8,128)(2,1)S(1)}, bf16[4,128,128]{2,1,0:T(8,128)(2,1)S(1)}, u32[]{:S(2)}, u32[]{:S(2)}) %collective-permute-start.8) | collective-permute-done | bytes 131104 | tf_op jit(solution)/shard_map/ppermute | solution.py:39
  124.2 5.2 %gradient_terms.1 = bf16[5120,128]{1,0:T(8,128)(2,1)} custom-call(s32[5]{0:T(128)} %copy-done.3, bf16[4,128,128]{2,1,0:T(8,128)(2,1)} %copy-done.12, bf16[128,5120]{1,0:T(8,128)(2,1)} %collective-permute-done.6.h0_ref, bf16[128,5120]{1,0:T(8,128)(2,1)} %copy-done.7, bf16[128,5120]{1,0:T(8,128)(2,1)} %collective-permute-done.7.h2_ref, ...), custom_call_target="tpu_custom_call" | custom-call | flops 671088640 | bytes 7340032 | tf_op jit(solution)/shard_map/gradient_terms/pallas_call | solution.py:184
  129.3 24.2 %all-to-all-start.2 = ((bf16[32,160,128]{2,1,0:T(8,128)(2,1)}), bf16[32,160,128]{2,1,0:T(8,128)(2,1)S(1)}, u32[]{:S(2)}, u32[]{:S(2)}) async-start(bf16[32,160,128]{2,1,0:T(8,128)(2,1)} %bitcast.174), calls=%async_computation.2 | async-start | bytes 2621440 | tf_op jit(solution)/shard_map/all_to_all | solution.py:369
  153.5 2.9 %fusion.9 = f32[4,32,8,128]{3,2,0,1:T(8,128)S(1)} fusion(bf16[4,32,8,512]{3,2,0,1:T(8,128)(2,1)S(1)} %copy-done.5, bf16[32,512,128]{2,1,0:T(8,128)(2,1)} %param.37), kind=kOutput, calls=%fused_computation.15 | convolution fusion | flops 134217728 | bytes 5767168 | tf_op jit(solution)/shard_map/srgc,rcd->srgd/dot_general | solution.py:450
  157.6 15.2 %all-to-all-done.2 = bf16[32,160,128]{2,1,0:T(8,128)(2,1)S(1)} async-done(((bf16[32,160,128]{2,1,0:T(8,128)(2,1)}), bf16[32,160,128]{2,1,0:T(8,128)(2,1)S(1)}, u32[]{:S(2)}, u32[]{:S(2)}) %all-to-all-start.2) | async-done | bytes 1310752 | tf_op jit(solution)/shard_map/all_to_all | solution.py:369
  173.1 1.2 broadcast_in_dim.89
  174.3 4.7 %all-to-all-start.3 = ((bf16[32,160,128]{2,1,0:T(8,128)(2,1)}), bf16[32,160,128]{2,1,0:T(8,128)(2,1)S(1)}, u32[]{:S(2)}, u32[]{:S(2)}) async-start(bf16[32,160,128]{2,1,0:T(8,128)(2,1)} %broadcast_in_dim.89), calls=%async_computation.3 | async-start | bytes 2621440 | tf_op jit(solution)/shard_map/all_to_all | solution.py:369
  179.8 4.7 %collective-permute-start.13 = (f32[3,40,128]{2,1,0:T(8,128)}, f32[3,40,128]{2,1,0:T(8,128)S(1)}, u32[]{:S(2)}, u32[]{:S(2)}) collective-permute-start(f32[3,40,128]{2,1,0:T(8,128)} %get-tuple-element.82), channel_id=1, source_target_pairs={{0,3},{1,2},{2,1},{3,0},{4,7},{5,6},{6,5},{7,4},{8,11},{9,10},{10,... | collective-permute-start | bytes 184328 | tf_op jit(solution)/shard_map/ppermute | solution.py:39
  184.9 14.6 %collective-permute-done.13 = f32[3,40,128]{2,1,0:T(8,128)S(1)} collective-permute-done((f32[3,40,128]{2,1,0:T(8,128)}, f32[3,40,128]{2,1,0:T(8,128)S(1)}, u32[]{:S(2)}, u32[]{:S(2)}) %collective-permute-start.13) | collective-permute-done | bytes 61472 | tf_op jit(solution)/shard_map/ppermute | solution.py:39
  199.5 0.9 pad_maximum_fusion.8
  200.7 4.0 %copy-done = bf16[1024,5120]{1,0:T(8,128)(2,1)S(1)} copy-done((bf16[1024,5120]{1,0:T(8,128)(2,1)S(1)}, bf16[1024,5120]{1,0:T(8,128)(2,1)}, u32[]{:S(2)}) %copy-start) | copy-done | bytes 10485784
  204.7 4.4 %decode_outputs.1 = (f32[128,2560]{1,0:T(8,128)}, bf16[128,1024]{1,0:T(8,128)(2,1)S(1)}) custom-call(s32[5]{0:T(128)S(1)} %copy-done.4, bf16[128,5120]{1,0:T(8,128)(2,1)S(1)} %bitcast.171, bf16[5120,128]{1,0:T(8,128)(2,1)S(1)} %bitcast.168, f32[128,1024]{1,0:T(8,128)S(1)} %bitcast.170, f32[128,32]{1,0:T(8,128)S(1)} %copy.53.weights_ref, ...), custom_call_target="tpu_custom_call" | custom-call | flops 838860800 | bytes 9437184 | tf_op jit(solution)/shard_map/decode_outputs/pallas_call | solution.py:264
  209.8 1.5 collective-permute-start.14
  211.3 5.7 %own_outputs.1 = f32[128,2560]{1,0:T(8,128)} custom-call(s32[5]{0:T(128)} %copy-done.3, bf16[128,1024]{1,0:T(8,128)(2,1)} %copy-done.2, bf16[1024,5120]{1,0:T(8,128)(2,1)} %out_weight_ref.3), custom_call_target="tpu_custom_call" | custom-call | flops 671088640 | bytes 7340032 | tf_op jit(solution)/shard_map/own_outputs/pallas_call | solution.py:304
  216.9 1.5 fusion.33
  218.4 3.3 %collective-permute-start.15 = (bf16[128,2560]{1,0:T(8,128)(2,1)S(1)}, bf16[128,2560]{1,0:T(8,128)(2,1)S(1)}, u32[]{:S(2)}, u32[]{:S(2)}) collective-permute-start(bf16[128,2560]{1,0:T(8,128)(2,1)S(1)} %get-tuple-element.61), channel_id=1, source_target_pairs={{0,2},{1,3},{2,0},{3,1},{4,6},{5,7},{6,4},{7,5},{8,10},{9,11},{10,... | collective-permute-start | bytes 1966088 | tf_op jit(solution)/shard_map/ppermute | solution.py:39
  221.7 15.1 %collective-permute-done.15 = bf16[128,2560]{1,0:T(8,128)(2,1)S(1)} collective-permute-done((bf16[128,2560]{1,0:T(8,128)(2,1)S(1)}, bf16[128,2560]{1,0:T(8,128)(2,1)S(1)}, u32[]{:S(2)}, u32[]{:S(2)}) %collective-permute-start.15) | collective-permute-done | bytes 655392 | tf_op jit(solution)/shard_map/ppermute | solution.py:39
  239.6 0.9 copy-done.9
  240.5 2.4 join_halves.1
  242.9 1.1 copy.85
  (95 shorter events, 14.2 us)
Async XLA Ops:
  5.4 1.7 copy-start.8
  9.2 17.5 %copy-start.13 = (s32[32]{0:T(128)S(1)}, s32[32]{0:T(128)}, u32[]{:S(2)}) copy-start(s32[32]{0:T(128)} %param.38) | copy-start | bytes 388
  9.2 17.5 %copy-start.11 = (bf16[4,32,1024]{2,1,0:T(8,128)(2,1)S(1)}, bf16[4,32,1024]{2,1,0:T(8,128)(2,1)}, u32[]{:S(2)}) copy-start(bf16[4,32,1024]{2,1,0:T(8,128)(2,1)} %param.34) | copy-start | bytes 786436
  10.4 30.6 %all-to-all-start = ((bf16[32,128,128]{2,1,0:T(8,128)(2,1)}), bf16[32,128,128]{2,1,0:T(8,128)(2,1)S(1)}, u32[]{:S(2)}, u32[]{:S(2)}) async-start(bf16[32,128,128]{2,1,0:T(8,128)(2,1)} %bitcast.16), calls=%async_computation | async-start | bytes 2097152 | tf_op jit(solution)/shard_map/all_to_all | solution.py:369
  21.7 25.2 %collective-permute-start.3 = (bf16[128,2048]{1,0:T(8,128)(2,1)}, bf16[128,2048]{1,0:T(8,128)(2,1)S(1)}, u32[]{:S(2)}, u32[]{:S(2)}) collective-permute-start(bf16[128,2048]{1,0:T(8,128)(2,1)} %get-tuple-element.38), channel_id=1, source_target_pairs={{0,32},{1,33},{2,34},{3,35},{4,36},{5,37},{6,38},{7,39},{8,40},{9,... | collective-permute-start | bytes 1572872 | tf_op jit(solution)/shard_map/ppermute | solution.py:39
  23.0 35.1 %collective-permute-start.4 = (bf16[128,2048]{1,0:T(8,128)(2,1)}, bf16[128,2048]{1,0:T(8,128)(2,1)S(1)}, u32[]{:S(2)}, u32[]{:S(2)}) collective-permute-start(bf16[128,2048]{1,0:T(8,128)(2,1)} %get-tuple-element.39), channel_id=1, source_target_pairs={{0,64},{1,65},{2,66},{3,67},{4,68},{5,69},{6,70},{7,71},{8,72},{9,... | collective-permute-start | bytes 1572872 | tf_op jit(solution)/shard_map/ppermute | solution.py:39
  25.5 32.6 %collective-permute-start.5 = (bf16[128,2048]{1,0:T(8,128)(2,1)}, bf16[128,2048]{1,0:T(8,128)(2,1)S(1)}, u32[]{:S(2)}, u32[]{:S(2)}) collective-permute-start(bf16[128,2048]{1,0:T(8,128)(2,1)} %get-tuple-element.40), channel_id=1, source_target_pairs={{0,96},{1,97},{2,98},{3,99},{4,100},{5,101},{6,102},{7,103},{8,104... | collective-permute-start | bytes 1572872 | tf_op jit(solution)/shard_map/ppermute | solution.py:39
  26.8 3.8 %copy-start.15 = (bf16[4,32,128]{2,1,0:T(8,128)(2,1)S(1)}, bf16[4,32,128]{2,1,0:T(8,128)(2,1)}, u32[]{:S(2)}) copy-start(bf16[4,32,128]{2,1,0:T(8,128)(2,1)} %param.35) | copy-start | bytes 98308
  32.9 17.5 %copy-start.14 = (s32[1,2]{1,0:T(1,128)S(1)}, s32[1,2]{1,0:T(1,128)}, u32[]{:S(2)}) copy-start(s32[1,2]{1,0:T(1,128)} %param.27) | copy-start | bytes 28
  43.2 21.7 %collective-permute-start.2 = (f32[3,40,128]{2,1,0:T(8,128)}, f32[3,40,128]{2,1,0:T(8,128)}, u32[]{:S(2)}, u32[]{:S(2)}) collective-permute-start(f32[3,40,128]{2,1,0:T(8,128)} %bitcast.23), channel_id=1, source_target_pairs={{0,3},{1,2},{2,1},{3,0},{4,7},{5,6},{6,5},{7,4},{8,11},{9,10},{10,... | collective-permute-start | bytes 184328 | tf_op jit(solution)/shard_map/ppermute | solution.py:39
  45.6 19.4 %collective-permute-start.1 = (f32[3,40,128]{2,1,0:T(8,128)}, f32[3,40,128]{2,1,0:T(8,128)}, u32[]{:S(2)}, u32[]{:S(2)}) collective-permute-start(f32[3,40,128]{2,1,0:T(8,128)} %bitcast.21), channel_id=1, source_target_pairs={{0,2},{1,3},{2,0},{3,1},{4,6},{5,7},{6,4},{7,5},{8,10},{9,11},{10,... | collective-permute-start | bytes 184328 | tf_op jit(solution)/shard_map/ppermute | solution.py:39
  46.9 18.1 %collective-permute-start = (f32[3,40,128]{2,1,0:T(8,128)}, f32[3,40,128]{2,1,0:T(8,128)}, u32[]{:S(2)}, u32[]{:S(2)}) collective-permute-start(f32[3,40,128]{2,1,0:T(8,128)} %bitcast.19), channel_id=1, source_target_pairs={{0,1},{1,0},{2,3},{3,2},{4,5},{5,4},{6,7},{7,6},{8,9},{9,8},{10,11... | collective-permute-start | bytes 184328 | tf_op jit(solution)/shard_map/ppermute | solution.py:39
  50.5 31.2 %copy-start.3 = (s32[5]{0:T(128)}, s32[5]{0:T(128)S(1)}, u32[]{:S(2)}) copy-start(s32[5]{0:T(128)S(1)} %stack.103.where_ref) | copy-start | bytes 64
  58.1 47.9 %collective-permute-start.6 = (bf16[128,5120]{1,0:T(8,128)(2,1)}, bf16[128,5120]{1,0:T(8,128)(2,1)}, u32[]{:S(2)}, u32[]{:S(2)}) collective-permute-start(bf16[128,5120]{1,0:T(8,128)(2,1)} %bitcast.202), channel_id=1, source_target_pairs={{0,0},{1,32},{2,64},{3,96},{4,4},{5,36},{6,68},{7,100},{8,8},{9,40... | collective-permute-start | bytes 3932168 | tf_op jit(solution)/shard_map/ppermute | solution.py:39
  61.4 44.6 %collective-permute-start.7 = (bf16[128,5120]{1,0:T(8,128)(2,1)}, bf16[128,5120]{1,0:T(8,128)(2,1)}, u32[]{:S(2)}, u32[]{:S(2)}) collective-permute-start(bf16[128,5120]{1,0:T(8,128)(2,1)} %bitcast.203), channel_id=1, source_target_pairs={{0,66},{1,98},{2,2},{3,34},{4,70},{5,102},{6,6},{7,38},{8,74},{9,1... | collective-permute-start | bytes 3932168 | tf_op jit(solution)/shard_map/ppermute | solution.py:39
  106.0 17.1 %collective-permute-start.9 = (bf16[128,5120]{1,0:T(8,128)(2,1)}, bf16[128,5120]{1,0:T(8,128)(2,1)S(1)}, u32[]{:S(2)}, u32[]{:S(2)}) collective-permute-start(bf16[128,5120]{1,0:T(8,128)(2,1)} %collective-permute-done.6.h0_ref), channel_id=1, source_target_pairs={{0,1},{1,0},{2,3},{3,2},{4,5},{5,4},{6,7},{7,6},{8,9},{9,8},{10,11... | collective-permute-start | bytes 3932168 | tf_op jit(solution)/shard_map/ppermute | solution.py:39
  116.5 6.5 %collective-permute-start.10 = (bf16[128,5120]{1,0:T(8,128)(2,1)}, bf16[128,5120]{1,0:T(8,128)(2,1)}, u32[]{:S(2)}, u32[]{:S(2)}) collective-permute-start(bf16[128,5120]{1,0:T(8,128)(2,1)} %collective-permute-done.7.h2_ref), channel_id=1, source_target_pairs={{0,1},{1,0},{2,3},{3,2},{4,5},{5,4},{6,7},{7,6},{8,9},{9,8},{10,11... | collective-permute-start | bytes 3932168 | tf_op jit(solution)/shard_map/ppermute | solution.py:39
  116.8 6.3 %collective-permute-start.8 = (bf16[4,128,128]{2,1,0:T(8,128)(2,1)S(1)}, bf16[4,128,128]{2,1,0:T(8,128)(2,1)S(1)}, u32[]{:S(2)}, u32[]{:S(2)}) collective-permute-start(bf16[4,128,128]{2,1,0:T(8,128)(2,1)S(1)} %bitcast.194), channel_id=1, source_target_pairs={{0,0},{1,32},{2,64},{3,96},{4,4},{5,36},{6,68},{7,100},{8,8},{9,40... | collective-permute-start | bytes 393224 | tf_op jit(solution)/shard_map/ppermute | solution.py:39
  123.1 0.7 copy-start.12
  123.1 1.1 copy-start.7
  129.3 24.2 %copy-start.5 = (bf16[4,32,8,512]{3,2,0,1:T(8,128)(2,1)S(1)}, bf16[4,32,8,512]{3,2,0,1:T(8,128)(2,1)}, u32[]{:S(2)}) copy-start(bf16[4,32,8,512]{3,2,0,1:T(8,128)(2,1)} %divide_convert_fusion) | copy-start | bytes 3145732
  129.3 43.5 %all-to-all-start.2 = ((bf16[32,160,128]{2,1,0:T(8,128)(2,1)}), bf16[32,160,128]{2,1,0:T(8,128)(2,1)S(1)}, u32[]{:S(2)}, u32[]{:S(2)}) async-start(bf16[32,160,128]{2,1,0:T(8,128)(2,1)} %bitcast.174), calls=%async_computation.2 | async-start | bytes 2621440 | tf_op jit(solution)/shard_map/all_to_all | solution.py:369
  156.4 0.9 copy-start.10
  174.3 26.4 %all-to-all-start.3 = ((bf16[32,160,128]{2,1,0:T(8,128)(2,1)}), bf16[32,160,128]{2,1,0:T(8,128)(2,1)S(1)}, u32[]{:S(2)}, u32[]{:S(2)}) async-start(bf16[32,160,128]{2,1,0:T(8,128)(2,1)} %broadcast_in_dim.89), calls=%async_computation.3 | async-start | bytes 2621440 | tf_op jit(solution)/shard_map/all_to_all | solution.py:369
  179.0 21.7 %copy-start.1 = (bf16[4,32,5120]{2,1,0:T(8,128)(2,1)S(1)}, bf16[4,32,5120]{2,1,0:T(8,128)(2,1)}, u32[]{:S(2)}) copy-start(bf16[4,32,5120]{2,1,0:T(8,128)(2,1)} %param.33) | copy-start | bytes 3932164
  179.0 21.7 %copy-start.4 = (s32[5]{0:T(128)S(1)}, s32[5]{0:T(128)}, u32[]{:S(2)}) copy-start(s32[5]{0:T(128)} %copy-done.3) | copy-start | bytes 64
  179.8 19.8 %collective-permute-start.13 = (f32[3,40,128]{2,1,0:T(8,128)}, f32[3,40,128]{2,1,0:T(8,128)S(1)}, u32[]{:S(2)}, u32[]{:S(2)}) collective-permute-start(f32[3,40,128]{2,1,0:T(8,128)} %get-tuple-element.82), channel_id=1, source_target_pairs={{0,3},{1,2},{2,1},{3,0},{4,7},{5,6},{6,5},{7,4},{8,11},{9,10},{10,... | collective-permute-start | bytes 184328 | tf_op jit(solution)/shard_map/ppermute | solution.py:39
  184.4 15.1 %collective-permute-start.12 = (f32[3,40,128]{2,1,0:T(8,128)S(1)}, f32[3,40,128]{2,1,0:T(8,128)S(1)}, u32[]{:S(2)}, u32[]{:S(2)}) collective-permute-start(f32[3,40,128]{2,1,0:T(8,128)S(1)} %get-tuple-element.83), channel_id=1, source_target_pairs={{0,2},{1,3},{2,0},{3,1},{4,6},{5,7},{6,4},{7,5},{8,10},{9,11},{10,... | collective-permute-start | bytes 184328 | tf_op jit(solution)/shard_map/ppermute | solution.py:39
  184.4 15.1 %collective-permute-start.11 = (f32[3,40,128]{2,1,0:T(8,128)S(1)}, f32[3,40,128]{2,1,0:T(8,128)}, u32[]{:S(2)}, u32[]{:S(2)}) collective-permute-start(f32[3,40,128]{2,1,0:T(8,128)S(1)} %get-tuple-element.84), channel_id=1, source_target_pairs={{0,1},{1,0},{2,3},{3,2},{4,5},{5,4},{6,7},{7,6},{8,9},{9,8},{10,11... | collective-permute-start | bytes 184328 | tf_op jit(solution)/shard_map/ppermute | solution.py:39
  200.7 4.0 %copy-start = (bf16[1024,5120]{1,0:T(8,128)(2,1)S(1)}, bf16[1024,5120]{1,0:T(8,128)(2,1)}, u32[]{:S(2)}) copy-start(bf16[1024,5120]{1,0:T(8,128)(2,1)} %out_weight_ref.3) | copy-start | bytes 31457284
  209.1 0.7 copy-start.2
  209.8 7.1 %collective-permute-start.14 = (f32[128,2560]{1,0:T(8,128)}, f32[128,2560]{1,0:T(8,128)S(1)}, u32[]{:S(2)}, u32[]{:S(2)}) collective-permute-start(f32[128,2560]{1,0:T(8,128)} %get-tuple-element.58), channel_id=1, source_target_pairs={{0,1},{1,0},{2,3},{3,2},{4,5},{5,4},{6,7},{7,6},{8,9},{9,8},{10,11... | collective-permute-start | bytes 3932168 | tf_op jit(solution)/shard_map/ppermute | solution.py:39
  218.4 18.4 %collective-permute-start.15 = (bf16[128,2560]{1,0:T(8,128)(2,1)S(1)}, bf16[128,2560]{1,0:T(8,128)(2,1)S(1)}, u32[]{:S(2)}, u32[]{:S(2)}) collective-permute-start(bf16[128,2560]{1,0:T(8,128)(2,1)S(1)} %get-tuple-element.61), channel_id=1, source_target_pairs={{0,2},{1,3},{2,0},{3,1},{4,6},{5,7},{6,4},{7,5},{8,10},{9,11},{10,... | collective-permute-start | bytes 1966088 | tf_op jit(solution)/shard_map/ppermute | solution.py:39
  237.0 2.6 %copy-start.6 = (bf16[128,2560]{1,0:T(8,128)(2,1)}, bf16[128,2560]{1,0:T(8,128)(2,1)S(1)}, u32[]{:S(2)}) copy-start(bf16[128,2560]{1,0:T(8,128)(2,1)S(1)} %add_convert_fusion.own_ref) | copy-start | bytes 1966084
  237.0 2.6 %collective-permute-start.16 = (bf16[128,2560]{1,0:T(8,128)(2,1)S(1)}, bf16[128,2560]{1,0:T(8,128)(2,1)S(1)}, u32[]{:S(2)}, u32[]{:S(2)}) collective-permute-start(bf16[128,2560]{1,0:T(8,128)(2,1)S(1)} %add_convert_fusion.own_ref), channel_id=1, source_target_pairs={{0,1},{1,0},{2,3},{3,2},{4,5},{5,4},{6,7},{7,6},{8,9},{9,8},{10,11... | collective-permute-start | bytes 1966088 | tf_op jit(solution)/shard_map/ppermute | solution.py:39
  239.6 0.9 copy-start.9

commit v3 on v2

--- a/solution.py
+++ b/solution.py
@@ -80,9 +80,17 @@
 
 
 def attention_kernel(where_ref, *refs):
-    block_refs, refs = refs[:NX], refs[NX:]
-    keys_ref, out_ref, query_rows, dout_rows, scores, sums = refs
+    block_refs, key_refs, refs = refs[:NX], refs[NX : NX + NG], refs[NX + NG :]
+    out_ref, keys_ref, query_rows, dout_rows, scores, sums = refs
     g, bound, own = where_ref[0], where_ref[1], where_ref[2]
+    for dz in range(NZ):
+        for dy in range(NY):
+            part = key_refs[dz * NY + dy]
+            part_g = lax.rem(g // NY - dz + NZ, NZ) * NY + lax.rem(g - dy + NG, NY)
+            for d in range(NX):
+                part_x = lax.rem(own - d + NX, NX)
+                rows = pl.ds(pl.multiple_of((part_x * NG + part_g) * BLOCK, BLOCK), BLOCK)
+                keys_ref[rows, :] = part[d]
     for slot in range(NX):
         for h in range(GROUP):
             rows = pl.ds(h * BLOCK, BLOCK)
@@ -146,17 +154,20 @@
 
     lax.fori_loop(0, NX, one_block, 0)
     for x in range(NX):
-        for g_to in range(NG):
-            out_ref[g_to, x] = sums[pl.ds((x * NG + g_to) * BLOCK, BLOCK), :].astype(out_ref.dtype)
+        for y in range(NY):
+            for z in range(NZ):
+                rows = pl.ds(((x * NZ + z) * NY + y) * BLOCK, BLOCK)
+                out_ref[x * NY + y, z] = sums[rows, :].astype(out_ref.dtype)
 
 
 def attention_terms(where, blocks, keys):
     return pl.pallas_call(
         attention_kernel,
-        out_shape=jax.ShapeDtypeStruct((NG, NX, BLOCK, HD), jnp.bfloat16),
-        in_specs=[in_smem()] + [in_vmem()] * (NX + 1),
+        out_shape=jax.ShapeDtypeStruct((NX * NY, NZ, BLOCK, HD), jnp.bfloat16),
+        in_specs=[in_smem()] + [in_vmem()] * (NX + NG),
         out_specs=in_vmem(),
         scratch_shapes=[
+            pltpu.VMEM((SLAB, HD), jnp.bfloat16),
             pltpu.VMEM((NX, ROWS, HD), jnp.bfloat16),
             pltpu.VMEM((NX, ROWS, HD), jnp.bfloat16),
             pltpu.VMEM((SLAB, ROWS), jnp.float32),
@@ -164,10 +175,10 @@
         ],
         compiler_params=pltpu.CompilerParams(vmem_limit_bytes=48 * 1024 * 1024),
         cost_estimate=pl.CostEstimate(
-            flops=4 * SLAB * SLAB * HD, bytes_accessed=6 << 20, transcendentals=SLAB * SLAB // 2
+            flops=SLAB, bytes_accessed=SLAB, transcendentals=0
         ),
         name="attention_terms",
-    )(where, *blocks, keys)
+    )(where, *blocks, *keys)
 
 
 def gradient_kernel(where_ref, dvalue_ref, h0_ref, h1_ref, h2_ref, h3_ref, out_ref):
@@ -226,115 +237,6 @@
     old_weights = (old_exp / denom).astype(jnp.bfloat16)
     new_weights = (new_exp / denom).astype(jnp.bfloat16)
     return old_weights, new_weights
-
-
-def decode_kernel(where_ref, hidden_ref, rollout_ref, cached_ref, weights_ref, out_weight_ref, out_ref, attended_ref):
-    steps = weights_ref.shape[1] // GROUP
-    rows = hidden_ref.shape[0] // steps
-
-    @pl.when(pl.program_id(0) == 0)
-    def _():
-        fresh = jnp.dot(hidden_ref[...], rollout_ref[...], preferred_element_type=jnp.float32)
-        fresh = fresh.astype(jnp.bfloat16).astype(jnp.float32)
-        repeated = [
-            jnp.concatenate([fresh[j * rows : (j + 1) * rows]] * steps, axis=0)
-            for j in range(steps)
-        ]
-        for h in range(GROUP):
-            columns = pl.ds(h * HD, HD)
-            total = cached_ref[:, columns]
-            for j in range(steps):
-                at = h * steps + j
-                total = total + weights_ref[:, at : at + 1] * repeated[j]
-            attended_ref[:, columns] = total.astype(attended_ref.dtype)
-
-    out_ref[...] = jnp.dot(
-        attended_ref[...], out_weight_ref[...], preferred_element_type=jnp.float32
-    )
-
-
-def decode_outputs(where, dec_hidden, rollout, cached, weights, out_weight):
-    rows, width = dec_hidden.shape
-    tile = 640
-    half_tiles = out_weight.shape[1] // tile // 2
-
-    def whole(*shape):
-        return pl.BlockSpec(shape, lambda i, where: (0, 0))
-
-    return pl.pallas_call(
-        decode_kernel,
-        grid_spec=pltpu.PrefetchScalarGridSpec(
-            num_scalar_prefetch=1,
-            grid=(half_tiles,),
-            in_specs=[
-                whole(rows, width),
-                whole(width, HD),
-                whole(rows, GROUP * HD),
-                whole(*weights.shape),
-                pl.BlockSpec((GROUP * HD, tile), lambda i, where: (0, (1 - where[4]) * half_tiles + i)),
-            ],
-            out_specs=[
-                pl.BlockSpec((rows, tile), lambda i, where: (0, i)),
-                whole(rows, GROUP * HD),
-            ],
-        ),
-        out_shape=[
-            jax.ShapeDtypeStruct((rows, half_tiles * tile), jnp.float32),
-            jax.ShapeDtypeStruct((rows, GROUP * HD), jnp.bfloat16),
-        ],
-        cost_estimate=pl.CostEstimate(
-            flops=rows * width * HD * 2 + rows * GROUP * HD * 2560 * 2,
-            bytes_accessed=9 << 20,
-            transcendentals=0,
-        ),
-        compiler_params=pltpu.CompilerParams(vmem_limit_bytes=32 * 1024 * 1024),
-        name="decode_outputs",
-    )(where, dec_hidden, rollout, cached, weights, out_weight)
-
-
-def own_kernel(where_ref, attended_ref, out_weight_ref, out_ref):
-    out_ref[...] = jnp.dot(
-        attended_ref[...], out_weight_ref[...], preferred_element_type=jnp.float32
-    )
-
-
-def own_outputs(where, attended, out_weight):
-    rows, tile = attended.shape[0], 640
-    half_tiles = out_weight.shape[1] // tile // 2
-    return pl.pallas_call(
-        own_kernel,
-        grid_spec=pltpu.PrefetchScalarGridSpec(
-            num_scalar_prefetch=1,
-            grid=(half_tiles,),
-            in_specs=[
-                pl.BlockSpec((rows, GROUP * HD), lambda i, where: (0, 0)),
-                pl.BlockSpec((GROUP * HD, tile), lambda i, where: (0, where[4] * half_tiles + i)),
-            ],
-            out_specs=pl.BlockSpec((rows, tile), lambda i, where: (0, i)),
-        ),
-        out_shape=jax.ShapeDtypeStruct((rows, half_tiles * tile), jnp.float32),
-        cost_estimate=pl.CostEstimate(
-            flops=rows * GROUP * HD * 2560 * 2, bytes_accessed=7 << 20, transcendentals=0
-        ),
-        name="own_outputs",
-    )(where, attended, out_weight)
-
-
-def join_kernel(where_ref, own_ref, rest_ref, out_ref):
-    half = own_ref.shape[1]
-    core = where_ref[4]
-    out_ref[:, pl.ds(pl.multiple_of(core * half, half), half)] = own_ref[...]
-    out_ref[:, pl.ds(pl.multiple_of((1 - core) * half, half), half)] = rest_ref[...]
-
-
-def join_halves(where, own, rest):
-    return pl.pallas_call(
-        join_kernel,
-        in_specs=[in_smem(), in_vmem(), in_vmem()],
-        out_specs=in_vmem(),
-        out_shape=jax.ShapeDtypeStruct((own.shape[0], 2 * own.shape[1]), own.dtype),
-        name="join_halves",
-    )(where, own, rest)
 
 
 def shards(
@@ -391,17 +293,34 @@
             axis=1,
         )
 
-    key_heads = attn_keys[0].reshape(BLOCK, KV, HD).transpose(1, 0, 2)
-    key_heads = jnp.broadcast_to(key_heads[:, None], (NX, NG, BLOCK, HD))
-    key_heads, *sent = together(key_heads, *[for_head((x + d) % NX) for d in range(NX)])
+    sent = [for_head((x + d) % NX) for d in range(NX)]
     blocks = [sent[0]] + [route(sent[d], along_x(d)) for d in range(1, NX)]
-    keys = exchange(key_heads.reshape(NX * NG, BLOCK, HD)).reshape(SLAB, HD)
+
+    def along_z(d):
+        return lambda x, z, y, t: (x, z + d, y, t)
+
+    def along_y(x, z, y, t):
+        return (x, z, y + 1, t)
+
+    key_heads = attn_keys[0].reshape(BLOCK, KV, HD)
+    own_part = jnp.stack(
+        [pick(key_heads, x, 1)]
+        + [route(pick(key_heads, (x + d) % NX, 1), along_x(d)) for d in range(1, NX)]
+    )
+    z_parts = [own_part] + [route(own_part, along_z(d)) for d in range(1, NZ)]
+    keys = [part for own in z_parts for part in (own, route(own, along_y))]
+
+    def owner(x, z, y, s, head):
+        return (x, s + 2 * (head // 2), y, head)
+
+    def near(x, z, y, t):
+        return owner(x, z, y, t, z ^ 1)
+
+    def far(x, z, y, t):
+        return owner(x, z, y, t, z ^ 3)
 
     def swap(x, z, y, t):
-        return (t + 2 * (x // 2), z, y, x)
-
-    def swap_and_flip(x, z, y, t):
-        return (t + 2 * ((x ^ 2) // 2), z, y, x ^ 2)
+        return owner(z, z, y, t, x)
 
     def flip_core(x, z, y, t):
         return (x, z, y, t ^ 1)
@@ -410,9 +329,8 @@
         return (x, z, y, t ^ 2)
 
     state = jnp.stack([master, first_moment, second_moment]).reshape(3, 40, KV, HD)
-    state, keys = together(state, keys)
-    own_rows, keys, *blocks = together(hidden[0], keys, *blocks)
-    hidden_parts = [route(own_rows, swap), None, route(own_rows, swap_and_flip), None]
+    own_rows = hidden[0]
+    hidden_parts = [None, route(own_rows, near), None, route(own_rows, far)]
 
     def over_tp(d):
         return lambda x, z, y, t: (x, z, y, t ^ d)
@@ -426,18 +344,18 @@
 
     old_weights, new_weights = decode_weights(dec_query, dec_key, cache_keys, cache_len)
 
-    where = jnp.stack([g, lengths[0, 0], x, t, t % 2]).astype(jnp.int32)
+    where = jnp.stack([g, lengths[0, 0], x, t]).astype(jnp.int32)
     where, by_row, old_weights, new_weights = together(where, by_row, old_weights, new_weights)
     old_master, old_first, old_second = by_row
     partial = attention_terms(where, blocks, keys)
 
     along_zy = [[a * NG + b for b in range(NG)] for a in range(NX)]
-    terms = exchange(partial.reshape(NG, NX * BLOCK, HD), along_zy)
-    terms, hidden_parts[0], hidden_parts[2] = together(terms, hidden_parts[0], hidden_parts[2])
-    dvalue = jnp.sum(terms.astype(f32), axis=0).astype(bf).reshape(NX, BLOCK, HD)
+    terms = exchange(partial.reshape(NG, NZ * BLOCK, HD), along_zy)
+    terms, hidden_parts[1], hidden_parts[3] = together(terms, hidden_parts[1], hidden_parts[3])
+    dvalue = jnp.sum(terms.astype(f32), axis=0).astype(bf).reshape(NZ, BLOCK, HD)
     dvalue = route(dvalue, swap)
-    hidden_parts[1] = route(hidden_parts[0], flip_core)
-    hidden_parts[3] = route(hidden_parts[2], flip_core)
+    hidden_parts[0] = route(hidden_parts[1], flip_core)
+    hidden_parts[2] = route(hidden_parts[3], flip_core)
     gradient = gradient_terms(where, dvalue, hidden_parts)
     terms = exchange(gradient.reshape(NX * NG, NT * 40, HD))
     gradient = jnp.sum(terms.astype(f32), axis=0)
@@ -449,9 +367,13 @@
     )
     cached = jnp.einsum(
         "srgc,rcd->srgd", old_weights, cache_values, preferred_element_type=f32
-    ).reshape(-1, GROUP * HD)
-    new_weights = new_weights.astype(f32).reshape(cached.shape[0], -1)
-    rounded, cached, new_weights = together(new_master.astype(bf), cached, new_weights)
+    )
+    core, half = t % 2, out_weight.shape[1] // 2
+    own_weight = lax.dynamic_slice_in_dim(out_weight, core * half, half, 1)
+    other_weight = lax.dynamic_slice_in_dim(out_weight, (1 - core) * half, half, 1)
+    rounded, cached, own_weight, other_weight = together(
+        new_master.astype(bf), cached, own_weight, other_weight
+    )
     rollout = exchange(jnp.broadcast_to(rounded[None], (NX * NG, NT * 40, HD))).reshape(5120, HD)
 
     news = jnp.stack([new_master, new_first, new_second]).reshape(3, NT, 40, HD)
@@ -465,19 +387,24 @@
 
     step_count, dec_rows = dec_hidden.shape[:2]
     rows = step_count * dec_rows
-    other, attended = decode_outputs(
-        where,
-        dec_hidden.reshape(rows, dec_hidden.shape[2]),
-        rollout,
-        cached,
-        new_weights,
-        out_weight,
-    )
-    received = route(other, flip_core)
-    on_chip = own_outputs(where, attended, out_weight) + received
+    fresh = jnp.dot(
+        dec_hidden.reshape(rows, dec_hidden.shape[2]), rollout, preferred_element_type=f32
+    )
+    fresh = fresh.reshape(step_count, dec_rows, HD).astype(bf).astype(f32)
+    attended = cached
+    for j in range(step_count):
+        attended = attended + new_weights[..., j : j + 1].astype(f32) * fresh[j][None, :, None, :]
+    attended = attended.astype(bf).reshape(rows, GROUP * HD)
+
+    received = route(jnp.dot(attended, other_weight, preferred_element_type=f32), flip_core)
+    (own_out,) = together(jnp.dot(attended, own_weight, preferred_element_type=f32))
+    on_chip = own_out + received
     both = (on_chip + route(on_chip.astype(bf), flip_chip).astype(f32)).astype(bf)
-    dec_out = join_halves(where, both, route(both, flip_core))
-    dec_out = dec_out.reshape(step_count, dec_rows, out_weight.shape[1])
+    rest = route(both, flip_core)
+    dec_out = jnp.zeros((rows, 2 * half), bf)
+    dec_out = lax.dynamic_update_slice_in_dim(dec_out, both, core * half, 1)
+    dec_out = lax.dynamic_update_slice_in_dim(dec_out, rest, (1 - core) * half, 1)
+    dec_out = dec_out.reshape(step_count, dec_rows, 2 * half)
     return (new_master, new_first, new_second, rollout, dec_out)
 
 

time: 246 us -> 221 us (0.90)
  blocking collectives: 24.2 us -> 0 us
  waiting for transfers between devices: 57.2 us -> 70 us
  Pallas kernels: 33.4 us -> 22.5 us
  starting transfers between devices: 81.1 us -> 72.4 us
  matrix products: 7.91 us -> 14.3 us
  other arithmetic: 14.9 us -> 12.3 us
    all_to_all x1 -> x0, blocking collectives: 24.2 us -> none  [exchange(): lax.all_to_all(value, 'ctx', split_axis=0, concat_axis=0, axis_index_grou...]
    all_to_all x3, starting transfers between devices: 40.2 us -> 24 us  [exchange(): lax.all_to_all(value, 'ctx', split_axis=0, concat_axis=0, axis_index_grou...]
    pallas_call x4 -> x1, Pallas kernels: 28.2 us -> 17.3 us  [attention_terms(): pl.pallas_call(attention_kernel, out_shape=jax.ShapeDtypeStruct((NX * NY,...]
    dynamic_slice x0 -> x1, local copies, waits for them, and re-layouts: none -> 8.74 us  [shards(): lax.dynamic_slice_in_dim(out_weight, (1 - core) * half, half, 1)]
    ppermute x17 -> x27, waiting for transfers between devices: 41.9 us -> 50.3 us  [route(): return lax.ppermute(value, ('ctx', 'tp'), pairs)]
    ppermute x17 -> x27, starting transfers between devices: 41 us -> 48.4 us  [route(): return lax.ppermute(value, ('ctx', 'tp'), pairs)]
    dot_general x0 -> x3, matrix products: none -> 5.99 us  [the longest x1 3.33 us: shards(): jnp.dot(attended, other_weight, preferred_element_type=f32)]
    all_to_all x3, waiting for transfers between devices: 15.3 us -> 19.7 us  [exchange(): lax.all_to_all(value, 'ctx', split_axis=0, concat_axis=0, axis_index_grou...]
  transfers between devices with their start and end apart: 20 -> 30, of which waited for: 6 -> 11; matrix products, arithmetic and copies ran while one was open for 11% -> 15% of each run, Pallas kernels for 9% -> 8%
where the time goes in v3:
time: 221 us; the launch traced here: 219 us
  starting transfers between devices  72.4 us (33%)
  waiting for transfers between devices  70 us (32%)
  local copies, waits for them, and re-layouts  25.8 us (12%)
  Pallas kernels  22.5 us (10%)
  matrix products  14.3 us (6%)
  other arithmetic  12.3 us (6%)
    ppermute x27, waiting for transfers between devices, route(): return lax.ppermute(value, ('ctx', 'tp'), pairs)  50.3 us
    ppermute x27, starting transfers between devices, route(): return lax.ppermute(value, ('ctx', 'tp'), pairs)  48.4 us
    all_to_all x3, starting transfers between devices, exchange(): lax.all_to_all(value, 'ctx', split_axis=0, concat_axis=0, axis_index_grou...  24 us
    all_to_all x3, waiting for transfers between devices, exchange(): lax.all_to_all(value, 'ctx', split_axis=0, concat_axis=0, axis_index_grou...  19.7 us
    pallas_call x1, Pallas kernels, attention_terms(): pl.pallas_call(attention_kernel, out_shape=jax.ShapeDtypeStruct((NX * NY,...  17.3 us
    unnamed x65, local copies, waits for them, and re-layouts  9.45 us
    dynamic_slice x1, local copies, waits for them, and re-layouts, shards(): lax.dynamic_slice_in_dim(out_weight, (1 - core) * half, half, 1)  8.74 us
    pallas_call x1, Pallas kernels, gradient_terms(): pl.pallas_call(gradient_kernel, grid=(width // tile,), out_shape=jax.Shap...  5.15 us
  transfers between devices with their start and end apart: 30, of which 11 were waited for; matrix products, arithmetic and copies ran while one was open for 15% of the time, Pallas kernels for 8%

profile of v3, /device:TPU:1, one launch (start us, length us, event | category | flops | bytes accessed | tf_op | source)
XLA Modules:
  0.0 218.6 jit_solution(13973783509781377679)
XLA Ops:
  0.7 1.0 reshape_squeeze.3
  2.1 2.1 collective-permute-start.6
  4.2 2.5 %collective-permute-start.7 = (bf16[128,128]{1,0:T(8,128)(2,1)S(1)}, bf16[128,128]{1,0:T(8,128)(2,1)S(1)}, u32[]{:S(2)}, u32[]{:S(2)}) collective-permute-start(bf16[128,128]{1,0:T(8,128)(2,1)S(1)} %bitcast.225), channel_id=1, source_target_pairs={{0,64},{1,65},{2,66},{3,67},{4,68},{5,69},{6,70},{7,71},{8,72},{9,... | collective-permute-start | bytes 98312 | tf_op jit(solution)/shard_map/ppermute | solution.py:39
  6.7 1.2 collective-permute-start.8
  7.8 0.9 stack.115
  8.8 0.9 stack.116
  9.7 0.9 stack.117
  11.5 2.7 %collective-permute-start.2 = (f32[3,40,128]{2,1,0:T(8,128)S(1)}, f32[3,40,128]{2,1,0:T(8,128)S(1)}, u32[]{:S(2)}, u32[]{:S(2)}) collective-permute-start(f32[3,40,128]{2,1,0:T(8,128)S(1)} %bitcast.221), channel_id=1, source_target_pairs={{0,3},{1,2},{2,1},{3,0},{4,7},{5,6},{6,5},{7,4},{8,11},{9,10},{10,... | collective-permute-start | bytes 184328 | tf_op jit(solution)/shard_map/ppermute | solution.py:39
  14.4 3.8 %fusion.5 = (f32[4,32,8]{2,0,1:T(4,128)S(1)}, f32[32,512,4,8]{1,3,2,0:T(8,128)S(1)}) fusion(pred[32,512]{1,0:T(8,128)(4,1)S(1)} %iota_compare_fusion, bf16[32,512,128]{2,1,0:T(8,128)(2,1)} %param.36, bf16[4,32,8,128]{3,2,1,0:T(8,128)(2,1)S(1)} %bitcast.196), kind=kOutput, calls=%fused_computation.9 | convolution fusion | flops 135789568 | bytes 6574080 | tf_op jit(solution)/shard_map/srgd,rcd->srgc/dot_general | solution.py:218
  18.2 1.3 select_reduce_fusion
  21.5 1.7 divide_convert_fusion
  26.7 1.7 collective-permute-start.10
  29.2 3.3 %collective-permute-start.12 = (bf16[4,128,128]{2,1,0:T(8,128)(2,1)S(1)}, bf16[4,128,128]{2,1,0:T(8,128)(2,1)}, u32[]{:S(2)}, u32[]{:S(2)}) collective-permute-start(bf16[4,128,128]{2,1,0:T(8,128)(2,1)S(1)} %pad_maximum_fusion.9.refs_4_), channel_id=1, source_target_pairs={{0,16},{1,17},{2,18},{3,19},{4,20},{5,21},{6,22},{7,23},{8,24},{9,... | collective-permute-start | bytes 393224 | tf_op jit(solution)/shard_map/ppermute | solution.py:39
  33.2 2.9 %collective-permute-start.9 = (bf16[4,128,128]{2,1,0:T(8,128)(2,1)S(1)}, bf16[4,128,128]{2,1,0:T(8,128)(2,1)S(1)}, u32[]{:S(2)}, u32[]{:S(2)}) collective-permute-start(bf16[4,128,128]{2,1,0:T(8,128)(2,1)S(1)} %pad_maximum_fusion.9.refs_4_), channel_id=1, source_target_pairs={{0,4},{1,5},{2,6},{3,7},{4,0},{5,1},{6,2},{7,3},{8,12},{9,13},{10,... | collective-permute-start | bytes 393224 | tf_op jit(solution)/shard_map/ppermute | solution.py:39
  37.4 2.2 collective-permute-start.4
  40.2 2.6 %collective-permute-start.13 = (bf16[4,128,128]{2,1,0:T(8,128)(2,1)}, bf16[4,128,128]{2,1,0:T(8,128)(2,1)}, u32[]{:S(2)}, u32[]{:S(2)}) collective-permute-start(bf16[4,128,128]{2,1,0:T(8,128)(2,1)} %collective-permute-done.12.refs_8_), channel_id=1, source_target_pairs={{0,4},{1,5},{2,6},{3,7},{4,0},{5,1},{6,2},{7,3},{8,12},{9,13},{10,... | collective-permute-start | bytes 393224 | tf_op jit(solution)/shard_map/ppermute | solution.py:39
  43.5 1.0 collective-permute-start.15
  44.5 1.5 collective-permute-done.13.refs_9_
  46.5 3.8 %collective-permute-done.15.refs_11_ = bf16[4,128,128]{2,1,0:T(8,128)(2,1)} collective-permute-done((bf16[4,128,128]{2,1,0:T(8,128)(2,1)}, bf16[4,128,128]{2,1,0:T(8,128)(2,1)}, u32[]{:S(2)}, u32[]{:S(2)}) %collective-permute-start.15) | collective-permute-done | bytes 131104 | tf_op jit(solution)/shard_map/ppermute | solution.py:39
  50.3 4.3 %collective-permute-start.17 = (bf16[128,5120]{1,0:T(8,128)(2,1)}, bf16[128,5120]{1,0:T(8,128)(2,1)}, u32[]{:S(2)}, u32[]{:S(2)}) collective-permute-start(bf16[128,5120]{1,0:T(8,128)(2,1)} %bitcast.234), channel_id=1, source_target_pairs={{0,19},{1,27},{2,3},{3,11},{4,23},{5,31},{6,7},{7,15},{8,18},{9,26... | collective-permute-start | bytes 3932168 | tf_op jit(solution)/shard_map/ppermute | solution.py:39
  54.7 0.9 pad_maximum_fusion.4
  56.4 7.9 %collective-permute-done.3.refs_1_ = bf16[128,2048]{1,0:T(8,128)(2,1)S(1)} collective-permute-done((bf16[128,2048]{1,0:T(8,128)(2,1)}, bf16[128,2048]{1,0:T(8,128)(2,1)S(1)}, u32[]{:S(2)}, u32[]{:S(2)}) %collective-permute-start.3) | collective-permute-done | bytes 524320 | tf_op jit(solution)/shard_map/ppermute | solution.py:39
  64.3 0.9 copy-done.2
  67.0 17.3 %attention_terms.1 = bf16[8,4,128,128]{3,2,1,0:T(8,128)(2,1)} custom-call(s32[4]{0:T(128)S(1)} %pad_add_fusion.where_ref, bf16[128,2048]{1,0:T(8,128)(2,1)S(1)} %pad_maximum_fusion.refs_0_, bf16[128,2048]{1,0:T(8,128)(2,1)S(1)} %collective-permute-done.3.refs_1_, bf16[128,2048]{1,0:T(8,128)(2,1)S(1)} %collective-permute-done.4.refs_2_, ...), custom_call_target="tpu_custom_call" | custom-call | flops 4096 | bytes 4096 | tf_op jit(solution)/shard_map/attention_terms/pallas_call | solution.py:164
  84.4 8.1 %all-to-all-start = ((bf16[8,512,128]{2,1,0:T(8,128)(2,1)}), bf16[8,512,128]{2,1,0:T(8,128)(2,1)S(1)}, u32[]{:S(2)}, u32[]{:S(2)}) async-start(bf16[8,512,128]{2,1,0:T(8,128)(2,1)} %bitcast.40), calls=%async_computation | async-start | bytes 2097152 | tf_op jit(solution)/shard_map/all_to_all | solution.py:271
  92.4 12.5 %all-to-all-done = bf16[8,512,128]{2,1,0:T(8,128)(2,1)S(1)} async-done(((bf16[8,512,128]{2,1,0:T(8,128)(2,1)}), bf16[8,512,128]{2,1,0:T(8,128)(2,1)S(1)}, u32[]{:S(2)}, u32[]{:S(2)}) %all-to-all-start) | async-done | bytes 1048608 | tf_op jit(solution)/shard_map/all_to_all | solution.py:271
  105.0 5.6 %collective-permute-start.19 = (bf16[128,5120]{1,0:T(8,128)(2,1)}, bf16[128,5120]{1,0:T(8,128)(2,1)}, u32[]{:S(2)}, u32[]{:S(2)}) collective-permute-start(bf16[128,5120]{1,0:T(8,128)(2,1)} %collective-permute-done.16.h1_ref), channel_id=1, source_target_pairs={{0,1},{1,0},{2,3},{3,2},{4,5},{5,4},{6,7},{7,6},{8,9},{9,8},{10,11... | collective-permute-start | bytes 3932168 | tf_op jit(solution)/shard_map/ppermute | solution.py:39
  110.7 1.9 collective-permute-start.18
  112.7 4.4 %collective-permute-done.18.dvalue_ref = bf16[4,128,128]{2,1,0:T(8,128)(2,1)S(1)} collective-permute-done((bf16[4,128,128]{2,1,0:T(8,128)(2,1)S(1)}, bf16[4,128,128]{2,1,0:T(8,128)(2,1)S(1)}, u32[]{:S(2)}, u32[]{:S(2)}) %collective-permute-start.18) | collective-permute-done | bytes 131104 | tf_op jit(solution)/shard_map/ppermute | solution.py:39
  117.7 5.2 %gradient_terms.1 = bf16[5120,128]{1,0:T(8,128)(2,1)} custom-call(s32[4]{0:T(128)} %copy-done.7, bf16[4,128,128]{2,1,0:T(8,128)(2,1)} %copy-done.14, bf16[128,5120]{1,0:T(8,128)(2,1)} %collective-permute-done.19.h0_ref, bf16[128,5120]{1,0:T(8,128)(2,1)} %collective-permute-done.16.h1_ref, bf16[128,5120]{1,0:T(8,128)(2,1)} %collective-permute-done.20.h2_ref, ...), custom_call_target="tpu_custom_call" | custom-call | flops 671088640 | bytes 7340032 | tf_op jit(solution)/shard_map/gradient_terms/pallas_call | solution.py:195
  122.8 10.2 %all-to-all-start.1 = ((bf16[32,160,128]{2,1,0:T(8,128)(2,1)}), bf16[32,160,128]{2,1,0:T(8,128)(2,1)S(1)}, u32[]{:S(2)}, u32[]{:S(2)}) async-start(bf16[32,160,128]{2,1,0:T(8,128)(2,1)} %bitcast.190), calls=%async_computation.1 | async-start | bytes 2621440 | tf_op jit(solution)/shard_map/all_to_all | solution.py:271
  133.0 8.7 %constant_dynamic-slice_fusion.4 = (bf16[1024,2560]{1,0:T(8,128)(2,1)}, bf16[1024,2560]{1,0:T(8,128)(2,1)}) fusion(bf16[1024,5120]{1,0:T(8,128)(2,1)} %param.39, s32[]{:T(128)S(6)} %select_n.146, s32[]{:T(128)S(6)} %select_n.145), kind=kLoop, calls=%fused_computation.93 | loop fusion | bytes 20971528 | tf_op jit(solution)/shard_map/dynamic_slice | solution.py:373
  141.8 3.2 %fusion.9 = f32[4,32,8,128]{3,2,0,1:T(8,128)S(1)} fusion(bf16[4,32,8,512]{3,2,0,1:T(8,128)(2,1)} %divide_convert_fusion, bf16[32,512,128]{2,1,0:T(8,128)(2,1)} %param.37), kind=kOutput, calls=%fused_computation.15 | convolution fusion | flops 134217728 | bytes 5767168 | tf_op jit(solution)/shard_map/srgc,rcd->srgd/dot_general | solution.py:368
  145.0 7.2 %all-to-all-done.1 = bf16[32,160,128]{2,1,0:T(8,128)(2,1)S(1)} async-done(((bf16[32,160,128]{2,1,0:T(8,128)(2,1)}), bf16[32,160,128]{2,1,0:T(8,128)(2,1)S(1)}, u32[]{:S(2)}, u32[]{:S(2)}) %all-to-all-start.1) | async-done | bytes 1310752 | tf_op jit(solution)/shard_map/all_to_all | solution.py:271
  152.4 1.2 broadcast_in_dim.85
  153.7 5.7 %all-to-all-start.2 = ((bf16[32,160,128]{2,1,0:T(8,128)(2,1)}), bf16[32,160,128]{2,1,0:T(8,128)(2,1)}, u32[]{:S(2)}, u32[]{:S(2)}) async-start(bf16[32,160,128]{2,1,0:T(8,128)(2,1)} %broadcast_in_dim.85), calls=%async_computation.2 | async-start | bytes 2621440 | tf_op jit(solution)/shard_map/all_to_all | solution.py:271
  159.5 2.7 %collective-permute-start.21 = (f32[3,40,128]{2,1,0:T(8,128)S(1)}, f32[3,40,128]{2,1,0:T(8,128)S(1)}, u32[]{:S(2)}, u32[]{:S(2)}) collective-permute-start(f32[3,40,128]{2,1,0:T(8,128)S(1)} %get-tuple-element.60), channel_id=1, source_target_pairs={{0,1},{1,0},{2,3},{3,2},{4,5},{5,4},{6,7},{7,6},{8,9},{9,8},{10,11... | collective-permute-start | bytes 184328 | tf_op jit(solution)/shard_map/ppermute | solution.py:39
  162.2 4.2 %collective-permute-start.22 = (f32[3,40,128]{2,1,0:T(8,128)S(1)}, f32[3,40,128]{2,1,0:T(8,128)S(1)}, u32[]{:S(2)}, u32[]{:S(2)}) collective-permute-start(f32[3,40,128]{2,1,0:T(8,128)S(1)} %get-tuple-element.59), channel_id=1, source_target_pairs={{0,2},{1,3},{2,0},{3,1},{4,6},{5,7},{6,4},{7,5},{8,10},{9,11},{10,... | collective-permute-start | bytes 184328 | tf_op jit(solution)/shard_map/ppermute | solution.py:39
  167.3 11.1 %collective-permute-done.22 = f32[3,40,128]{2,1,0:T(8,128)S(1)} collective-permute-done((f32[3,40,128]{2,1,0:T(8,128)S(1)}, f32[3,40,128]{2,1,0:T(8,128)S(1)}, u32[]{:S(2)}, u32[]{:S(2)}) %collective-permute-start.22) | collective-permute-done | bytes 61472 | tf_op jit(solution)/shard_map/ppermute | solution.py:39
  178.5 4.3 %collective-permute-done.23 = f32[3,40,128]{2,1,0:T(8,128)S(1)} collective-permute-done((f32[3,40,128]{2,1,0:T(8,128)S(1)}, f32[3,40,128]{2,1,0:T(8,128)S(1)}, u32[]{:S(2)}, u32[]{:S(2)}) %collective-permute-start.23) | collective-permute-done | bytes 61472 | tf_op jit(solution)/shard_map/ppermute | solution.py:39
  183.1 1.8 fusion.14
  184.9 1.6 add_convert_fusion.1
  186.6 3.3 %fusion.15 = f32[128,2560]{1,0:T(8,128)S(1)} fusion(bf16[1024,2560]{1,0:T(8,128)(2,1)} %get-tuple-element.30, bf16[16,8,8,128]{3,2,1,0:T(8,128)(2,1)S(1)} %bitcast.191), kind=kOutput, calls=%fused_computation.26 | convolution fusion | flops 671088640 | bytes 6815744 | tf_op jit(solution)/shard_map/dot_general | solution.py:399
  191.0 2.1 collective-permute-done.24
  193.3 4.6 %collective-permute-start.25 = (bf16[128,2560]{1,0:T(8,128)(2,1)S(1)}, bf16[128,2560]{1,0:T(8,128)(2,1)S(1)}, u32[]{:S(2)}, u32[]{:S(2)}) collective-permute-start(bf16[128,2560]{1,0:T(8,128)(2,1)S(1)} %get-tuple-element.35), channel_id=1, source_target_pairs={{0,2},{1,3},{2,0},{3,1},{4,6},{5,7},{6,4},{7,5},{8,10},{9,11},{10,... | collective-permute-start | bytes 1966088 | tf_op jit(solution)/shard_map/ppermute | solution.py:39
  197.8 14.8 %collective-permute-done.25 = bf16[128,2560]{1,0:T(8,128)(2,1)S(1)} collective-permute-done((bf16[128,2560]{1,0:T(8,128)(2,1)S(1)}, bf16[128,2560]{1,0:T(8,128)(2,1)S(1)}, u32[]{:S(2)}, u32[]{:S(2)}) %collective-permute-start.25) | collective-permute-done | bytes 655392 | tf_op jit(solution)/shard_map/ppermute | solution.py:39
  212.9 1.0 collective-permute-start.26
  215.7 2.9 %copy.108 = bf16[5120,128]{1,0:T(8,128)(2,1)} copy(bf16[5120,128]{1,0:T(8,128)(2,1)} %bitcast.48) | data formatting | bytes 2621440
  (146 shorter events, 19.6 us)
Async XLA Ops:
  0.6 182.5 %copy-start = (bf16[4,32,5120]{2,1,0:T(8,128)(2,1)S(1)}, bf16[4,32,5120]{2,1,0:T(8,128)(2,1)}, u32[]{:S(2)}) copy-start(bf16[4,32,5120]{2,1,0:T(8,128)(2,1)} %param.33) | copy-start | bytes 3932164
  0.6 13.6 %copy-start.19 = (s32[32]{0:T(128)S(1)}, s32[32]{0:T(128)}, u32[]{:S(2)}) copy-start(s32[32]{0:T(128)} %param.38) | copy-start | bytes 388
  0.7 13.7 %copy-start.13 = (bf16[4,32,1024]{2,1,0:T(8,128)(2,1)S(1)}, bf16[4,32,1024]{2,1,0:T(8,128)(2,1)}, u32[]{:S(2)}) copy-start(bf16[4,32,1024]{2,1,0:T(8,128)(2,1)} %param.34) | copy-start | bytes 786436
  2.1 24.3 %collective-permute-start.6 = (bf16[128,128]{1,0:T(8,128)(2,1)S(1)}, bf16[128,128]{1,0:T(8,128)(2,1)S(1)}, u32[]{:S(2)}, u32[]{:S(2)}) collective-permute-start(bf16[128,128]{1,0:T(8,128)(2,1)S(1)} %bitcast.226), channel_id=1, source_target_pairs={{0,32},{1,33},{2,34},{3,35},{4,36},{5,37},{6,38},{7,39},{8,40},{9,... | collective-permute-start | bytes 98312 | tf_op jit(solution)/shard_map/ppermute | solution.py:39
  4.2 22.4 %collective-permute-start.7 = (bf16[128,128]{1,0:T(8,128)(2,1)S(1)}, bf16[128,128]{1,0:T(8,128)(2,1)S(1)}, u32[]{:S(2)}, u32[]{:S(2)}) collective-permute-start(bf16[128,128]{1,0:T(8,128)(2,1)S(1)} %bitcast.225), channel_id=1, source_target_pairs={{0,64},{1,65},{2,66},{3,67},{4,68},{5,69},{6,70},{7,71},{8,72},{9,... | collective-permute-start | bytes 98312 | tf_op jit(solution)/shard_map/ppermute | solution.py:39
  6.7 19.9 %collective-permute-start.8 = (bf16[128,128]{1,0:T(8,128)(2,1)S(1)}, bf16[128,128]{1,0:T(8,128)(2,1)S(1)}, u32[]{:S(2)}, u32[]{:S(2)}) collective-permute-start(bf16[128,128]{1,0:T(8,128)(2,1)S(1)} %bitcast.227), channel_id=1, source_target_pairs={{0,96},{1,97},{2,98},{3,99},{4,100},{5,101},{6,102},{7,103},{8,104... | collective-permute-start | bytes 98312 | tf_op jit(solution)/shard_map/ppermute | solution.py:39
  11.5 21.0 %collective-permute-start.2 = (f32[3,40,128]{2,1,0:T(8,128)S(1)}, f32[3,40,128]{2,1,0:T(8,128)S(1)}, u32[]{:S(2)}, u32[]{:S(2)}) collective-permute-start(f32[3,40,128]{2,1,0:T(8,128)S(1)} %bitcast.221), channel_id=1, source_target_pairs={{0,3},{1,2},{2,1},{3,0},{4,7},{5,6},{6,5},{7,4},{8,11},{9,10},{10,... | collective-permute-start | bytes 184328 | tf_op jit(solution)/shard_map/ppermute | solution.py:39
  14.2 19.0 %collective-permute-start = (f32[3,40,128]{2,1,0:T(8,128)S(1)}, f32[3,40,128]{2,1,0:T(8,128)S(1)}, u32[]{:S(2)}, u32[]{:S(2)}) collective-permute-start(f32[3,40,128]{2,1,0:T(8,128)S(1)} %bitcast.220), channel_id=1, source_target_pairs={{0,1},{1,0},{2,3},{3,2},{4,5},{5,4},{6,7},{7,6},{8,9},{9,8},{10,11... | collective-permute-start | bytes 184328 | tf_op jit(solution)/shard_map/ppermute | solution.py:39
  14.4 3.8 %copy-start.24 = (bf16[4,32,128]{2,1,0:T(8,128)(2,1)S(1)}, bf16[4,32,128]{2,1,0:T(8,128)(2,1)}, u32[]{:S(2)}) copy-start(bf16[4,32,128]{2,1,0:T(8,128)(2,1)} %param.35) | copy-start | bytes 98308
  20.5 3.3 %copy-start.23 = (s32[1,2]{1,0:T(1,128)S(1)}, s32[1,2]{1,0:T(1,128)}, u32[]{:S(2)}) copy-start(s32[1,2]{1,0:T(1,128)} %param.27) | copy-start | bytes 28
  20.5 3.6 %copy-start.20 = (f32[1,128]{1,0:T(1,128)S(1)}, f32[1,128]{1,0:T(1,128)}, u32[]{:S(2)}) copy-start(f32[1,128]{1,0:T(1,128)} %param.26) | copy-start | bytes 1540
  20.6 3.6 %copy-start.21 = (f32[1,128]{1,0:T(1,128)S(1)}, f32[1,128]{1,0:T(1,128)}, u32[]{:S(2)}) copy-start(f32[1,128]{1,0:T(1,128)} %param.24) | copy-start | bytes 1540
  20.6 3.6 %copy-start.22 = (f32[1,128]{1,0:T(1,128)S(1)}, f32[1,128]{1,0:T(1,128)}, u32[]{:S(2)}) copy-start(f32[1,128]{1,0:T(1,128)} %param.25) | copy-start | bytes 1540
  20.6 3.6 %copy-start.11 = (bf16[1,128,4096]{2,1,0:T(8,128)(2,1)S(1)}, bf16[1,128,4096]{2,1,0:T(8,128)(2,1)}, u32[]{:S(2)}) copy-start(bf16[1,128,4096]{2,1,0:T(8,128)(2,1)} %param.23) | copy-start | bytes 3145732
  26.4 11.0 %collective-permute-start.1 = (f32[3,40,128]{2,1,0:T(8,128)S(1)}, f32[3,40,128]{2,1,0:T(8,128)}, u32[]{:S(2)}, u32[]{:S(2)}) collective-permute-start(f32[3,40,128]{2,1,0:T(8,128)S(1)} %bitcast.219), channel_id=1, source_target_pairs={{0,2},{1,3},{2,0},{3,1},{4,6},{5,7},{6,4},{7,5},{8,10},{9,11},{10,... | collective-permute-start | bytes 184328 | tf_op jit(solution)/shard_map/ppermute | solution.py:39
  26.7 9.5 %collective-permute-start.10 = (bf16[4,128,128]{2,1,0:T(8,128)(2,1)S(1)}, bf16[4,128,128]{2,1,0:T(8,128)(2,1)S(1)}, u32[]{:S(2)}, u32[]{:S(2)}) collective-permute-start(bf16[4,128,128]{2,1,0:T(8,128)(2,1)S(1)} %pad_maximum_fusion.9.refs_4_), channel_id=1, source_target_pairs={{0,8},{1,9},{2,10},{3,11},{4,12},{5,13},{6,14},{7,15},{8,16},{9,17... | collective-permute-start | bytes 393224 | tf_op jit(solution)/shard_map/ppermute | solution.py:39
  29.2 8.2 %collective-permute-start.12 = (bf16[4,128,128]{2,1,0:T(8,128)(2,1)S(1)}, bf16[4,128,128]{2,1,0:T(8,128)(2,1)}, u32[]{:S(2)}, u32[]{:S(2)}) collective-permute-start(bf16[4,128,128]{2,1,0:T(8,128)(2,1)S(1)} %pad_maximum_fusion.9.refs_4_), channel_id=1, source_target_pairs={{0,16},{1,17},{2,18},{3,19},{4,20},{5,21},{6,22},{7,23},{8,24},{9,... | collective-permute-start | bytes 393224 | tf_op jit(solution)/shard_map/ppermute | solution.py:39
  32.5 4.8 %copy-start.15 = (f32[3,40,128]{2,1,0:T(8,128)}, f32[3,40,128]{2,1,0:T(8,128)S(1)}, u32[]{:S(2)}) copy-start(f32[3,40,128]{2,1,0:T(8,128)S(1)} %collective-permute-done.2) | copy-start | bytes 184324
  32.5 7.0 %collective-permute-start.14 = (bf16[4,128,128]{2,1,0:T(8,128)(2,1)S(1)}, bf16[4,128,128]{2,1,0:T(8,128)(2,1)}, u32[]{:S(2)}, u32[]{:S(2)}) collective-permute-start(bf16[4,128,128]{2,1,0:T(8,128)(2,1)S(1)} %pad_maximum_fusion.9.refs_4_), channel_id=1, source_target_pairs={{0,24},{1,25},{2,26},{3,27},{4,28},{5,29},{6,30},{7,31},{8,0},{9,1... | collective-permute-start | bytes 393224 | tf_op jit(solution)/shard_map/ppermute | solution.py:39
  33.2 4.1 %copy-start.16 = (f32[3,40,128]{2,1,0:T(8,128)}, f32[3,40,128]{2,1,0:T(8,128)S(1)}, u32[]{:S(2)}) copy-start(f32[3,40,128]{2,1,0:T(8,128)S(1)} %collective-permute-done) | copy-start | bytes 184324
  33.2 6.3 %collective-permute-start.9 = (bf16[4,128,128]{2,1,0:T(8,128)(2,1)S(1)}, bf16[4,128,128]{2,1,0:T(8,128)(2,1)S(1)}, u32[]{:S(2)}, u32[]{:S(2)}) collective-permute-start(bf16[4,128,128]{2,1,0:T(8,128)(2,1)S(1)} %pad_maximum_fusion.9.refs_4_), channel_id=1, source_target_pairs={{0,4},{1,5},{2,6},{3,7},{4,0},{5,1},{6,2},{7,3},{8,12},{9,13},{10,... | collective-permute-start | bytes 393224 | tf_op jit(solution)/shard_map/ppermute | solution.py:39
  36.2 8.3 %copy-start.1 = (bf16[4,128,128]{2,1,0:T(8,128)(2,1)}, bf16[4,128,128]{2,1,0:T(8,128)(2,1)S(1)}, u32[]{:S(2)}) copy-start(bf16[4,128,128]{2,1,0:T(8,128)(2,1)S(1)} %collective-permute-done.10.refs_6_) | copy-start | bytes 393220
  36.2 6.7 %collective-permute-start.11 = (bf16[4,128,128]{2,1,0:T(8,128)(2,1)S(1)}, bf16[4,128,128]{2,1,0:T(8,128)(2,1)S(1)}, u32[]{:S(2)}, u32[]{:S(2)}) collective-permute-start(bf16[4,128,128]{2,1,0:T(8,128)(2,1)S(1)} %collective-permute-done.10.refs_6_), channel_id=1, source_target_pairs={{0,4},{1,5},{2,6},{3,7},{4,0},{5,1},{6,2},{7,3},{8,12},{9,13},{10,... | collective-permute-start | bytes 393224 | tf_op jit(solution)/shard_map/ppermute | solution.py:39
  37.3 19.1 %collective-permute-start.5 = (bf16[128,2048]{1,0:T(8,128)(2,1)}, bf16[128,2048]{1,0:T(8,128)(2,1)S(1)}, u32[]{:S(2)}, u32[]{:S(2)}) collective-permute-start(bf16[128,2048]{1,0:T(8,128)(2,1)} %pad_maximum_fusion.3), channel_id=1, source_target_pairs={{0,96},{1,97},{2,98},{3,99},{4,100},{5,101},{6,102},{7,103},{8,104... | collective-permute-start | bytes 1572872 | tf_op jit(solution)/shard_map/ppermute | solution.py:39
  37.4 19.1 %collective-permute-start.4 = (bf16[128,2048]{1,0:T(8,128)(2,1)}, bf16[128,2048]{1,0:T(8,128)(2,1)S(1)}, u32[]{:S(2)}, u32[]{:S(2)}) collective-permute-start(bf16[128,2048]{1,0:T(8,128)(2,1)} %pad_maximum_fusion.2), channel_id=1, source_target_pairs={{0,64},{1,65},{2,66},{3,67},{4,68},{5,69},{6,70},{7,71},{8,72},{9,... | collective-permute-start | bytes 1572872 | tf_op jit(solution)/shard_map/ppermute | solution.py:39
  39.5 24.8 %collective-permute-start.3 = (bf16[128,2048]{1,0:T(8,128)(2,1)}, bf16[128,2048]{1,0:T(8,128)(2,1)S(1)}, u32[]{:S(2)}, u32[]{:S(2)}) collective-permute-start(bf16[128,2048]{1,0:T(8,128)(2,1)} %pad_maximum_fusion.1), channel_id=1, source_target_pairs={{0,32},{1,33},{2,34},{3,35},{4,36},{5,37},{6,38},{7,39},{8,40},{9,... | collective-permute-start | bytes 1572872 | tf_op jit(solution)/shard_map/ppermute | solution.py:39
  40.2 5.8 %collective-permute-start.13 = (bf16[4,128,128]{2,1,0:T(8,128)(2,1)}, bf16[4,128,128]{2,1,0:T(8,128)(2,1)}, u32[]{:S(2)}, u32[]{:S(2)}) collective-permute-start(bf16[4,128,128]{2,1,0:T(8,128)(2,1)} %collective-permute-done.12.refs_8_), channel_id=1, source_target_pairs={{0,4},{1,5},{2,6},{3,7},{4,0},{5,1},{6,2},{7,3},{8,12},{9,13},{10,... | collective-permute-start | bytes 393224 | tf_op jit(solution)/shard_map/ppermute | solution.py:39
  43.5 6.9 %collective-permute-start.15 = (bf16[4,128,128]{2,1,0:T(8,128)(2,1)}, bf16[4,128,128]{2,1,0:T(8,128)(2,1)}, u32[]{:S(2)}, u32[]{:S(2)}) collective-permute-start(bf16[4,128,128]{2,1,0:T(8,128)(2,1)} %collective-permute-done.14.refs_10_), channel_id=1, source_target_pairs={{0,4},{1,5},{2,6},{3,7},{4,0},{5,1},{6,2},{7,3},{8,12},{9,13},{10,... | collective-permute-start | bytes 393224 | tf_op jit(solution)/shard_map/ppermute | solution.py:39
  46.0 46.4 %collective-permute-start.16 = (bf16[128,5120]{1,0:T(8,128)(2,1)}, bf16[128,5120]{1,0:T(8,128)(2,1)}, u32[]{:S(2)}, u32[]{:S(2)}) collective-permute-start(bf16[128,5120]{1,0:T(8,128)(2,1)} %bitcast.233), channel_id=1, source_target_pairs={{0,1},{1,9},{2,17},{3,25},{4,5},{5,13},{6,21},{7,29},{8,0},{9,8},{... | collective-permute-start | bytes 3932168 | tf_op jit(solution)/shard_map/ppermute | solution.py:39
  50.3 42.1 %collective-permute-start.17 = (bf16[128,5120]{1,0:T(8,128)(2,1)}, bf16[128,5120]{1,0:T(8,128)(2,1)}, u32[]{:S(2)}, u32[]{:S(2)}) collective-permute-start(bf16[128,5120]{1,0:T(8,128)(2,1)} %bitcast.234), channel_id=1, source_target_pairs={{0,19},{1,27},{2,3},{3,11},{4,23},{5,31},{6,7},{7,15},{8,18},{9,26... | collective-permute-start | bytes 3932168 | tf_op jit(solution)/shard_map/ppermute | solution.py:39
  54.7 29.6 %copy-start.7 = (s32[4]{0:T(128)}, s32[4]{0:T(128)S(1)}, u32[]{:S(2)}) copy-start(s32[4]{0:T(128)S(1)} %pad_add_fusion.where_ref) | copy-start | bytes 52
  84.4 20.6 %all-to-all-start = ((bf16[8,512,128]{2,1,0:T(8,128)(2,1)}), bf16[8,512,128]{2,1,0:T(8,128)(2,1)S(1)}, u32[]{:S(2)}, u32[]{:S(2)}) async-start(bf16[8,512,128]{2,1,0:T(8,128)(2,1)} %bitcast.40), calls=%async_computation | async-start | bytes 2097152 | tf_op jit(solution)/shard_map/all_to_all | solution.py:271
  105.0 12.1 %collective-permute-start.19 = (bf16[128,5120]{1,0:T(8,128)(2,1)}, bf16[128,5120]{1,0:T(8,128)(2,1)}, u32[]{:S(2)}, u32[]{:S(2)}) collective-permute-start(bf16[128,5120]{1,0:T(8,128)(2,1)} %collective-permute-done.16.h1_ref), channel_id=1, source_target_pairs={{0,1},{1,0},{2,3},{3,2},{4,5},{5,4},{6,7},{7,6},{8,9},{9,8},{10,11... | collective-permute-start | bytes 3932168 | tf_op jit(solution)/shard_map/ppermute | solution.py:39
  110.6 6.4 %collective-permute-start.20 = (bf16[128,5120]{1,0:T(8,128)(2,1)}, bf16[128,5120]{1,0:T(8,128)(2,1)}, u32[]{:S(2)}, u32[]{:S(2)}) collective-permute-start(bf16[128,5120]{1,0:T(8,128)(2,1)} %collective-permute-done.17.h3_ref), channel_id=1, source_target_pairs={{0,1},{1,0},{2,3},{3,2},{4,5},{5,4},{6,7},{7,6},{8,9},{9,8},{10,11... | collective-permute-start | bytes 3932168 | tf_op jit(solution)/shard_map/ppermute | solution.py:39
  110.7 6.3 %collective-permute-start.18 = (bf16[4,128,128]{2,1,0:T(8,128)(2,1)S(1)}, bf16[4,128,128]{2,1,0:T(8,128)(2,1)S(1)}, u32[]{:S(2)}, u32[]{:S(2)}) collective-permute-start(bf16[4,128,128]{2,1,0:T(8,128)(2,1)S(1)} %bitcast.214), channel_id=1, source_target_pairs={{0,0},{1,8},{2,16},{3,24},{4,4},{5,12},{6,20},{7,28},{8,32},{9,40}... | collective-permute-start | bytes 393224 | tf_op jit(solution)/shard_map/ppermute | solution.py:39
  122.8 29.3 %all-to-all-start.1 = ((bf16[32,160,128]{2,1,0:T(8,128)(2,1)}), bf16[32,160,128]{2,1,0:T(8,128)(2,1)S(1)}, u32[]{:S(2)}, u32[]{:S(2)}) async-start(bf16[32,160,128]{2,1,0:T(8,128)(2,1)} %bitcast.190), calls=%async_computation.1 | async-start | bytes 2621440 | tf_op jit(solution)/shard_map/all_to_all | solution.py:271
  141.8 10.6 %copy-start.8 = (f32[3,4,40,128]{3,2,1,0:T(8,128)S(1)}, f32[3,4,40,128]{3,2,1,0:T(8,128)}, u32[]{:S(2)}) copy-start(f32[3,4,40,128]{3,2,1,0:T(8,128)} %pad_maximum_fusion.5) | copy-start | bytes 737284
  153.7 12.8 %copy-start.10 = (bf16[4,32,8,4]{2,3,0,1:T(4,128)(2,1)S(1)}, bf16[4,32,8,4]{2,3,0,1:T(4,128)(2,1)}, u32[]{:S(2)}) copy-start(bf16[4,32,8,4]{2,3,0,1:T(4,128)(2,1)} %divide_convert_fusion.1) | copy-start | bytes 24580
  153.7 29.4 %all-to-all-start.2 = ((bf16[32,160,128]{2,1,0:T(8,128)(2,1)}), bf16[32,160,128]{2,1,0:T(8,128)(2,1)}, u32[]{:S(2)}, u32[]{:S(2)}) async-start(bf16[32,160,128]{2,1,0:T(8,128)(2,1)} %broadcast_in_dim.85), calls=%async_computation.2 | async-start | bytes 2621440 | tf_op jit(solution)/shard_map/all_to_all | solution.py:271
  159.4 30.7 %slice-start = ((s8[5242880]{0:T(1024)(128)(4,1)}), s8[1048576]{0:T(1024)(128)(4,1)S(1)}, s32[]{:S(2)}) async-start(s8[5242880]{0:T(1024)(128)(4,1)} %bitcast.188), calls=%async_computation.3 | async-start | bytes 2097152
  159.5 7.8 %collective-permute-start.21 = (f32[3,40,128]{2,1,0:T(8,128)S(1)}, f32[3,40,128]{2,1,0:T(8,128)S(1)}, u32[]{:S(2)}, u32[]{:S(2)}) collective-permute-start(f32[3,40,128]{2,1,0:T(8,128)S(1)} %get-tuple-element.60), channel_id=1, source_target_pairs={{0,1},{1,0},{2,3},{3,2},{4,5},{5,4},{6,7},{7,6},{8,9},{9,8},{10,11... | collective-permute-start | bytes 184328 | tf_op jit(solution)/shard_map/ppermute | solution.py:39
  162.2 16.2 %collective-permute-start.22 = (f32[3,40,128]{2,1,0:T(8,128)S(1)}, f32[3,40,128]{2,1,0:T(8,128)S(1)}, u32[]{:S(2)}, u32[]{:S(2)}) collective-permute-start(f32[3,40,128]{2,1,0:T(8,128)S(1)} %get-tuple-element.59), channel_id=1, source_target_pairs={{0,2},{1,3},{2,0},{3,1},{4,6},{5,7},{6,4},{7,5},{8,10},{9,11},{10,... | collective-permute-start | bytes 184328 | tf_op jit(solution)/shard_map/ppermute | solution.py:39
  166.4 16.3 %collective-permute-start.23 = (f32[3,40,128]{2,1,0:T(8,128)S(1)}, f32[3,40,128]{2,1,0:T(8,128)S(1)}, u32[]{:S(2)}, u32[]{:S(2)}) collective-permute-start(f32[3,40,128]{2,1,0:T(8,128)S(1)} %get-tuple-element.58), channel_id=1, source_target_pairs={{0,3},{1,2},{2,1},{3,0},{4,7},{5,6},{6,5},{7,4},{8,11},{9,10},{10,... | collective-permute-start | bytes 184328 | tf_op jit(solution)/shard_map/ppermute | solution.py:39
  184.9 5.2 %slice-start.1 = ((s8[5242880]{0:T(1024)(128)(4,1)}), s8[4194304]{0:T(1024)(128)(4,1)S(1)}, s32[]{:S(2)}) async-start(s8[5242880]{0:T(1024)(128)(4,1)} %bitcast.188), calls=%async_computation.4 | async-start | bytes 8388608
  190.0 3.1 %collective-permute-start.24 = (f32[128,2560]{1,0:T(8,128)S(1)}, f32[128,2560]{1,0:T(8,128)S(1)}, u32[]{:S(2)}, u32[]{:S(2)}) collective-permute-start(f32[128,2560]{1,0:T(8,128)S(1)} %fusion.15), channel_id=1, source_target_pairs={{0,1},{1,0},{2,3},{3,2},{4,5},{5,4},{6,7},{7,6},{8,9},{9,8},{10,11... | collective-permute-start | bytes 3932168 | tf_op jit(solution)/shard_map/ppermute | solution.py:39
  193.3 19.4 %collective-permute-start.25 = (bf16[128,2560]{1,0:T(8,128)(2,1)S(1)}, bf16[128,2560]{1,0:T(8,128)(2,1)S(1)}, u32[]{:S(2)}, u32[]{:S(2)}) collective-permute-start(bf16[128,2560]{1,0:T(8,128)(2,1)S(1)} %get-tuple-element.35), channel_id=1, source_target_pairs={{0,2},{1,3},{2,0},{3,1},{4,6},{5,7},{6,4},{7,5},{8,10},{9,11},{10,... | collective-permute-start | bytes 1966088 | tf_op jit(solution)/shard_map/ppermute | solution.py:39
  212.9 2.7 %collective-permute-start.26 = (bf16[128,2560]{1,0:T(8,128)(2,1)S(1)}, bf16[128,2560]{1,0:T(8,128)(2,1)S(1)}, u32[]{:S(2)}, u32[]{:S(2)}) collective-permute-start(bf16[128,2560]{1,0:T(8,128)(2,1)S(1)} %get-tuple-element.34), channel_id=1, source_target_pairs={{0,1},{1,0},{2,3},{3,2},{4,5},{5,4},{6,7},{7,6},{8,9},{9,8},{10,11... | collective-permute-start | bytes 1966088 | tf_op jit(solution)/shard_map/ppermute | solution.py:39
  215.7 2.9 %copy-start.9 = (bf16[128,5120]{1,0:T(8,128)(2,1)}, bf16[128,5120]{1,0:T(8,128)(2,1)S(1)}, u32[]{:S(2)}) copy-start(bf16[128,5120]{1,0:T(8,128)(2,1)S(1)} %constant_dynamic-update-slice_fusion) | copy-start | bytes 3932164
  (9 other events, 11.3 us)

commit v4 on v3

--- a/solution.py
+++ b/solution.py
@@ -81,7 +81,7 @@
 
 def attention_kernel(where_ref, *refs):
     block_refs, key_refs, refs = refs[:NX], refs[NX : NX + NG], refs[NX + NG :]
-    out_ref, keys_ref, query_rows, dout_rows, scores, sums = refs
+    out_ref, keys_ref, query_columns, dout_rows, scores, sums, powers_sum = refs
     g, bound, own = where_ref[0], where_ref[1], where_ref[2]
     for dz in range(NZ):
         for dy in range(NY):
@@ -94,52 +94,87 @@
     for slot in range(NX):
         for h in range(GROUP):
             rows = pl.ds(h * BLOCK, BLOCK)
-            query_rows[slot, rows, :] = block_refs[slot][:, pl.ds(h * HD, HD)]
+            query_columns[slot, :, rows] = block_refs[slot][:, pl.ds(h * HD, HD)].T
             dout_rows[slot, rows, :] = block_refs[slot][:, pl.ds((GROUP + h) * HD, HD)]
     sums[...] = jnp.zeros_like(sums)
+
+    def key_norm(i, longest):
+        rows = pl.ds(pl.multiple_of(i * CHUNK, CHUNK), CHUNK)
+        block = keys_ref[rows, :].astype(jnp.float32)
+        norms = jnp.sum(block * block, axis=1, keepdims=True)
+        return jnp.maximum(longest, jnp.max(norms, axis=0, keepdims=True))
+
+    longest_key = lax.fori_loop(0, SLAB // CHUNK, key_norm, jnp.zeros((1, 1), jnp.float32))
 
     def one_block(slot, _):
         block_start = (lax.rem(own - slot + NX, NX) * NG + g) * BLOCK
         latest_from = jnp.where(block_start + BLOCK - 1 >= bound, bound, 0)
         first = jnp.where(block_start >= bound, bound, 0) // CHUNK
         stop = (block_start + BLOCK - 1) // CHUNK + 1
-        block_queries, block_douts = query_rows[slot], dout_rows[slot]
-
-        def scored(chunk, row_max):
+        block_queries, block_douts = query_columns[slot], dout_rows[slot]
+
+        def scored(rows):
+            return jnp.dot(keys_ref[rows, :], block_queries, preferred_element_type=jnp.float32)
+
+        def is_visible(start):
+            key_at = start + lax.broadcasted_iota(jnp.int32, (CHUNK, ROWS), 0)
+            query_at = block_start + (lax.broadcasted_iota(jnp.int32, (1, ROWS), 1) & (BLOCK - 1))
+            from_at = jnp.where(query_at >= bound, bound, 0)
+            return (key_at <= query_at) & (key_at >= from_at)
+
+        def by_tile(value):
+            return value.reshape(CHUNK // 8, 8, ROWS)
+
+        def add_powers(rows, powers):
+            scores[rows, :] = powers
+            powers_sum[...] += jnp.sum(by_tile(powers), axis=0)
+
+        as_float = block_queries.astype(jnp.float32)
+        norms = jnp.sum(as_float * as_float, axis=0, keepdims=True)
+        limit = jnp.sqrt(norms * longest_key) * (1.001 * exp2_scale)
+        powers_sum[...] = jnp.zeros_like(powers_sum)
+
+        def from_limit(chunk, _):
             start = pl.multiple_of(chunk * CHUNK, CHUNK)
             rows = pl.ds(start, CHUNK)
-            scores[rows, :] = lax.dot_general(
-                keys_ref[rows, :],
-                block_queries,
-                (((1,), (1,)), ((), ())),
-                preferred_element_type=jnp.float32,
-            )
             whole = (start + CHUNK - 1 <= block_start) & (start >= latest_from)
+
+            @pl.when(whole)
+            def _():
+                add_powers(rows, jnp.exp2(scored(rows) * exp2_scale - limit))
 
             @pl.when(jnp.logical_not(whole))
             def _():
-                key_at = start + lax.broadcasted_iota(jnp.int32, (CHUNK, ROWS), 0)
-                query_at = block_start + (
-                    lax.broadcasted_iota(jnp.int32, (1, ROWS), 1) & (BLOCK - 1)
-                )
-                from_at = jnp.where(query_at >= bound, bound, 0)
-                visible = (key_at <= query_at) & (key_at >= from_at)
-                scores[rows, :] = jnp.where(visible, scores[rows, :], LOWEST)
-
-            by_tile = scores[rows, :].reshape(CHUNK // 8, 8, ROWS)
-            return jnp.maximum(row_max, jnp.max(by_tile, axis=0))
-
-        row_max = lax.fori_loop(first, stop, scored, jnp.full((8, ROWS), LOWEST, jnp.float32))
-        row_max = jnp.max(row_max, axis=0, keepdims=True) * exp2_scale
-
-        def summed(chunk, row_sum):
-            rows = pl.ds(pl.multiple_of(chunk * CHUNK, CHUNK), CHUNK)
-            powers = jnp.exp2(scores[rows, :] * exp2_scale - row_max)
-            scores[rows, :] = powers
-            return row_sum + jnp.sum(powers.reshape(CHUNK // 8, 8, ROWS), axis=0)
-
-        row_sum = lax.fori_loop(first, stop, summed, jnp.zeros((8, ROWS), jnp.float32))
-        inverse = 1.0 / jnp.sum(row_sum, axis=0, keepdims=True)
+                powers = jnp.exp2(scored(rows) * exp2_scale - limit)
+                add_powers(rows, jnp.where(is_visible(start), powers, 0.0))
+
+            return 0
+
+        lax.fori_loop(first, stop, from_limit, 0)
+
+        total = jnp.sum(powers_sum[...], axis=0, keepdims=True)
+        kept = jnp.min(jnp.where(total >= 2.0**-60, 1.0, 0.0))
+
+        @pl.when(kept < 0.5)
+        def _():
+            def masked(chunk, row_max):
+                start = pl.multiple_of(chunk * CHUNK, CHUNK)
+                rows = pl.ds(start, CHUNK)
+                scores[rows, :] = jnp.where(is_visible(start), scored(rows), LOWEST)
+                return jnp.maximum(row_max, jnp.max(by_tile(scores[rows, :]), axis=0))
+
+            row_max = lax.fori_loop(first, stop, masked, jnp.full((8, ROWS), LOWEST, jnp.float32))
+            row_max = jnp.max(row_max, axis=0, keepdims=True) * exp2_scale
+            powers_sum[...] = jnp.zeros_like(powers_sum)
+
+            def from_maximum(chunk, _):
+                rows = pl.ds(pl.multiple_of(chunk * CHUNK, CHUNK), CHUNK)
+                add_powers(rows, jnp.exp2(scores[rows, :] * exp2_scale - row_max))
+                return 0
+
+            lax.fori_loop(first, stop, from_maximum, 0)
+
+        inverse = 1.0 / jnp.sum(powers_sum[...], axis=0, keepdims=True)
 
         def added(chunk, _):
             rows = pl.ds(pl.multiple_of(chunk * CHUNK, CHUNK), CHUNK)
@@ -168,10 +203,11 @@
         out_specs=in_vmem(),
         scratch_shapes=[
             pltpu.VMEM((SLAB, HD), jnp.bfloat16),
-            pltpu.VMEM((NX, ROWS, HD), jnp.bfloat16),
+            pltpu.VMEM((NX, HD, ROWS), jnp.bfloat16),
             pltpu.VMEM((NX, ROWS, HD), jnp.bfloat16),
             pltpu.VMEM((SLAB, ROWS), jnp.float32),
             pltpu.VMEM((SLAB, HD), jnp.float32),
+            pltpu.VMEM((8, ROWS), jnp.float32),
         ],
         compiler_params=pltpu.CompilerParams(vmem_limit_bytes=48 * 1024 * 1024),
         cost_estimate=pl.CostEstimate(
@@ -207,6 +243,25 @@
         ),
         name="gradient_terms",
     )(where, dvalue, *hidden_parts)
+
+
+def copy_kernel(from_ref, to_ref):
+    to_ref[...] = from_ref[...]
+
+
+def copied(value):
+    tile = pl.BlockSpec((value.shape[0] // 4, value.shape[1]), lambda i: (i, 0))
+    return pl.pallas_call(
+        copy_kernel,
+        grid=(4,),
+        in_specs=[tile],
+        out_specs=tile,
+        out_shape=jax.ShapeDtypeStruct(value.shape, value.dtype),
+        cost_estimate=pl.CostEstimate(
+            flops=0, bytes_accessed=4 * value.size, transcendentals=0
+        ),
+        name="copied",
+    )(value)
 
 
 def decode_weights(dec_query, dec_key, cache_keys, cache_len):
@@ -294,8 +349,6 @@
         )
 
     sent = [for_head((x + d) % NX) for d in range(NX)]
-    blocks = [sent[0]] + [route(sent[d], along_x(d)) for d in range(1, NX)]
-
     def along_z(d):
         return lambda x, z, y, t: (x, z + d, y, t)
 
@@ -307,6 +360,7 @@
         [pick(key_heads, x, 1)]
         + [route(pick(key_heads, (x + d) % NX, 1), along_x(d)) for d in range(1, NX)]
     )
+    blocks = [sent[0]] + [route(sent[d], along_x(d)) for d in range(1, NX)]
     z_parts = [own_part] + [route(own_part, along_z(d)) for d in range(1, NZ)]
     keys = [part for own in z_parts for part in (own, route(own, along_y))]
 
@@ -328,9 +382,14 @@
     def flip_chip(x, z, y, t):
         return (x, z, y, t ^ 2)
 
-    state = jnp.stack([master, first_moment, second_moment]).reshape(3, 40, KV, HD)
     own_rows = hidden[0]
     hidden_parts = [None, route(own_rows, near), None, route(own_rows, far)]
+
+    where = jnp.stack([g, lengths[0, 0], x, t]).astype(jnp.int32)
+    partial = attention_terms(where, blocks, keys)
+    partial, dec_query, *state = together(partial, dec_query, master, first_moment, second_moment)
+
+    state = jnp.stack(state).reshape(3, 40, KV, HD)
 
     def over_tp(d):
         return lambda x, z, y, t: (x, z, y, t ^ d)
@@ -344,19 +403,18 @@
 
     old_weights, new_weights = decode_weights(dec_query, dec_key, cache_keys, cache_len)
 
-    where = jnp.stack([g, lengths[0, 0], x, t]).astype(jnp.int32)
-    where, by_row, old_weights, new_weights = together(where, by_row, old_weights, new_weights)
-    old_master, old_first, old_second = by_row
-    partial = attention_terms(where, blocks, keys)
-
     along_zy = [[a * NG + b for b in range(NG)] for a in range(NX)]
     terms = exchange(partial.reshape(NG, NZ * BLOCK, HD), along_zy)
-    terms, hidden_parts[1], hidden_parts[3] = together(terms, hidden_parts[1], hidden_parts[3])
+    terms, hidden_parts[1], hidden_parts[3], by_row, old_weights, new_weights = together(
+        terms, hidden_parts[1], hidden_parts[3], by_row, old_weights, new_weights
+    )
+    old_master, old_first, old_second = by_row
     dvalue = jnp.sum(terms.astype(f32), axis=0).astype(bf).reshape(NZ, BLOCK, HD)
     dvalue = route(dvalue, swap)
     hidden_parts[0] = route(hidden_parts[1], flip_core)
     hidden_parts[2] = route(hidden_parts[3], flip_core)
     gradient = gradient_terms(where, dvalue, hidden_parts)
+    gradient, out_weight, old_weights = together(gradient, out_weight, old_weights)
     terms = exchange(gradient.reshape(NX * NG, NT * 40, HD))
     gradient = jnp.sum(terms.astype(f32), axis=0)
 
@@ -399,7 +457,8 @@
     received = route(jnp.dot(attended, other_weight, preferred_element_type=f32), flip_core)
     (own_out,) = together(jnp.dot(attended, own_weight, preferred_element_type=f32))
     on_chip = own_out + received
-    both = (on_chip + route(on_chip.astype(bf), flip_chip).astype(f32)).astype(bf)
+    from_chip, rollout = together(route(on_chip.astype(bf), flip_chip), copied(rollout))
+    both = (on_chip + from_chip.astype(f32)).astype(bf)
     rest = route(both, flip_core)
     dec_out = jnp.zeros((rows, 2 * half), bf)
     dec_out = lax.dynamic_update_slice_in_dim(dec_out, both, core * half, 1)

time: 221 us -> 221 us (level)
  waiting for transfers between devices: 70 us -> 53.3 us
  Pallas kernels: 22.5 us -> 31.6 us
  starting transfers between devices: 72.4 us -> 78.2 us
  other arithmetic: 12.3 us -> 15.7 us
    ppermute x27, waiting for transfers between devices: 50.3 us -> 38 us  [route(): return lax.ppermute(value, ('ctx', 'tp'), pairs)]
    all_to_all x3, starting transfers between devices: 24 us -> 29.8 us  [exchange(): lax.all_to_all(value, 'ctx', split_axis=0, concat_axis=0, axis_index_grou...]
    pallas_call x1, Pallas kernels: 17.3 us -> 23 us  [attention_terms(): pl.pallas_call(attention_kernel, out_shape=jax.ShapeDtypeStruct((NX * NY,...]
    all_to_all x3, waiting for transfers between devices: 19.7 us -> 15.3 us  [exchange(): lax.all_to_all(value, 'ctx', split_axis=0, concat_axis=0, axis_index_grou...]
    pallas_call x0 -> x1, Pallas kernels: none -> 3.46 us  [copied(): pl.pallas_call(copy_kernel, grid=(4,), in_specs=[tile], out_specs=tile, o...]
    unnamed x65 -> x52, local copies, waits for them, and re-layouts: 9.45 us -> 8.66 us
  transfers between devices with their start and end apart: 30 -> 30, of which waited for: 11 -> 13; matrix products, arithmetic and copies ran while one was open for 15% -> 17% of each run, Pallas kernels for 8% -> 12%
where the time goes in v4:
time: 221 us; the launch traced here: 219 us
  starting transfers between devices  78.2 us (35%)
  waiting for transfers between devices  53.3 us (24%)
  Pallas kernels  31.6 us (14%)
  local copies, waits for them, and re-layouts  24.5 us (11%)
  other arithmetic  15.7 us (7%)
  matrix products  14.2 us (6%)
    ppermute x27, starting transfers between devices, route(): return lax.ppermute(value, ('ctx', 'tp'), pairs)  48.4 us
    ppermute x27, waiting for transfers between devices, route(): return lax.ppermute(value, ('ctx', 'tp'), pairs)  38 us
    all_to_all x3, starting transfers between devices, exchange(): lax.all_to_all(value, 'ctx', split_axis=0, concat_axis=0, axis_index_grou...  29.8 us
    pallas_call x1, Pallas kernels, attention_terms(): pl.pallas_call(attention_kernel, out_shape=jax.ShapeDtypeStruct((NX * NY,...  23 us
    all_to_all x3, waiting for transfers between devices, exchange(): lax.all_to_all(value, 'ctx', split_axis=0, concat_axis=0, axis_index_grou...  15.3 us
    dynamic_slice x1, local copies, waits for them, and re-layouts, shards(): lax.dynamic_slice_in_dim(out_weight, (1 - core) * half, half, 1)  8.78 us
    unnamed x52, local copies, waits for them, and re-layouts  8.66 us
    pallas_call x1, Pallas kernels, gradient_terms(): pl.pallas_call(gradient_kernel, grid=(width // tile,), out_shape=jax.Shap...  5.15 us
  transfers between devices with their start and end apart: 30, of which 13 were waited for; matrix products, arithmetic and copies ran while one was open for 17% of the time, Pallas kernels for 12%

profile of v4, /device:TPU:1, one launch (start us, length us, event | category | flops | bytes accessed | tf_op | source)
XLA Modules:
  0.0 218.9 jit_solution(9339900595478713335)
XLA Ops:
  0.7 1.1 reshape_squeeze.3
  2.1 2.1 collective-permute-start.3
  4.3 2.5 %collective-permute-start.4 = (bf16[128,128]{1,0:T(8,128)(2,1)S(1)}, bf16[128,128]{1,0:T(8,128)(2,1)S(1)}, u32[]{:S(2)}, u32[]{:S(2)}) collective-permute-start(bf16[128,128]{1,0:T(8,128)(2,1)S(1)} %bitcast.226), channel_id=1, source_target_pairs={{0,64},{1,65},{2,66},{3,67},{4,68},{5,69},{6,70},{7,71},{8,72},{9,... | collective-permute-start | bytes 98312 | tf_op jit(solution)/shard_map/ppermute | solution.py:39
  6.7 1.2 collective-permute-start.5
  11.6 1.5 fusion.4
  15.0 2.0 collective-permute-start.1
  17.1 3.7 %collective-permute-start.9 = (bf16[4,128,128]{2,1,0:T(8,128)(2,1)S(1)}, bf16[4,128,128]{2,1,0:T(8,128)(2,1)S(1)}, u32[]{:S(2)}, u32[]{:S(2)}) collective-permute-start(bf16[4,128,128]{2,1,0:T(8,128)(2,1)S(1)} %pad_maximum_fusion.9.refs_4_), channel_id=1, source_target_pairs={{0,16},{1,17},{2,18},{3,19},{4,20},{5,21},{6,22},{7,23},{8,24},{9,... | collective-permute-start | bytes 393224 | tf_op jit(solution)/shard_map/ppermute | solution.py:39
  22.1 1.4 collective-permute-done.9.refs_8_
  23.4 1.0 collective-permute-start.7
  24.5 1.7 collective-permute-done.11.refs_10_
  26.2 2.9 %collective-permute-start.6 = (bf16[4,128,128]{2,1,0:T(8,128)(2,1)S(1)}, bf16[4,128,128]{2,1,0:T(8,128)(2,1)S(1)}, u32[]{:S(2)}, u32[]{:S(2)}) collective-permute-start(bf16[4,128,128]{2,1,0:T(8,128)(2,1)S(1)} %pad_maximum_fusion.9.refs_4_), channel_id=1, source_target_pairs={{0,4},{1,5},{2,6},{3,7},{4,0},{5,1},{6,2},{7,3},{8,12},{9,13},{10,... | collective-permute-start | bytes 393224 | tf_op jit(solution)/shard_map/ppermute | solution.py:39
  29.2 2.9 %collective-permute-start.10 = (bf16[4,128,128]{2,1,0:T(8,128)(2,1)S(1)}, bf16[4,128,128]{2,1,0:T(8,128)(2,1)S(1)}, u32[]{:S(2)}, u32[]{:S(2)}) collective-permute-start(bf16[4,128,128]{2,1,0:T(8,128)(2,1)S(1)} %collective-permute-done.9.refs_8_), channel_id=1, source_target_pairs={{0,4},{1,5},{2,6},{3,7},{4,0},{5,1},{6,2},{7,3},{8,12},{9,13},{10,... | collective-permute-start | bytes 393224 | tf_op jit(solution)/shard_map/ppermute | solution.py:39
  32.9 2.6 %collective-permute-start.12 = (bf16[4,128,128]{2,1,0:T(8,128)(2,1)}, bf16[4,128,128]{2,1,0:T(8,128)(2,1)}, u32[]{:S(2)}, u32[]{:S(2)}) collective-permute-start(bf16[4,128,128]{2,1,0:T(8,128)(2,1)} %collective-permute-done.11.refs_10_), channel_id=1, source_target_pairs={{0,4},{1,5},{2,6},{3,7},{4,0},{5,1},{6,2},{7,3},{8,12},{9,13},{10,... | collective-permute-start | bytes 393224 | tf_op jit(solution)/shard_map/ppermute | solution.py:39
  36.6 2.9 %collective-permute-start.8 = (bf16[4,128,128]{2,1,0:T(8,128)(2,1)}, bf16[4,128,128]{2,1,0:T(8,128)(2,1)}, u32[]{:S(2)}, u32[]{:S(2)}) collective-permute-start(bf16[4,128,128]{2,1,0:T(8,128)(2,1)} %collective-permute-done.7.refs_6_), channel_id=1, source_target_pairs={{0,4},{1,5},{2,6},{3,7},{4,0},{5,1},{6,2},{7,3},{8,12},{9,13},{10,... | collective-permute-start | bytes 393224 | tf_op jit(solution)/shard_map/ppermute | solution.py:39
  40.9 1.9 collective-permute-done.8.refs_7_
  42.8 5.6 %collective-permute-start.14 = (bf16[128,5120]{1,0:T(8,128)(2,1)}, bf16[128,5120]{1,0:T(8,128)(2,1)}, u32[]{:S(2)}, u32[]{:S(2)}) collective-permute-start(bf16[128,5120]{1,0:T(8,128)(2,1)} %bitcast.234), channel_id=1, source_target_pairs={{0,19},{1,27},{2,3},{3,11},{4,23},{5,31},{6,7},{7,15},{8,18},{9,26... | collective-permute-start | bytes 3932168 | tf_op jit(solution)/shard_map/ppermute | solution.py:39
  51.1 23.0 %attention_terms.1 = bf16[8,4,128,128]{3,2,1,0:T(8,128)(2,1)} custom-call(s32[4]{0:T(128)S(1)} %pad_add_fusion.where_ref, bf16[128,2048]{1,0:T(8,128)(2,1)S(1)} %pad_maximum_fusion.refs_0_, bf16[128,2048]{1,0:T(8,128)(2,1)S(1)} %collective-permute-done.refs_1_, bf16[128,2048]{1,0:T(8,128)(2,1)S(1)} %collective-permute-done.1.refs_2_, ...), custom_call_target="tpu_custom_call" | custom-call | flops 4096 | bytes 4096 | tf_op jit(solution)/shard_map/attention_terms/pallas_call | solution.py:199
  77.2 3.0 %collective-permute-start.15 = (f32[3,40,128]{2,1,0:T(8,128)S(1)}, f32[3,40,128]{2,1,0:T(8,128)S(1)}, u32[]{:S(2)}, u32[]{:S(2)}) collective-permute-start(f32[3,40,128]{2,1,0:T(8,128)S(1)} %bitcast.221), channel_id=1, source_target_pairs={{0,1},{1,0},{2,3},{3,2},{4,5},{5,4},{6,7},{7,6},{8,9},{9,8},{10,11... | collective-permute-start | bytes 184328 | tf_op jit(solution)/shard_map/ppermute | solution.py:39
  80.2 1.7 collective-permute-start.17
  81.9 14.5 %all-to-all-start = ((bf16[8,512,128]{2,1,0:T(8,128)(2,1)}), bf16[8,512,128]{2,1,0:T(8,128)(2,1)S(1)}, u32[]{:S(2)}, u32[]{:S(2)}) async-start(bf16[8,512,128]{2,1,0:T(8,128)(2,1)} %bitcast.21), calls=%async_computation | async-start | bytes 2097152 | tf_op jit(solution)/shard_map/all_to_all | solution.py:326
  96.4 3.7 %fusion.5 = (f32[4,32,8]{2,0,1:T(4,128)S(1)}, f32[32,4,8,512]{3,2,1,0:T(8,128)S(1)}) fusion(pred[32,512]{1,0:T(8,128)(4,1)S(1)} %iota_compare_fusion, bf16[32,512,128]{2,1,0:T(8,128)(2,1)} %param.36, bf16[4,32,8,128]{3,2,1,0:T(8,128)(2,1)S(1)} %bitcast.196), kind=kOutput, calls=%fused_computation.9 | convolution fusion | flops 135789568 | bytes 6574080 | tf_op jit(solution)/shard_map/srgd,rcd->srgc/dot_general | solution.py:273
  100.2 1.3 select_reduce_fusion
  102.5 1.6 divide_convert_fusion
  105.3 7.9 %all-to-all-done = bf16[8,512,128]{2,1,0:T(8,128)(2,1)S(1)} async-done(((bf16[8,512,128]{2,1,0:T(8,128)(2,1)}), bf16[8,512,128]{2,1,0:T(8,128)(2,1)S(1)}, u32[]{:S(2)}, u32[]{:S(2)}) %all-to-all-start) | async-done | bytes 1048608 | tf_op jit(solution)/shard_map/all_to_all | solution.py:326
  113.2 1.3 collective-permute-start.19
  114.7 1.9 collective-permute-start.18
  116.6 4.5 %collective-permute-done.18.dvalue_ref = bf16[4,128,128]{2,1,0:T(8,128)(2,1)S(1)} collective-permute-done((bf16[4,128,128]{2,1,0:T(8,128)(2,1)S(1)}, bf16[4,128,128]{2,1,0:T(8,128)(2,1)S(1)}, u32[]{:S(2)}, u32[]{:S(2)}) %collective-permute-start.18) | collective-permute-done | bytes 131104 | tf_op jit(solution)/shard_map/ppermute | solution.py:39
  121.8 5.2 %gradient_terms.1 = bf16[5120,128]{1,0:T(8,128)(2,1)} custom-call(s32[4]{0:T(128)} %copy-done.7, bf16[4,128,128]{2,1,0:T(8,128)(2,1)} %copy-done.15, bf16[128,5120]{1,0:T(8,128)(2,1)} %collective-permute-done.19.h0_ref, bf16[128,5120]{1,0:T(8,128)(2,1)} %collective-permute-done.13.h1_ref, bf16[128,5120]{1,0:T(8,128)(2,1)} %collective-permute-done.20.h2_ref, ...), custom_call_target="tpu_custom_call" | custom-call | flops 671088640 | bytes 7340032 | tf_op jit(solution)/shard_map/gradient_terms/pallas_call | solution.py:231
  126.9 10.7 %all-to-all-start.1 = ((bf16[32,160,128]{2,1,0:T(8,128)(2,1)}), bf16[32,160,128]{2,1,0:T(8,128)(2,1)S(1)}, u32[]{:S(2)}, u32[]{:S(2)}) async-start(bf16[32,160,128]{2,1,0:T(8,128)(2,1)} %bitcast.190), calls=%async_computation.1 | async-start | bytes 2621440 | tf_op jit(solution)/shard_map/all_to_all | solution.py:326
  137.6 3.2 %fusion.9 = f32[4,32,8,128]{3,2,0,1:T(8,128)S(1)} fusion(bf16[4,32,8,512]{3,2,0,1:T(8,128)(2,1)} %divide_convert_fusion, bf16[32,512,128]{2,1,0:T(8,128)(2,1)} %param.37), kind=kOutput, calls=%fused_computation.15 | convolution fusion | flops 134217728 | bytes 5767168 | tf_op jit(solution)/shard_map/srgc,rcd->srgd/dot_general | solution.py:426
  140.8 8.8 %constant_dynamic-slice_fusion.4 = (bf16[1024,2560]{1,0:T(8,128)(2,1)}, bf16[1024,2560]{1,0:T(8,128)(2,1)}) fusion(bf16[1024,5120]{1,0:T(8,128)(2,1)} %param.39, s32[]{:T(128)S(6)} %select_n.146, s32[]{:T(128)S(6)} %select_n.145), kind=kLoop, calls=%fused_computation.93 | loop fusion | bytes 20971528 | tf_op jit(solution)/shard_map/dynamic_slice | solution.py:431
  149.6 7.4 %all-to-all-done.1 = bf16[32,160,128]{2,1,0:T(8,128)(2,1)S(1)} async-done(((bf16[32,160,128]{2,1,0:T(8,128)(2,1)}), bf16[32,160,128]{2,1,0:T(8,128)(2,1)S(1)}, u32[]{:S(2)}, u32[]{:S(2)}) %all-to-all-start.1) | async-done | bytes 1310752 | tf_op jit(solution)/shard_map/all_to_all | solution.py:326
  157.9 1.2 broadcast_in_dim.85
  159.1 4.7 %all-to-all-start.2 = ((bf16[32,160,128]{2,1,0:T(8,128)(2,1)}), bf16[32,160,128]{2,1,0:T(8,128)(2,1)}, u32[]{:S(2)}, u32[]{:S(2)}) async-start(bf16[32,160,128]{2,1,0:T(8,128)(2,1)} %broadcast_in_dim.85), calls=%async_computation.2 | async-start | bytes 2621440 | tf_op jit(solution)/shard_map/all_to_all | solution.py:326
  164.0 3.3 %collective-permute-start.21 = (f32[3,40,128]{2,1,0:T(8,128)S(1)}, f32[3,40,128]{2,1,0:T(8,128)S(1)}, u32[]{:S(2)}, u32[]{:S(2)}) collective-permute-start(f32[3,40,128]{2,1,0:T(8,128)S(1)} %get-tuple-element.78), channel_id=1, source_target_pairs={{0,1},{1,0},{2,3},{3,2},{4,5},{5,4},{6,7},{7,6},{8,9},{9,8},{10,11... | collective-permute-start | bytes 184328 | tf_op jit(solution)/shard_map/ppermute | solution.py:39
  167.5 1.6 collective-permute-start.23
  169.9 9.6 %collective-permute-done.22 = f32[3,40,128]{2,1,0:T(8,128)S(1)} collective-permute-done((f32[3,40,128]{2,1,0:T(8,128)S(1)}, f32[3,40,128]{2,1,0:T(8,128)S(1)}, u32[]{:S(2)}, u32[]{:S(2)}) %collective-permute-start.22) | collective-permute-done | bytes 61472 | tf_op jit(solution)/shard_map/ppermute | solution.py:39
  179.5 4.7 %collective-permute-done.23 = f32[3,40,128]{2,1,0:T(8,128)S(1)} collective-permute-done((f32[3,40,128]{2,1,0:T(8,128)S(1)}, f32[3,40,128]{2,1,0:T(8,128)S(1)}, u32[]{:S(2)}, u32[]{:S(2)}) %collective-permute-start.23) | collective-permute-done | bytes 61472 | tf_op jit(solution)/shard_map/ppermute | solution.py:39
  184.5 1.8 fusion.14
  186.4 1.6 add_convert_fusion.1
  188.1 3.3 %fusion.15 = f32[128,2560]{1,0:T(8,128)S(1)} fusion(bf16[1024,2560]{1,0:T(8,128)(2,1)} %get-tuple-element.46, bf16[16,8,8,128]{3,2,1,0:T(8,128)(2,1)S(1)} %bitcast.191), kind=kOutput, calls=%fused_computation.26 | convolution fusion | flops 671088640 | bytes 6815744 | tf_op jit(solution)/shard_map/dot_general | solution.py:457
  191.4 2.1 collective-permute-start.24
  194.3 1.8 collective-permute-done.24
  196.3 2.5 %collective-permute-start.25 = (bf16[128,2560]{1,0:T(8,128)(2,1)S(1)}, bf16[128,2560]{1,0:T(8,128)(2,1)}, u32[]{:S(2)}, u32[]{:S(2)}) collective-permute-start(bf16[128,2560]{1,0:T(8,128)(2,1)S(1)} %get-tuple-element.53), channel_id=1, source_target_pairs={{0,2},{1,3},{2,0},{3,1},{4,6},{5,7},{6,4},{7,5},{8,10},{9,11},{10,... | collective-permute-start | bytes 1966088 | tf_op jit(solution)/shard_map/ppermute | solution.py:39
  198.8 3.5 %copied.1 = bf16[5120,128]{1,0:T(8,128)(2,1)} custom-call(bf16[5120,128]{1,0:T(8,128)(2,1)} %bitcast.48.from_ref), custom_call_target="tpu_custom_call" | custom-call | bytes 2621440 | tf_op jit(solution)/shard_map/copied/pallas_call | solution.py:254
  202.3 11.5 %collective-permute-done.25 = bf16[128,2560]{1,0:T(8,128)(2,1)} collective-permute-done((bf16[128,2560]{1,0:T(8,128)(2,1)S(1)}, bf16[128,2560]{1,0:T(8,128)(2,1)}, u32[]{:S(2)}, u32[]{:S(2)}) %collective-permute-start.25) | collective-permute-done | bytes 655392 | tf_op jit(solution)/shard_map/ppermute | solution.py:39
  213.9 1.2 constant_dynamic-update-slice_fusion.1
  217.9 1.0 copy-done.8
  (134 shorter events, 25.6 us)
Async XLA Ops:
  0.6 183.9 %copy-start = (bf16[4,32,5120]{2,1,0:T(8,128)(2,1)S(1)}, bf16[4,32,5120]{2,1,0:T(8,128)(2,1)}, u32[]{:S(2)}) copy-start(bf16[4,32,5120]{2,1,0:T(8,128)(2,1)} %param.33) | copy-start | bytes 3932164
  0.6 12.4 %copy-start.9 = (bf16[1,128,4096]{2,1,0:T(8,128)(2,1)S(1)}, bf16[1,128,4096]{2,1,0:T(8,128)(2,1)}, u32[]{:S(2)}) copy-start(bf16[1,128,4096]{2,1,0:T(8,128)(2,1)} %param.20) | copy-start | bytes 3145732
  2.1 14.9 %collective-permute-start.3 = (bf16[128,128]{1,0:T(8,128)(2,1)S(1)}, bf16[128,128]{1,0:T(8,128)(2,1)S(1)}, u32[]{:S(2)}, u32[]{:S(2)}) collective-permute-start(bf16[128,128]{1,0:T(8,128)(2,1)S(1)} %bitcast.225), channel_id=1, source_target_pairs={{0,32},{1,33},{2,34},{3,35},{4,36},{5,37},{6,38},{7,39},{8,40},{9,... | collective-permute-start | bytes 98312 | tf_op jit(solution)/shard_map/ppermute | solution.py:39
  4.3 12.8 %collective-permute-start.4 = (bf16[128,128]{1,0:T(8,128)(2,1)S(1)}, bf16[128,128]{1,0:T(8,128)(2,1)S(1)}, u32[]{:S(2)}, u32[]{:S(2)}) collective-permute-start(bf16[128,128]{1,0:T(8,128)(2,1)S(1)} %bitcast.226), channel_id=1, source_target_pairs={{0,64},{1,65},{2,66},{3,67},{4,68},{5,69},{6,70},{7,71},{8,72},{9,... | collective-permute-start | bytes 98312 | tf_op jit(solution)/shard_map/ppermute | solution.py:39
  6.7 10.4 %collective-permute-start.5 = (bf16[128,128]{1,0:T(8,128)(2,1)S(1)}, bf16[128,128]{1,0:T(8,128)(2,1)S(1)}, u32[]{:S(2)}, u32[]{:S(2)}) collective-permute-start(bf16[128,128]{1,0:T(8,128)(2,1)S(1)} %bitcast.227), channel_id=1, source_target_pairs={{0,96},{1,97},{2,98},{3,99},{4,100},{5,101},{6,102},{7,103},{8,104... | collective-permute-start | bytes 98312 | tf_op jit(solution)/shard_map/ppermute | solution.py:39
  13.3 18.9 %copy-start.17 = (s32[32]{0:T(128)S(1)}, s32[32]{0:T(128)}, u32[]{:S(2)}) copy-start(s32[32]{0:T(128)} %param.38) | copy-start | bytes 388
  14.1 34.2 %collective-permute-start.2 = (bf16[128,2048]{1,0:T(8,128)(2,1)}, bf16[128,2048]{1,0:T(8,128)(2,1)S(1)}, u32[]{:S(2)}, u32[]{:S(2)}) collective-permute-start(bf16[128,2048]{1,0:T(8,128)(2,1)} %pad_maximum_fusion.3), channel_id=1, source_target_pairs={{0,96},{1,97},{2,98},{3,99},{4,100},{5,101},{6,102},{7,103},{8,104... | collective-permute-start | bytes 1572872 | tf_op jit(solution)/shard_map/ppermute | solution.py:39
  15.0 33.3 %collective-permute-start.1 = (bf16[128,2048]{1,0:T(8,128)(2,1)}, bf16[128,2048]{1,0:T(8,128)(2,1)S(1)}, u32[]{:S(2)}, u32[]{:S(2)}) collective-permute-start(bf16[128,2048]{1,0:T(8,128)(2,1)} %pad_maximum_fusion.2), channel_id=1, source_target_pairs={{0,64},{1,65},{2,66},{3,67},{4,68},{5,69},{6,70},{7,71},{8,72},{9,... | collective-permute-start | bytes 1572872 | tf_op jit(solution)/shard_map/ppermute | solution.py:39
  17.1 6.3 %collective-permute-start.9 = (bf16[4,128,128]{2,1,0:T(8,128)(2,1)S(1)}, bf16[4,128,128]{2,1,0:T(8,128)(2,1)S(1)}, u32[]{:S(2)}, u32[]{:S(2)}) collective-permute-start(bf16[4,128,128]{2,1,0:T(8,128)(2,1)S(1)} %pad_maximum_fusion.9.refs_4_), channel_id=1, source_target_pairs={{0,16},{1,17},{2,18},{3,19},{4,20},{5,21},{6,22},{7,23},{8,24},{9,... | collective-permute-start | bytes 393224 | tf_op jit(solution)/shard_map/ppermute | solution.py:39
  21.6 26.7 %collective-permute-start = (bf16[128,2048]{1,0:T(8,128)(2,1)}, bf16[128,2048]{1,0:T(8,128)(2,1)S(1)}, u32[]{:S(2)}, u32[]{:S(2)}) collective-permute-start(bf16[128,2048]{1,0:T(8,128)(2,1)} %pad_maximum_fusion.1), channel_id=1, source_target_pairs={{0,32},{1,33},{2,34},{3,35},{4,36},{5,37},{6,38},{7,39},{8,40},{9,... | collective-permute-start | bytes 1572872 | tf_op jit(solution)/shard_map/ppermute | solution.py:39
  21.6 4.5 %collective-permute-start.11 = (bf16[4,128,128]{2,1,0:T(8,128)(2,1)S(1)}, bf16[4,128,128]{2,1,0:T(8,128)(2,1)}, u32[]{:S(2)}, u32[]{:S(2)}) collective-permute-start(bf16[4,128,128]{2,1,0:T(8,128)(2,1)S(1)} %pad_maximum_fusion.9.refs_4_), channel_id=1, source_target_pairs={{0,24},{1,25},{2,26},{3,27},{4,28},{5,29},{6,30},{7,31},{8,0},{9,1... | collective-permute-start | bytes 393224 | tf_op jit(solution)/shard_map/ppermute | solution.py:39
  23.4 8.8 %copy-start.1 = (bf16[4,128,128]{2,1,0:T(8,128)(2,1)}, bf16[4,128,128]{2,1,0:T(8,128)(2,1)S(1)}, u32[]{:S(2)}) copy-start(bf16[4,128,128]{2,1,0:T(8,128)(2,1)S(1)} %collective-permute-done.9.refs_8_) | copy-start | bytes 393220
  23.4 5.8 %collective-permute-start.7 = (bf16[4,128,128]{2,1,0:T(8,128)(2,1)S(1)}, bf16[4,128,128]{2,1,0:T(8,128)(2,1)}, u32[]{:S(2)}, u32[]{:S(2)}) collective-permute-start(bf16[4,128,128]{2,1,0:T(8,128)(2,1)S(1)} %pad_maximum_fusion.9.refs_4_), channel_id=1, source_target_pairs={{0,8},{1,9},{2,10},{3,11},{4,12},{5,13},{6,14},{7,15},{8,16},{9,17... | collective-permute-start | bytes 393224 | tf_op jit(solution)/shard_map/ppermute | solution.py:39
  26.2 6.1 %collective-permute-start.6 = (bf16[4,128,128]{2,1,0:T(8,128)(2,1)S(1)}, bf16[4,128,128]{2,1,0:T(8,128)(2,1)S(1)}, u32[]{:S(2)}, u32[]{:S(2)}) collective-permute-start(bf16[4,128,128]{2,1,0:T(8,128)(2,1)S(1)} %pad_maximum_fusion.9.refs_4_), channel_id=1, source_target_pairs={{0,4},{1,5},{2,6},{3,7},{4,0},{5,1},{6,2},{7,3},{8,12},{9,13},{10,... | collective-permute-start | bytes 393224 | tf_op jit(solution)/shard_map/ppermute | solution.py:39
  29.2 6.7 %collective-permute-start.10 = (bf16[4,128,128]{2,1,0:T(8,128)(2,1)S(1)}, bf16[4,128,128]{2,1,0:T(8,128)(2,1)S(1)}, u32[]{:S(2)}, u32[]{:S(2)}) collective-permute-start(bf16[4,128,128]{2,1,0:T(8,128)(2,1)S(1)} %collective-permute-done.9.refs_8_), channel_id=1, source_target_pairs={{0,4},{1,5},{2,6},{3,7},{4,0},{5,1},{6,2},{7,3},{8,12},{9,13},{10,... | collective-permute-start | bytes 393224 | tf_op jit(solution)/shard_map/ppermute | solution.py:39
  32.9 7.9 %collective-permute-start.12 = (bf16[4,128,128]{2,1,0:T(8,128)(2,1)}, bf16[4,128,128]{2,1,0:T(8,128)(2,1)}, u32[]{:S(2)}, u32[]{:S(2)}) collective-permute-start(bf16[4,128,128]{2,1,0:T(8,128)(2,1)} %collective-permute-done.11.refs_10_), channel_id=1, source_target_pairs={{0,4},{1,5},{2,6},{3,7},{4,0},{5,1},{6,2},{7,3},{8,12},{9,13},{10,... | collective-permute-start | bytes 393224 | tf_op jit(solution)/shard_map/ppermute | solution.py:39
  36.0 0.7 copy-start.5
  36.6 6.2 %collective-permute-start.8 = (bf16[4,128,128]{2,1,0:T(8,128)(2,1)}, bf16[4,128,128]{2,1,0:T(8,128)(2,1)}, u32[]{:S(2)}, u32[]{:S(2)}) collective-permute-start(bf16[4,128,128]{2,1,0:T(8,128)(2,1)} %collective-permute-done.7.refs_6_), channel_id=1, source_target_pairs={{0,4},{1,5},{2,6},{3,7},{4,0},{5,1},{6,2},{7,3},{8,12},{9,13},{10,... | collective-permute-start | bytes 393224 | tf_op jit(solution)/shard_map/ppermute | solution.py:39
  40.8 33.3 %copy-start.7 = (s32[4]{0:T(128)}, s32[4]{0:T(128)S(1)}, u32[]{:S(2)}) copy-start(s32[4]{0:T(128)S(1)} %pad_add_fusion.where_ref) | copy-start | bytes 52
  40.8 64.5 %collective-permute-start.13 = (bf16[128,5120]{1,0:T(8,128)(2,1)}, bf16[128,5120]{1,0:T(8,128)(2,1)}, u32[]{:S(2)}, u32[]{:S(2)}) collective-permute-start(bf16[128,5120]{1,0:T(8,128)(2,1)} %bitcast.233), channel_id=1, source_target_pairs={{0,1},{1,9},{2,17},{3,25},{4,5},{5,13},{6,21},{7,29},{8,0},{9,8},{... | collective-permute-start | bytes 3932168 | tf_op jit(solution)/shard_map/ppermute | solution.py:39
  42.8 62.5 %collective-permute-start.14 = (bf16[128,5120]{1,0:T(8,128)(2,1)}, bf16[128,5120]{1,0:T(8,128)(2,1)}, u32[]{:S(2)}, u32[]{:S(2)}) collective-permute-start(bf16[128,5120]{1,0:T(8,128)(2,1)} %bitcast.234), channel_id=1, source_target_pairs={{0,19},{1,27},{2,3},{3,11},{4,23},{5,31},{6,7},{7,15},{8,18},{9,26... | collective-permute-start | bytes 3932168 | tf_op jit(solution)/shard_map/ppermute | solution.py:39
  48.4 0.9 copy-start.2
  49.3 0.9 copy-start.4
  50.2 0.9 copy-start.6
  51.1 23.0 %copy-start.12 = (bf16[4,32,1024]{2,1,0:T(8,128)(2,1)S(1)}, bf16[4,32,1024]{2,1,0:T(8,128)(2,1)}, u32[]{:S(2)}) copy-start(bf16[4,32,1024]{2,1,0:T(8,128)(2,1)} %param.34) | copy-start | bytes 786436
  77.2 27.2 %collective-permute-start.15 = (f32[3,40,128]{2,1,0:T(8,128)S(1)}, f32[3,40,128]{2,1,0:T(8,128)S(1)}, u32[]{:S(2)}, u32[]{:S(2)}) collective-permute-start(f32[3,40,128]{2,1,0:T(8,128)S(1)} %bitcast.221), channel_id=1, source_target_pairs={{0,1},{1,0},{2,3},{3,2},{4,5},{5,4},{6,7},{7,6},{8,9},{9,8},{10,11... | collective-permute-start | bytes 184328 | tf_op jit(solution)/shard_map/ppermute | solution.py:39
  80.2 24.2 %collective-permute-start.16 = (f32[3,40,128]{2,1,0:T(8,128)S(1)}, f32[3,40,128]{2,1,0:T(8,128)S(1)}, u32[]{:S(2)}, u32[]{:S(2)}) collective-permute-start(f32[3,40,128]{2,1,0:T(8,128)S(1)} %bitcast.219), channel_id=1, source_target_pairs={{0,2},{1,3},{2,0},{3,1},{4,6},{5,7},{6,4},{7,5},{8,10},{9,11},{10,... | collective-permute-start | bytes 184328 | tf_op jit(solution)/shard_map/ppermute | solution.py:39
  80.2 24.2 %collective-permute-start.17 = (f32[3,40,128]{2,1,0:T(8,128)S(1)}, f32[3,40,128]{2,1,0:T(8,128)}, u32[]{:S(2)}, u32[]{:S(2)}) collective-permute-start(f32[3,40,128]{2,1,0:T(8,128)S(1)} %bitcast.217), channel_id=1, source_target_pairs={{0,3},{1,2},{2,1},{3,0},{4,7},{5,6},{6,5},{7,4},{8,11},{9,10},{10,... | collective-permute-start | bytes 184328 | tf_op jit(solution)/shard_map/ppermute | solution.py:39
  81.9 31.4 %all-to-all-start = ((bf16[8,512,128]{2,1,0:T(8,128)(2,1)}), bf16[8,512,128]{2,1,0:T(8,128)(2,1)S(1)}, u32[]{:S(2)}, u32[]{:S(2)}) async-start(bf16[8,512,128]{2,1,0:T(8,128)(2,1)} %bitcast.21), calls=%async_computation | async-start | bytes 2097152 | tf_op jit(solution)/shard_map/all_to_all | solution.py:326
  96.4 3.8 %copy-start.16 = (pred[4,4]{1,0:T(4,128)(4,1)S(1)}, pred[4,4]{1,0:T(4,128)(4,1)}, u32[]{:S(2)}) copy-start(pred[4,4]{1,0:T(4,128)(4,1)} %iota_compare_fusion.1) | copy-start | bytes 52
  96.4 3.8 %copy-start.18 = (bf16[4,32,128]{2,1,0:T(8,128)(2,1)S(1)}, bf16[4,32,128]{2,1,0:T(8,128)(2,1)}, u32[]{:S(2)}) copy-start(bf16[4,32,128]{2,1,0:T(8,128)(2,1)} %param.35) | copy-start | bytes 98308
  113.2 7.9 %collective-permute-start.19 = (bf16[128,5120]{1,0:T(8,128)(2,1)}, bf16[128,5120]{1,0:T(8,128)(2,1)}, u32[]{:S(2)}, u32[]{:S(2)}) collective-permute-start(bf16[128,5120]{1,0:T(8,128)(2,1)} %collective-permute-done.13.h1_ref), channel_id=1, source_target_pairs={{0,1},{1,0},{2,3},{3,2},{4,5},{5,4},{6,7},{7,6},{8,9},{9,8},{10,11... | collective-permute-start | bytes 3932168 | tf_op jit(solution)/shard_map/ppermute | solution.py:39
  114.6 6.6 %collective-permute-start.20 = (bf16[128,5120]{1,0:T(8,128)(2,1)}, bf16[128,5120]{1,0:T(8,128)(2,1)}, u32[]{:S(2)}, u32[]{:S(2)}) collective-permute-start(bf16[128,5120]{1,0:T(8,128)(2,1)} %collective-permute-done.14.h3_ref), channel_id=1, source_target_pairs={{0,1},{1,0},{2,3},{3,2},{4,5},{5,4},{6,7},{7,6},{8,9},{9,8},{10,11... | collective-permute-start | bytes 3932168 | tf_op jit(solution)/shard_map/ppermute | solution.py:39
  114.7 6.4 %collective-permute-start.18 = (bf16[4,128,128]{2,1,0:T(8,128)(2,1)S(1)}, bf16[4,128,128]{2,1,0:T(8,128)(2,1)S(1)}, u32[]{:S(2)}, u32[]{:S(2)}) collective-permute-start(bf16[4,128,128]{2,1,0:T(8,128)(2,1)S(1)} %bitcast.214), channel_id=1, source_target_pairs={{0,0},{1,8},{2,16},{3,24},{4,4},{5,12},{6,20},{7,28},{8,32},{9,40}... | collective-permute-start | bytes 393224 | tf_op jit(solution)/shard_map/ppermute | solution.py:39
  126.9 30.1 %all-to-all-start.1 = ((bf16[32,160,128]{2,1,0:T(8,128)(2,1)}), bf16[32,160,128]{2,1,0:T(8,128)(2,1)S(1)}, u32[]{:S(2)}, u32[]{:S(2)}) async-start(bf16[32,160,128]{2,1,0:T(8,128)(2,1)} %bitcast.190), calls=%async_computation.1 | async-start | bytes 2621440 | tf_op jit(solution)/shard_map/all_to_all | solution.py:326
  157.9 5.9 %copy-start.11 = (f32[160,128]{1,0:T(8,128)S(1)}, f32[160,128]{1,0:T(8,128)}, u32[]{:S(2)}) copy-start(f32[160,128]{1,0:T(8,128)} %copy-done.10) | copy-start | bytes 245764
  159.1 25.4 %all-to-all-start.2 = ((bf16[32,160,128]{2,1,0:T(8,128)(2,1)}), bf16[32,160,128]{2,1,0:T(8,128)(2,1)}, u32[]{:S(2)}, u32[]{:S(2)}) async-start(bf16[32,160,128]{2,1,0:T(8,128)(2,1)} %broadcast_in_dim.85), calls=%async_computation.2 | async-start | bytes 2621440 | tf_op jit(solution)/shard_map/all_to_all | solution.py:326
  163.8 29.6 %slice-start = ((s8[5242880]{0:T(1024)(128)(4,1)}), s8[1048576]{0:T(1024)(128)(4,1)S(1)}, s32[]{:S(2)}) async-start(s8[5242880]{0:T(1024)(128)(4,1)} %bitcast.188), calls=%async_computation.3 | async-start | bytes 2097152
  164.0 5.9 %collective-permute-start.21 = (f32[3,40,128]{2,1,0:T(8,128)S(1)}, f32[3,40,128]{2,1,0:T(8,128)S(1)}, u32[]{:S(2)}, u32[]{:S(2)}) collective-permute-start(f32[3,40,128]{2,1,0:T(8,128)S(1)} %get-tuple-element.78), channel_id=1, source_target_pairs={{0,1},{1,0},{2,3},{3,2},{4,5},{5,4},{6,7},{7,6},{8,9},{9,8},{10,11... | collective-permute-start | bytes 184328 | tf_op jit(solution)/shard_map/ppermute | solution.py:39
  167.3 12.2 %collective-permute-start.22 = (f32[3,40,128]{2,1,0:T(8,128)S(1)}, f32[3,40,128]{2,1,0:T(8,128)S(1)}, u32[]{:S(2)}, u32[]{:S(2)}) collective-permute-start(f32[3,40,128]{2,1,0:T(8,128)S(1)} %get-tuple-element.77), channel_id=1, source_target_pairs={{0,2},{1,3},{2,0},{3,1},{4,6},{5,7},{6,4},{7,5},{8,10},{9,11},{10,... | collective-permute-start | bytes 184328 | tf_op jit(solution)/shard_map/ppermute | solution.py:39
  167.5 16.7 %collective-permute-start.23 = (f32[3,40,128]{2,1,0:T(8,128)S(1)}, f32[3,40,128]{2,1,0:T(8,128)S(1)}, u32[]{:S(2)}, u32[]{:S(2)}) collective-permute-start(f32[3,40,128]{2,1,0:T(8,128)S(1)} %get-tuple-element.76), channel_id=1, source_target_pairs={{0,3},{1,2},{2,1},{3,0},{4,7},{5,6},{6,5},{7,4},{8,11},{9,10},{10,... | collective-permute-start | bytes 184328 | tf_op jit(solution)/shard_map/ppermute | solution.py:39
  184.2 2.2 copy-start.13
  184.2 2.2 copy-start.14
  186.4 7.1 %slice-start.1 = ((s8[5242880]{0:T(1024)(128)(4,1)}), s8[4194304]{0:T(1024)(128)(4,1)S(1)}, s32[]{:S(2)}) async-start(s8[5242880]{0:T(1024)(128)(4,1)} %bitcast.188), calls=%async_computation.4 | async-start | bytes 8388608
  191.4 4.7 %collective-permute-start.24 = (f32[128,2560]{1,0:T(8,128)S(1)}, f32[128,2560]{1,0:T(8,128)S(1)}, u32[]{:S(2)}, u32[]{:S(2)}) collective-permute-start(f32[128,2560]{1,0:T(8,128)S(1)} %fusion.15), channel_id=1, source_target_pairs={{0,1},{1,0},{2,3},{3,2},{4,5},{5,4},{6,7},{7,6},{8,9},{9,8},{10,11... | collective-permute-start | bytes 3932168 | tf_op jit(solution)/shard_map/ppermute | solution.py:39
  196.3 17.5 %collective-permute-start.25 = (bf16[128,2560]{1,0:T(8,128)(2,1)S(1)}, bf16[128,2560]{1,0:T(8,128)(2,1)}, u32[]{:S(2)}, u32[]{:S(2)}) collective-permute-start(bf16[128,2560]{1,0:T(8,128)(2,1)S(1)} %get-tuple-element.53), channel_id=1, source_target_pairs={{0,2},{1,3},{2,0},{3,1},{4,6},{5,7},{6,4},{7,5},{8,10},{9,11},{10,... | collective-permute-start | bytes 1966088 | tf_op jit(solution)/shard_map/ppermute | solution.py:39
  215.1 2.7 %collective-permute-start.26 = (bf16[128,2560]{1,0:T(8,128)(2,1)S(1)}, bf16[128,2560]{1,0:T(8,128)(2,1)S(1)}, u32[]{:S(2)}, u32[]{:S(2)}) collective-permute-start(bf16[128,2560]{1,0:T(8,128)(2,1)S(1)} %get-tuple-element.52), channel_id=1, source_target_pairs={{0,1},{1,0},{2,3},{3,2},{4,5},{5,4},{6,7},{7,6},{8,9},{9,8},{10,11... | collective-permute-start | bytes 1966088 | tf_op jit(solution)/shard_map/ppermute | solution.py:39
  217.9 1.1 copy-start.8
  (3 other events, 1.9 us)

commit v5 on v4

--- a/solution.py
+++ b/solution.py
@@ -387,7 +387,18 @@
 
     where = jnp.stack([g, lengths[0, 0], x, t]).astype(jnp.int32)
     partial = attention_terms(where, blocks, keys)
-    partial, dec_query, *state = together(partial, dec_query, master, first_moment, second_moment)
+
+    along_zy = [[a * NG + b for b in range(NG)] for a in range(NX)]
+    terms = exchange(partial.reshape(NG, NZ * BLOCK, HD), along_zy)
+    terms, hidden_parts[1], hidden_parts[3] = together(terms, hidden_parts[1], hidden_parts[3])
+    hidden_parts[0] = route(hidden_parts[1], flip_core)
+    hidden_parts[2] = route(hidden_parts[3], flip_core)
+    dvalue = jnp.sum(terms.astype(f32), axis=0).astype(bf).reshape(NZ, BLOCK, HD)
+    dvalue = route(dvalue, swap)
+    gradient = gradient_terms(where, dvalue, hidden_parts)
+    gradient, dec_query, *state = together(
+        gradient, dec_query, master, first_moment, second_moment
+    )
 
     state = jnp.stack(state).reshape(3, 40, KV, HD)
 
@@ -399,22 +410,9 @@
     ]
     moved = jnp.stack(moved)
     by_row = jnp.stack([pick(moved, t ^ d) for d in range(NT)], axis=1)
-    by_row = by_row.reshape(3, NT * 40, HD)
+    old_master, old_first, old_second = by_row.reshape(3, NT * 40, HD)
 
     old_weights, new_weights = decode_weights(dec_query, dec_key, cache_keys, cache_len)
-
-    along_zy = [[a * NG + b for b in range(NG)] for a in range(NX)]
-    terms = exchange(partial.reshape(NG, NZ * BLOCK, HD), along_zy)
-    terms, hidden_parts[1], hidden_parts[3], by_row, old_weights, new_weights = together(
-        terms, hidden_parts[1], hidden_parts[3], by_row, old_weights, new_weights
-    )
-    old_master, old_first, old_second = by_row
-    dvalue = jnp.sum(terms.astype(f32), axis=0).astype(bf).reshape(NZ, BLOCK, HD)
-    dvalue = route(dvalue, swap)
-    hidden_parts[0] = route(hidden_parts[1], flip_core)
-    hidden_parts[2] = route(hidden_parts[3], flip_core)
-    gradient = gradient_terms(where, dvalue, hidden_parts)
-    gradient, out_weight, old_weights = together(gradient, out_weight, old_weights)
     terms = exchange(gradient.reshape(NX * NG, NT * 40, HD))
     gradient = jnp.sum(terms.astype(f32), axis=0)
 
@@ -426,12 +424,12 @@
     cached = jnp.einsum(
         "srgc,rcd->srgd", old_weights, cache_values, preferred_element_type=f32
     )
+    rounded, cached, new_weights, out_weight = together(
+        new_master.astype(bf), cached, new_weights, out_weight
+    )
     core, half = t % 2, out_weight.shape[1] // 2
     own_weight = lax.dynamic_slice_in_dim(out_weight, core * half, half, 1)
     other_weight = lax.dynamic_slice_in_dim(out_weight, (1 - core) * half, half, 1)
-    rounded, cached, own_weight, other_weight = together(
-        new_master.astype(bf), cached, own_weight, other_weight
-    )
     rollout = exchange(jnp.broadcast_to(rounded[None], (NX * NG, NT * 40, HD))).reshape(5120, HD)
 
     news = jnp.stack([new_master, new_first, new_second]).reshape(3, NT, 40, HD)
@@ -440,7 +438,7 @@
     ]
     back = jnp.stack(back)
     back = jnp.stack([pick(back, t ^ d) for d in range(NT)], axis=2)
-    rollout, back = together(rollout, back)
+    rollout, back, own_weight, other_weight = together(rollout, back, own_weight, other_weight)
     new_master, new_first, new_second = back.reshape(3, 40, KV * HD)
 
     step_count, dec_rows = dec_hidden.shape[:2]

time: 221 us -> 215 us (0.973)
  starting transfers between devices: 78.2 us -> 64.4 us
  waiting for transfers between devices: 53.3 us -> 60 us
  Pallas kernels: 31.6 us -> 37.8 us
  matrix products: 14.2 us -> 10.9 us
    ppermute x27, starting transfers between devices: 48.4 us -> 41.2 us  [route(): return lax.ppermute(value, ('ctx', 'tp'), pairs)]
    all_to_all x3, starting transfers between devices: 29.8 us -> 23.1 us  [exchange(): lax.all_to_all(value, 'ctx', split_axis=0, concat_axis=0, axis_index_grou...]
    pallas_call x1, Pallas kernels: 23 us -> 29.2 us  [attention_terms(): pl.pallas_call(attention_kernel, out_shape=jax.ShapeDtypeStruct((NX * NY,...]
    all_to_all x3, waiting for transfers between devices: 15.3 us -> 20 us  [exchange(): lax.all_to_all(value, 'ctx', split_axis=0, concat_axis=0, axis_index_grou...]
    another operation x4, local copies, waits for them, and re-layouts: 2.76 us -> 0.11 us  [shards(): state = jnp.stack(state).reshape(3, 40, KV, HD)]
    dot_general x1, matrix products: 3.19 us -> 0.9 us  [shards(): jnp.einsum('srgc,rcd->srgd', old_weights, cache_values, preferred_element...]
    unnamed x52 -> x62, local copies, waits for them, and re-layouts: 8.66 us -> 9.79 us
  transfers between devices with their start and end apart: 30 -> 30, of which waited for: 13 -> 12; matrix products, arithmetic and copies ran while one was open for 17% -> 16% of each run, Pallas kernels for 12% -> 15%
where the time goes in v5:
time: 215 us; the launch traced here: 214 us
  starting transfers between devices  64.4 us (30%)
  waiting for transfers between devices  60 us (28%)
  Pallas kernels  37.8 us (18%)
  local copies, waits for them, and re-layouts  24.9 us (12%)
  other arithmetic  14.5 us (7%)
  matrix products  10.9 us (5%)
    ppermute x27, starting transfers between devices, route(): return lax.ppermute(value, ('ctx', 'tp'), pairs)  41.2 us
    ppermute x27, waiting for transfers between devices, route(): return lax.ppermute(value, ('ctx', 'tp'), pairs)  40 us
    pallas_call x1, Pallas kernels, attention_terms(): pl.pallas_call(attention_kernel, out_shape=jax.ShapeDtypeStruct((NX * NY,...  29.2 us
    all_to_all x3, starting transfers between devices, exchange(): lax.all_to_all(value, 'ctx', split_axis=0, concat_axis=0, axis_index_grou...  23.1 us
    all_to_all x3, waiting for transfers between devices, exchange(): lax.all_to_all(value, 'ctx', split_axis=0, concat_axis=0, axis_index_grou...  20 us
    unnamed x62, local copies, waits for them, and re-layouts  9.79 us
    dynamic_slice x1, local copies, waits for them, and re-layouts, shards(): lax.dynamic_slice_in_dim(out_weight, (1 - core) * half, half, 1)  8.75 us
    pallas_call x1, Pallas kernels, gradient_terms(): pl.pallas_call(gradient_kernel, grid=(width // tile,), out_shape=jax.Shap...  5.15 us
  transfers between devices with their start and end apart: 30, of which 12 were waited for; matrix products, arithmetic and copies ran while one was open for 16% of the time, Pallas kernels for 15%

profile of v5, /device:TPU:1, one launch (start us, length us, event | category | flops | bytes accessed | tf_op | source)
XLA Modules:
  0.0 213.8 jit_solution(14793934054592843908)
XLA Ops:
  0.7 1.0 reshape_squeeze.3
  2.1 3.4 %collective-permute-start.5 = (bf16[128,128]{1,0:T(8,128)(2,1)S(1)}, bf16[128,128]{1,0:T(8,128)(2,1)}, u32[]{:S(2)}, u32[]{:S(2)}) collective-permute-start(bf16[128,128]{1,0:T(8,128)(2,1)S(1)} %bitcast.209), channel_id=1, source_target_pairs={{0,96},{1,97},{2,98},{3,99},{4,100},{5,101},{6,102},{7,103},{8,104... | collective-permute-start | bytes 98312 | tf_op jit(solution)/shard_map/ppermute | solution.py:39
  10.9 1.6 fusion.4
  14.9 1.5 collective-permute-start
  17.3 1.7 collective-permute-start.7
  19.8 2.9 %collective-permute-start.6 = (bf16[4,128,128]{2,1,0:T(8,128)(2,1)S(1)}, bf16[4,128,128]{2,1,0:T(8,128)(2,1)S(1)}, u32[]{:S(2)}, u32[]{:S(2)}) collective-permute-start(bf16[4,128,128]{2,1,0:T(8,128)(2,1)S(1)} %pad_maximum_fusion.9.refs_4_), channel_id=1, source_target_pairs={{0,4},{1,5},{2,6},{3,7},{4,0},{5,1},{6,2},{7,3},{8,12},{9,13},{10,... | collective-permute-start | bytes 393224 | tf_op jit(solution)/shard_map/ppermute | solution.py:39
  22.8 3.3 %collective-permute-start.9 = (bf16[4,128,128]{2,1,0:T(8,128)(2,1)S(1)}, bf16[4,128,128]{2,1,0:T(8,128)(2,1)S(1)}, u32[]{:S(2)}, u32[]{:S(2)}) collective-permute-start(bf16[4,128,128]{2,1,0:T(8,128)(2,1)S(1)} %pad_maximum_fusion.9.refs_4_), channel_id=1, source_target_pairs={{0,16},{1,17},{2,18},{3,19},{4,20},{5,21},{6,22},{7,23},{8,24},{9,... | collective-permute-start | bytes 393224 | tf_op jit(solution)/shard_map/ppermute | solution.py:39
  26.9 0.9 pad_maximum_fusion.3
  27.7 1.7 collective-permute-start.1
  29.5 2.9 %collective-permute-start.10 = (bf16[4,128,128]{2,1,0:T(8,128)(2,1)S(1)}, bf16[4,128,128]{2,1,0:T(8,128)(2,1)S(1)}, u32[]{:S(2)}, u32[]{:S(2)}) collective-permute-start(bf16[4,128,128]{2,1,0:T(8,128)(2,1)S(1)} %collective-permute-done.9.refs_8_), channel_id=1, source_target_pairs={{0,4},{1,5},{2,6},{3,7},{4,0},{5,1},{6,2},{7,3},{8,12},{9,13},{10,... | collective-permute-start | bytes 393224 | tf_op jit(solution)/shard_map/ppermute | solution.py:39
  33.8 2.0 collective-permute-done.10.refs_9_
  37.2 3.2 %collective-permute-done.12.refs_11_ = bf16[4,128,128]{2,1,0:T(8,128)(2,1)S(1)} collective-permute-done((bf16[4,128,128]{2,1,0:T(8,128)(2,1)S(1)}, bf16[4,128,128]{2,1,0:T(8,128)(2,1)S(1)}, u32[]{:S(2)}, u32[]{:S(2)}) %collective-permute-start.12) | collective-permute-done | bytes 131104 | tf_op jit(solution)/shard_map/ppermute | solution.py:39
  41.1 4.5 %collective-permute-start.14 = (bf16[128,5120]{1,0:T(8,128)(2,1)}, bf16[128,5120]{1,0:T(8,128)(2,1)}, u32[]{:S(2)}, u32[]{:S(2)}) collective-permute-start(bf16[128,5120]{1,0:T(8,128)(2,1)} %bitcast.22), channel_id=1, source_target_pairs={{0,19},{1,27},{2,3},{3,11},{4,23},{5,31},{6,7},{7,15},{8,18},{9,26... | collective-permute-start | bytes 3932168 | tf_op jit(solution)/shard_map/ppermute | solution.py:39
  45.7 1.1 pad_maximum_fusion.refs_0_
  46.8 5.1 %collective-permute-done.2.refs_3_ = bf16[128,2048]{1,0:T(8,128)(2,1)S(1)} collective-permute-done((bf16[128,2048]{1,0:T(8,128)(2,1)}, bf16[128,2048]{1,0:T(8,128)(2,1)S(1)}, u32[]{:S(2)}, u32[]{:S(2)}) %collective-permute-start.2) | collective-permute-done | bytes 524320 | tf_op jit(solution)/shard_map/ppermute | solution.py:39
  51.9 0.9 copy-done.2
  52.8 0.9 copy-done.4
  53.7 0.9 copy-done.6
  54.6 29.2 %attention_terms.1 = bf16[8,4,128,128]{3,2,1,0:T(8,128)(2,1)} custom-call(s32[4]{0:T(128)S(1)} %pad_add_fusion.where_ref, bf16[128,2048]{1,0:T(8,128)(2,1)S(1)} %pad_maximum_fusion.refs_0_, bf16[128,2048]{1,0:T(8,128)(2,1)S(1)} %collective-permute-done.refs_1_, bf16[128,2048]{1,0:T(8,128)(2,1)S(1)} %collective-permute-done.1.refs_2_, ...), custom_call_target="tpu_custom_call" | custom-call | flops 4096 | bytes 4096 | tf_op jit(solution)/shard_map/attention_terms/pallas_call | solution.py:199
  83.7 3.7 %all-to-all-start = ((bf16[8,512,128]{2,1,0:T(8,128)(2,1)}), bf16[8,512,128]{2,1,0:T(8,128)(2,1)S(1)}, u32[]{:S(2)}, u32[]{:S(2)}) async-start(bf16[8,512,128]{2,1,0:T(8,128)(2,1)} %bitcast.21), calls=%async_computation | async-start | bytes 2097152 | tf_op jit(solution)/shard_map/all_to_all | solution.py:326
  87.5 15.4 %all-to-all-done = bf16[8,512,128]{2,1,0:T(8,128)(2,1)S(1)} async-done(((bf16[8,512,128]{2,1,0:T(8,128)(2,1)}), bf16[8,512,128]{2,1,0:T(8,128)(2,1)S(1)}, u32[]{:S(2)}, u32[]{:S(2)}) %all-to-all-start) | async-done | bytes 1048608 | tf_op jit(solution)/shard_map/all_to_all | solution.py:326
  102.8 2.7 %collective-permute-start.16 = (bf16[128,5120]{1,0:T(8,128)(2,1)}, bf16[128,5120]{1,0:T(8,128)(2,1)}, u32[]{:S(2)}, u32[]{:S(2)}) collective-permute-start(bf16[128,5120]{1,0:T(8,128)(2,1)} %collective-permute-done.13.h1_ref), channel_id=1, source_target_pairs={{0,1},{1,0},{2,3},{3,2},{4,5},{5,4},{6,7},{7,6},{8,9},{9,8},{10,11... | collective-permute-start | bytes 3932168 | tf_op jit(solution)/shard_map/ppermute | solution.py:39
  105.7 1.9 collective-permute-start.15
  107.8 6.6 %collective-permute-done.15.dvalue_ref = bf16[4,128,128]{2,1,0:T(8,128)(2,1)S(1)} collective-permute-done((bf16[4,128,128]{2,1,0:T(8,128)(2,1)S(1)}, bf16[4,128,128]{2,1,0:T(8,128)(2,1)S(1)}, u32[]{:S(2)}, u32[]{:S(2)}) %collective-permute-start.15) | collective-permute-done | bytes 131104 | tf_op jit(solution)/shard_map/ppermute | solution.py:39
  115.0 5.2 %gradient_terms.1 = bf16[5120,128]{1,0:T(8,128)(2,1)} custom-call(s32[4]{0:T(128)} %copy-done.7, bf16[4,128,128]{2,1,0:T(8,128)(2,1)} %copy-done.18, bf16[128,5120]{1,0:T(8,128)(2,1)} %collective-permute-done.16.h0_ref, bf16[128,5120]{1,0:T(8,128)(2,1)} %collective-permute-done.13.h1_ref, bf16[128,5120]{1,0:T(8,128)(2,1)} %collective-permute-done.17.h2_ref, ...), custom_call_target="tpu_custom_call" | custom-call | flops 671088640 | bytes 7340032 | tf_op jit(solution)/shard_map/gradient_terms/pallas_call | solution.py:231
  120.2 11.1 %all-to-all-start.1 = ((bf16[32,160,128]{2,1,0:T(8,128)(2,1)}), bf16[32,160,128]{2,1,0:T(8,128)(2,1)S(1)}, u32[]{:S(2)}, u32[]{:S(2)}) async-start(bf16[32,160,128]{2,1,0:T(8,128)(2,1)} %bitcast.180), calls=%async_computation.1 | async-start | bytes 2621440 | tf_op jit(solution)/shard_map/all_to_all | solution.py:326
  131.8 3.3 %collective-permute-start.20 = (f32[3,40,128]{2,1,0:T(8,128)S(1)}, f32[3,40,128]{2,1,0:T(8,128)S(1)}, u32[]{:S(2)}, u32[]{:S(2)}) collective-permute-start(f32[3,40,128]{2,1,0:T(8,128)S(1)} %bitcast.207), channel_id=1, source_target_pairs={{0,3},{1,2},{2,1},{3,0},{4,7},{5,6},{6,5},{7,4},{8,11},{9,10},{10,... | collective-permute-start | bytes 184328 | tf_op jit(solution)/shard_map/ppermute | solution.py:39
  135.6 3.9 %fusion.5 = (f32[4,32,8]{2,0,1:T(4,128)S(1)}, f32[32,4,8,512]{3,2,1,0:T(8,128)S(1)}) fusion(pred[32,512]{1,0:T(8,128)(4,1)S(1)} %iota_compare_fusion, bf16[32,512,128]{2,1,0:T(8,128)(2,1)} %param.36, bf16[4,32,8,128]{3,2,1,0:T(8,128)(2,1)S(1)} %bitcast.184), kind=kOutput, calls=%fused_computation.9 | convolution fusion | flops 135789568 | bytes 6574080 | tf_op jit(solution)/shard_map/srgd,rcd->srgc/dot_general | solution.py:273
  139.5 1.3 select_reduce_fusion
  141.9 0.9 fusion.9
  143.0 5.4 %collective-permute-done.20 = f32[3,40,128]{2,1,0:T(8,128)S(1)} collective-permute-done((f32[3,40,128]{2,1,0:T(8,128)S(1)}, f32[3,40,128]{2,1,0:T(8,128)S(1)}, u32[]{:S(2)}, u32[]{:S(2)}) %collective-permute-start.20) | collective-permute-done | bytes 61472 | tf_op jit(solution)/shard_map/ppermute | solution.py:39
  148.4 2.4 %all-to-all-done.1 = bf16[32,160,128]{2,1,0:T(8,128)(2,1)S(1)} async-done(((bf16[32,160,128]{2,1,0:T(8,128)(2,1)}), bf16[32,160,128]{2,1,0:T(8,128)(2,1)S(1)}, u32[]{:S(2)}, u32[]{:S(2)}) %all-to-all-start.1) | async-done | bytes 1310752 | tf_op jit(solution)/shard_map/all_to_all | solution.py:326
  151.8 1.2 broadcast_in_dim.85
  153.0 8.3 %all-to-all-start.2 = ((bf16[32,160,128]{2,1,0:T(8,128)(2,1)}), bf16[32,160,128]{2,1,0:T(8,128)(2,1)S(1)}, u32[]{:S(2)}, u32[]{:S(2)}) async-start(bf16[32,160,128]{2,1,0:T(8,128)(2,1)} %broadcast_in_dim.85), calls=%async_computation.2 | async-start | bytes 2621440 | tf_op jit(solution)/shard_map/all_to_all | solution.py:326
  162.9 2.2 %collective-permute-start.22 = (f32[3,40,128]{2,1,0:T(8,128)}, f32[3,40,128]{2,1,0:T(8,128)}, u32[]{:S(2)}, u32[]{:S(2)}) collective-permute-start(f32[3,40,128]{2,1,0:T(8,128)} %get-tuple-element.69), channel_id=1, source_target_pairs={{0,2},{1,3},{2,0},{3,1},{4,6},{5,7},{6,4},{7,5},{8,10},{9,11},{10,... | collective-permute-start | bytes 184328 | tf_op jit(solution)/shard_map/ppermute | solution.py:39
  165.0 8.8 %constant_dynamic-slice_fusion = (bf16[1024,2560]{1,0:T(8,128)(2,1)}, bf16[1024,2560]{1,0:T(8,128)(2,1)}) fusion(bf16[1024,5120]{1,0:T(8,128)(2,1)} %param.39, s32[]{:T(128)S(6)} %select_n.146, s32[]{:T(128)S(6)} %select_n.145), kind=kLoop, calls=%fused_computation.93 | loop fusion | bytes 20971528 | tf_op jit(solution)/shard_map/dynamic_slice | solution.py:432
  174.6 2.8 %collective-permute-done.23 = f32[3,40,128]{2,1,0:T(8,128)} collective-permute-done((f32[3,40,128]{2,1,0:T(8,128)}, f32[3,40,128]{2,1,0:T(8,128)}, u32[]{:S(2)}, u32[]{:S(2)}) %collective-permute-start.23) | collective-permute-done | bytes 61472 | tf_op jit(solution)/shard_map/ppermute | solution.py:39
  177.5 0.9 pad_maximum_fusion.7
  178.7 2.3 %all-to-all-done.2 = bf16[32,160,128]{2,1,0:T(8,128)(2,1)S(1)} async-done(((bf16[32,160,128]{2,1,0:T(8,128)(2,1)}), bf16[32,160,128]{2,1,0:T(8,128)(2,1)S(1)}, u32[]{:S(2)}, u32[]{:S(2)}) %all-to-all-start.2) | async-done | bytes 1310752 | tf_op jit(solution)/shard_map/all_to_all | solution.py:326
  182.6 3.5 %fusion.20 = f32[128,2560]{1,0:T(8,128)S(1)} fusion(bf16[1024,2560]{1,0:T(8,128)(2,1)} %get-tuple-element.38, bf16[16,8,8,128]{3,2,1,0:T(8,128)(2,1)S(1)} %bitcast.181), kind=kOutput, calls=%fused_computation.31 | convolution fusion | flops 671088640 | bytes 6815744 | tf_op jit(solution)/shard_map/dot_general | solution.py:455
  186.1 3.2 %collective-permute-start.24 = (f32[128,2560]{1,0:T(8,128)S(1)}, f32[128,2560]{1,0:T(8,128)S(1)}, u32[]{:S(2)}, u32[]{:S(2)}) collective-permute-start(f32[128,2560]{1,0:T(8,128)S(1)} %fusion.20), channel_id=1, source_target_pairs={{0,1},{1,0},{2,3},{3,2},{4,5},{5,4},{6,7},{7,6},{8,9},{9,8},{10,11... | collective-permute-start | bytes 3932168 | tf_op jit(solution)/shard_map/ppermute | solution.py:39
  189.3 0.8 fusion.22
  190.1 1.8 collective-permute-done.24
  192.2 3.5 %copied.1 = bf16[5120,128]{1,0:T(8,128)(2,1)} custom-call(bf16[5120,128]{1,0:T(8,128)(2,1)} %bitcast.179), custom_call_target="tpu_custom_call" | custom-call | bytes 2621440 | tf_op jit(solution)/shard_map/copied/pallas_call | solution.py:254
  195.7 12.6 %collective-permute-done.25 = bf16[128,2560]{1,0:T(8,128)(2,1)} collective-permute-done((bf16[128,2560]{1,0:T(8,128)(2,1)S(1)}, bf16[128,2560]{1,0:T(8,128)(2,1)}, u32[]{:S(2)}, u32[]{:S(2)}) %collective-permute-start.25) | collective-permute-done | bytes 655392 | tf_op jit(solution)/shard_map/ppermute | solution.py:39
  208.4 1.2 constant_dynamic-update-slice_fusion.1
  209.6 1.3 collective-permute-start.26
  212.7 1.0 copy-done.10
  (142 shorter events, 24.7 us)
Async XLA Ops:
  0.6 180.3 %copy-start = (bf16[4,32,5120]{2,1,0:T(8,128)(2,1)S(1)}, bf16[4,32,5120]{2,1,0:T(8,128)(2,1)}, u32[]{:S(2)}) copy-start(bf16[4,32,5120]{2,1,0:T(8,128)(2,1)} %param.33) | copy-start | bytes 3932164
  2.1 14.4 %collective-permute-start.5 = (bf16[128,128]{1,0:T(8,128)(2,1)S(1)}, bf16[128,128]{1,0:T(8,128)(2,1)}, u32[]{:S(2)}, u32[]{:S(2)}) collective-permute-start(bf16[128,128]{1,0:T(8,128)(2,1)S(1)} %bitcast.209), channel_id=1, source_target_pairs={{0,96},{1,97},{2,98},{3,99},{4,100},{5,101},{6,102},{7,103},{8,104... | collective-permute-start | bytes 98312 | tf_op jit(solution)/shard_map/ppermute | solution.py:39
  5.5 11.0 %collective-permute-start.4 = (bf16[128,128]{1,0:T(8,128)(2,1)S(1)}, bf16[128,128]{1,0:T(8,128)(2,1)}, u32[]{:S(2)}, u32[]{:S(2)}) collective-permute-start(bf16[128,128]{1,0:T(8,128)(2,1)S(1)} %bitcast.210), channel_id=1, source_target_pairs={{0,64},{1,65},{2,66},{3,67},{4,68},{5,69},{6,70},{7,71},{8,72},{9,... | collective-permute-start | bytes 98312 | tf_op jit(solution)/shard_map/ppermute | solution.py:39
  6.6 9.9 %collective-permute-start.3 = (bf16[128,128]{1,0:T(8,128)(2,1)}, bf16[128,128]{1,0:T(8,128)(2,1)}, u32[]{:S(2)}, u32[]{:S(2)}) collective-permute-start(bf16[128,128]{1,0:T(8,128)(2,1)} %bitcast.168), channel_id=1, source_target_pairs={{0,32},{1,33},{2,34},{3,35},{4,36},{5,37},{6,38},{7,39},{8,40},{9,... | collective-permute-start | bytes 98312 | tf_op jit(solution)/shard_map/ppermute | solution.py:39
  10.9 2.4 %copy-start.11 = (bf16[1,128,4096]{2,1,0:T(8,128)(2,1)S(1)}, bf16[1,128,4096]{2,1,0:T(8,128)(2,1)}, u32[]{:S(2)}) copy-start(bf16[1,128,4096]{2,1,0:T(8,128)(2,1)} %param.20) | copy-start | bytes 3145732
  14.1 31.4 %copy-start.22 = (s32[1,2]{1,0:T(1,128)S(1)}, s32[1,2]{1,0:T(1,128)}, u32[]{:S(2)}) copy-start(s32[1,2]{1,0:T(1,128)} %param.27) | copy-start | bytes 28
  14.9 31.8 %collective-permute-start = (bf16[128,2048]{1,0:T(8,128)(2,1)}, bf16[128,2048]{1,0:T(8,128)(2,1)S(1)}, u32[]{:S(2)}, u32[]{:S(2)}) collective-permute-start(bf16[128,2048]{1,0:T(8,128)(2,1)} %pad_maximum_fusion.1), channel_id=1, source_target_pairs={{0,32},{1,33},{2,34},{3,35},{4,36},{5,37},{6,38},{7,39},{8,40},{9,... | collective-permute-start | bytes 1572872 | tf_op jit(solution)/shard_map/ppermute | solution.py:39
  17.3 9.5 %collective-permute-start.7 = (bf16[4,128,128]{2,1,0:T(8,128)(2,1)S(1)}, bf16[4,128,128]{2,1,0:T(8,128)(2,1)S(1)}, u32[]{:S(2)}, u32[]{:S(2)}) collective-permute-start(bf16[4,128,128]{2,1,0:T(8,128)(2,1)S(1)} %pad_maximum_fusion.9.refs_4_), channel_id=1, source_target_pairs={{0,8},{1,9},{2,10},{3,11},{4,12},{5,13},{6,14},{7,15},{8,16},{9,17... | collective-permute-start | bytes 393224 | tf_op jit(solution)/shard_map/ppermute | solution.py:39
  19.8 7.9 %collective-permute-start.6 = (bf16[4,128,128]{2,1,0:T(8,128)(2,1)S(1)}, bf16[4,128,128]{2,1,0:T(8,128)(2,1)S(1)}, u32[]{:S(2)}, u32[]{:S(2)}) collective-permute-start(bf16[4,128,128]{2,1,0:T(8,128)(2,1)S(1)} %pad_maximum_fusion.9.refs_4_), channel_id=1, source_target_pairs={{0,4},{1,5},{2,6},{3,7},{4,0},{5,1},{6,2},{7,3},{8,12},{9,13},{10,... | collective-permute-start | bytes 393224 | tf_op jit(solution)/shard_map/ppermute | solution.py:39
  22.8 6.7 %collective-permute-start.9 = (bf16[4,128,128]{2,1,0:T(8,128)(2,1)S(1)}, bf16[4,128,128]{2,1,0:T(8,128)(2,1)S(1)}, u32[]{:S(2)}, u32[]{:S(2)}) collective-permute-start(bf16[4,128,128]{2,1,0:T(8,128)(2,1)S(1)} %pad_maximum_fusion.9.refs_4_), channel_id=1, source_target_pairs={{0,16},{1,17},{2,18},{3,19},{4,20},{5,21},{6,22},{7,23},{8,24},{9,... | collective-permute-start | bytes 393224 | tf_op jit(solution)/shard_map/ppermute | solution.py:39
  26.1 6.3 %collective-permute-start.11 = (bf16[4,128,128]{2,1,0:T(8,128)(2,1)S(1)}, bf16[4,128,128]{2,1,0:T(8,128)(2,1)S(1)}, u32[]{:S(2)}, u32[]{:S(2)}) collective-permute-start(bf16[4,128,128]{2,1,0:T(8,128)(2,1)S(1)} %pad_maximum_fusion.9.refs_4_), channel_id=1, source_target_pairs={{0,24},{1,25},{2,26},{3,27},{4,28},{5,29},{6,30},{7,31},{8,0},{9,1... | collective-permute-start | bytes 393224 | tf_op jit(solution)/shard_map/ppermute | solution.py:39
  26.8 6.2 %collective-permute-start.8 = (bf16[4,128,128]{2,1,0:T(8,128)(2,1)S(1)}, bf16[4,128,128]{2,1,0:T(8,128)(2,1)S(1)}, u32[]{:S(2)}, u32[]{:S(2)}) collective-permute-start(bf16[4,128,128]{2,1,0:T(8,128)(2,1)S(1)} %collective-permute-done.7.refs_6_), channel_id=1, source_target_pairs={{0,4},{1,5},{2,6},{3,7},{4,0},{5,1},{6,2},{7,3},{8,12},{9,13},{10,... | collective-permute-start | bytes 393224 | tf_op jit(solution)/shard_map/ppermute | solution.py:39
  27.7 19.0 %collective-permute-start.1 = (bf16[128,2048]{1,0:T(8,128)(2,1)}, bf16[128,2048]{1,0:T(8,128)(2,1)S(1)}, u32[]{:S(2)}, u32[]{:S(2)}) collective-permute-start(bf16[128,2048]{1,0:T(8,128)(2,1)} %pad_maximum_fusion.2), channel_id=1, source_target_pairs={{0,64},{1,65},{2,66},{3,67},{4,68},{5,69},{6,70},{7,71},{8,72},{9,... | collective-permute-start | bytes 1572872 | tf_op jit(solution)/shard_map/ppermute | solution.py:39
  29.5 6.4 %collective-permute-start.10 = (bf16[4,128,128]{2,1,0:T(8,128)(2,1)S(1)}, bf16[4,128,128]{2,1,0:T(8,128)(2,1)S(1)}, u32[]{:S(2)}, u32[]{:S(2)}) collective-permute-start(bf16[4,128,128]{2,1,0:T(8,128)(2,1)S(1)} %collective-permute-done.9.refs_8_), channel_id=1, source_target_pairs={{0,4},{1,5},{2,6},{3,7},{4,0},{5,1},{6,2},{7,3},{8,12},{9,13},{10,... | collective-permute-start | bytes 393224 | tf_op jit(solution)/shard_map/ppermute | solution.py:39
  32.4 19.5 %collective-permute-start.2 = (bf16[128,2048]{1,0:T(8,128)(2,1)}, bf16[128,2048]{1,0:T(8,128)(2,1)S(1)}, u32[]{:S(2)}, u32[]{:S(2)}) collective-permute-start(bf16[128,2048]{1,0:T(8,128)(2,1)} %pad_maximum_fusion.3), channel_id=1, source_target_pairs={{0,96},{1,97},{2,98},{3,99},{4,100},{5,101},{6,102},{7,103},{8,104... | collective-permute-start | bytes 1572872 | tf_op jit(solution)/shard_map/ppermute | solution.py:39
  33.7 6.7 %collective-permute-start.12 = (bf16[4,128,128]{2,1,0:T(8,128)(2,1)S(1)}, bf16[4,128,128]{2,1,0:T(8,128)(2,1)S(1)}, u32[]{:S(2)}, u32[]{:S(2)}) collective-permute-start(bf16[4,128,128]{2,1,0:T(8,128)(2,1)S(1)} %collective-permute-done.11.refs_10_), channel_id=1, source_target_pairs={{0,4},{1,5},{2,6},{3,7},{4,0},{5,1},{6,2},{7,3},{8,12},{9,13},{10,... | collective-permute-start | bytes 393224 | tf_op jit(solution)/shard_map/ppermute | solution.py:39
  36.5 51.0 %collective-permute-start.13 = (bf16[128,5120]{1,0:T(8,128)(2,1)}, bf16[128,5120]{1,0:T(8,128)(2,1)}, u32[]{:S(2)}, u32[]{:S(2)}) collective-permute-start(bf16[128,5120]{1,0:T(8,128)(2,1)} %bitcast.22), channel_id=1, source_target_pairs={{0,1},{1,9},{2,17},{3,25},{4,5},{5,13},{6,21},{7,29},{8,0},{9,8},{... | collective-permute-start | bytes 3932168 | tf_op jit(solution)/shard_map/ppermute | solution.py:39
  41.1 46.4 %collective-permute-start.14 = (bf16[128,5120]{1,0:T(8,128)(2,1)}, bf16[128,5120]{1,0:T(8,128)(2,1)}, u32[]{:S(2)}, u32[]{:S(2)}) collective-permute-start(bf16[128,5120]{1,0:T(8,128)(2,1)} %bitcast.22), channel_id=1, source_target_pairs={{0,19},{1,27},{2,3},{3,11},{4,23},{5,31},{6,7},{7,15},{8,18},{9,26... | collective-permute-start | bytes 3932168 | tf_op jit(solution)/shard_map/ppermute | solution.py:39
  45.7 38.1 %copy-start.7 = (s32[4]{0:T(128)}, s32[4]{0:T(128)S(1)}, u32[]{:S(2)}) copy-start(s32[4]{0:T(128)S(1)} %pad_add_fusion.where_ref) | copy-start | bytes 52
  83.7 23.9 %copy-start.23 = (s32[32]{0:T(128)S(1)}, s32[32]{0:T(128)}, u32[]{:S(2)}) copy-start(s32[32]{0:T(128)} %param.38) | copy-start | bytes 388
  83.7 19.1 %all-to-all-start = ((bf16[8,512,128]{2,1,0:T(8,128)(2,1)}), bf16[8,512,128]{2,1,0:T(8,128)(2,1)S(1)}, u32[]{:S(2)}, u32[]{:S(2)}) async-start(bf16[8,512,128]{2,1,0:T(8,128)(2,1)} %bitcast.21), calls=%async_computation | async-start | bytes 2097152 | tf_op jit(solution)/shard_map/all_to_all | solution.py:326
  102.8 11.5 %collective-permute-start.16 = (bf16[128,5120]{1,0:T(8,128)(2,1)}, bf16[128,5120]{1,0:T(8,128)(2,1)}, u32[]{:S(2)}, u32[]{:S(2)}) collective-permute-start(bf16[128,5120]{1,0:T(8,128)(2,1)} %collective-permute-done.13.h1_ref), channel_id=1, source_target_pairs={{0,1},{1,0},{2,3},{3,2},{4,5},{5,4},{6,7},{7,6},{8,9},{9,8},{10,11... | collective-permute-start | bytes 3932168 | tf_op jit(solution)/shard_map/ppermute | solution.py:39
  105.5 8.8 %collective-permute-start.17 = (bf16[128,5120]{1,0:T(8,128)(2,1)}, bf16[128,5120]{1,0:T(8,128)(2,1)}, u32[]{:S(2)}, u32[]{:S(2)}) collective-permute-start(bf16[128,5120]{1,0:T(8,128)(2,1)} %collective-permute-done.14.h3_ref), channel_id=1, source_target_pairs={{0,1},{1,0},{2,3},{3,2},{4,5},{5,4},{6,7},{7,6},{8,9},{9,8},{10,11... | collective-permute-start | bytes 3932168 | tf_op jit(solution)/shard_map/ppermute | solution.py:39
  105.7 8.7 %collective-permute-start.15 = (bf16[4,128,128]{2,1,0:T(8,128)(2,1)S(1)}, bf16[4,128,128]{2,1,0:T(8,128)(2,1)S(1)}, u32[]{:S(2)}, u32[]{:S(2)}) collective-permute-start(bf16[4,128,128]{2,1,0:T(8,128)(2,1)S(1)} %bitcast.200), channel_id=1, source_target_pairs={{0,0},{1,8},{2,16},{3,24},{4,4},{5,12},{6,20},{7,28},{8,32},{9,40}... | collective-permute-start | bytes 393224 | tf_op jit(solution)/shard_map/ppermute | solution.py:39
  120.2 11.2 %copy-start.19 = (f32[40,512]{1,0:T(8,128)S(1)}, f32[40,512]{1,0:T(8,128)}, u32[]{:S(2)}) copy-start(f32[40,512]{1,0:T(8,128)} %param.30) | copy-start | bytes 245764
  120.2 11.3 %copy-start.20 = (f32[40,512]{1,0:T(8,128)S(1)}, f32[40,512]{1,0:T(8,128)}, u32[]{:S(2)}) copy-start(f32[40,512]{1,0:T(8,128)} %param.31) | copy-start | bytes 245764
  120.2 11.3 %copy-start.21 = (f32[40,512]{1,0:T(8,128)S(1)}, f32[40,512]{1,0:T(8,128)}, u32[]{:S(2)}) copy-start(f32[40,512]{1,0:T(8,128)} %param.32) | copy-start | bytes 245764
  120.2 15.3 %copy-start.15 = (bf16[4,32,1024]{2,1,0:T(8,128)(2,1)S(1)}, bf16[4,32,1024]{2,1,0:T(8,128)(2,1)}, u32[]{:S(2)}) copy-start(bf16[4,32,1024]{2,1,0:T(8,128)(2,1)} %param.34) | copy-start | bytes 786436
  120.2 30.6 %all-to-all-start.1 = ((bf16[32,160,128]{2,1,0:T(8,128)(2,1)}), bf16[32,160,128]{2,1,0:T(8,128)(2,1)S(1)}, u32[]{:S(2)}, u32[]{:S(2)}) async-start(bf16[32,160,128]{2,1,0:T(8,128)(2,1)} %bitcast.180), calls=%async_computation.1 | async-start | bytes 2621440 | tf_op jit(solution)/shard_map/all_to_all | solution.py:326
  131.8 16.6 %collective-permute-start.20 = (f32[3,40,128]{2,1,0:T(8,128)S(1)}, f32[3,40,128]{2,1,0:T(8,128)S(1)}, u32[]{:S(2)}, u32[]{:S(2)}) collective-permute-start(f32[3,40,128]{2,1,0:T(8,128)S(1)} %bitcast.207), channel_id=1, source_target_pairs={{0,3},{1,2},{2,1},{3,0},{4,7},{5,6},{6,5},{7,4},{8,11},{9,10},{10,... | collective-permute-start | bytes 184328 | tf_op jit(solution)/shard_map/ppermute | solution.py:39
  135.0 13.3 %collective-permute-start.19 = (f32[3,40,128]{2,1,0:T(8,128)S(1)}, f32[3,40,128]{2,1,0:T(8,128)S(1)}, u32[]{:S(2)}, u32[]{:S(2)}) collective-permute-start(f32[3,40,128]{2,1,0:T(8,128)S(1)} %bitcast.205), channel_id=1, source_target_pairs={{0,2},{1,3},{2,0},{3,1},{4,6},{5,7},{6,4},{7,5},{8,10},{9,11},{10,... | collective-permute-start | bytes 184328 | tf_op jit(solution)/shard_map/ppermute | solution.py:39
  135.0 13.3 %collective-permute-start.18 = (f32[3,40,128]{2,1,0:T(8,128)S(1)}, f32[3,40,128]{2,1,0:T(8,128)S(1)}, u32[]{:S(2)}, u32[]{:S(2)}) collective-permute-start(f32[3,40,128]{2,1,0:T(8,128)S(1)} %bitcast.203), channel_id=1, source_target_pairs={{0,1},{1,0},{2,3},{3,2},{4,5},{5,4},{6,7},{7,6},{8,9},{9,8},{10,11... | collective-permute-start | bytes 184328 | tf_op jit(solution)/shard_map/ppermute | solution.py:39
  135.6 3.9 %copy-start.25 = (bf16[4,32,128]{2,1,0:T(8,128)(2,1)S(1)}, bf16[4,32,128]{2,1,0:T(8,128)(2,1)}, u32[]{:S(2)}) copy-start(bf16[4,32,128]{2,1,0:T(8,128)(2,1)} %param.35) | copy-start | bytes 98308
  135.6 6.3 %copy-start.24 = (bf16[32,512,128]{2,1,0:T(8,128)(2,1)S(1)}, bf16[32,512,128]{2,1,0:T(8,128)(2,1)}, u32[]{:S(2)}) copy-start(bf16[32,512,128]{2,1,0:T(8,128)(2,1)} %param.37) | copy-start | bytes 12582916
  151.7 9.6 %copy-start.12 = (f32[1,4,40,128]{3,2,1,0:T(8,128)S(1)}, f32[1,4,40,128]{3,2,1,0:T(8,128)}, u32[]{:S(2)}) copy-start(f32[1,4,40,128]{3,2,1,0:T(8,128)} %get-tuple-element.47) | copy-start | bytes 245764
  151.7 9.6 %copy-start.13 = (f32[1,4,40,128]{3,2,1,0:T(8,128)S(1)}, f32[1,4,40,128]{3,2,1,0:T(8,128)}, u32[]{:S(2)}) copy-start(f32[1,4,40,128]{3,2,1,0:T(8,128)} %get-tuple-element.48) | copy-start | bytes 245764
  151.7 9.6 %copy-start.14 = (f32[1,4,40,128]{3,2,1,0:T(8,128)S(1)}, f32[1,4,40,128]{3,2,1,0:T(8,128)}, u32[]{:S(2)}) copy-start(f32[1,4,40,128]{3,2,1,0:T(8,128)} %get-tuple-element.49) | copy-start | bytes 245764
  153.0 27.9 %all-to-all-start.2 = ((bf16[32,160,128]{2,1,0:T(8,128)(2,1)}), bf16[32,160,128]{2,1,0:T(8,128)(2,1)S(1)}, u32[]{:S(2)}, u32[]{:S(2)}) async-start(bf16[32,160,128]{2,1,0:T(8,128)(2,1)} %broadcast_in_dim.85), calls=%async_computation.2 | async-start | bytes 2621440 | tf_op jit(solution)/shard_map/all_to_all | solution.py:326
  162.1 15.4 %collective-permute-start.23 = (f32[3,40,128]{2,1,0:T(8,128)}, f32[3,40,128]{2,1,0:T(8,128)}, u32[]{:S(2)}, u32[]{:S(2)}) collective-permute-start(f32[3,40,128]{2,1,0:T(8,128)} %get-tuple-element.68), channel_id=1, source_target_pairs={{0,3},{1,2},{2,1},{3,0},{4,7},{5,6},{6,5},{7,4},{8,11},{9,10},{10,... | collective-permute-start | bytes 184328 | tf_op jit(solution)/shard_map/ppermute | solution.py:39
  162.9 14.6 %collective-permute-start.22 = (f32[3,40,128]{2,1,0:T(8,128)}, f32[3,40,128]{2,1,0:T(8,128)}, u32[]{:S(2)}, u32[]{:S(2)}) collective-permute-start(f32[3,40,128]{2,1,0:T(8,128)} %get-tuple-element.69), channel_id=1, source_target_pairs={{0,2},{1,3},{2,0},{3,1},{4,6},{5,7},{6,4},{7,5},{8,10},{9,11},{10,... | collective-permute-start | bytes 184328 | tf_op jit(solution)/shard_map/ppermute | solution.py:39
  165.0 12.4 %collective-permute-start.21 = (f32[3,40,128]{2,1,0:T(8,128)}, f32[3,40,128]{2,1,0:T(8,128)}, u32[]{:S(2)}, u32[]{:S(2)}) collective-permute-start(f32[3,40,128]{2,1,0:T(8,128)} %get-tuple-element.70), channel_id=1, source_target_pairs={{0,1},{1,0},{2,3},{3,2},{4,5},{5,4},{6,7},{7,6},{8,9},{9,8},{10,11... | collective-permute-start | bytes 184328 | tf_op jit(solution)/shard_map/ppermute | solution.py:39
  180.9 1.7 copy-start.9
  180.9 1.0 copy-start.17
  182.6 6.7 %copy-start.8 = (bf16[1024,2560]{1,0:T(8,128)(2,1)S(1)}, bf16[1024,2560]{1,0:T(8,128)(2,1)}, u32[]{:S(2)}) copy-start(bf16[1024,2560]{1,0:T(8,128)(2,1)} %get-tuple-element.37) | copy-start | bytes 15728644
  186.1 5.8 %collective-permute-start.24 = (f32[128,2560]{1,0:T(8,128)S(1)}, f32[128,2560]{1,0:T(8,128)S(1)}, u32[]{:S(2)}, u32[]{:S(2)}) collective-permute-start(f32[128,2560]{1,0:T(8,128)S(1)} %fusion.20), channel_id=1, source_target_pairs={{0,1},{1,0},{2,3},{3,2},{4,5},{5,4},{6,7},{7,6},{8,9},{9,8},{10,11... | collective-permute-start | bytes 3932168 | tf_op jit(solution)/shard_map/ppermute | solution.py:39
  192.1 16.1 %collective-permute-start.25 = (bf16[128,2560]{1,0:T(8,128)(2,1)S(1)}, bf16[128,2560]{1,0:T(8,128)(2,1)}, u32[]{:S(2)}, u32[]{:S(2)}) collective-permute-start(bf16[128,2560]{1,0:T(8,128)(2,1)S(1)} %get-tuple-element.45), channel_id=1, source_target_pairs={{0,2},{1,3},{2,0},{3,1},{4,6},{5,7},{6,4},{7,5},{8,10},{9,11},{10,... | collective-permute-start | bytes 1966088 | tf_op jit(solution)/shard_map/ppermute | solution.py:39
  209.6 3.0 %collective-permute-start.26 = (bf16[128,2560]{1,0:T(8,128)(2,1)S(1)}, bf16[128,2560]{1,0:T(8,128)(2,1)S(1)}, u32[]{:S(2)}, u32[]{:S(2)}) collective-permute-start(bf16[128,2560]{1,0:T(8,128)(2,1)S(1)} %get-tuple-element.44), channel_id=1, source_target_pairs={{0,1},{1,0},{2,3},{3,2},{4,5},{5,4},{6,7},{7,6},{8,9},{9,8},{10,11... | collective-permute-start | bytes 1966088 | tf_op jit(solution)/shard_map/ppermute | solution.py:39
  212.7 1.1 copy-start.10
  (8 other events, 6.2 us)
